TPU v7x, 32 devices: a whole 2x2x4 slice. The times are simulated.
32 devices in a mesh: grp: 2 (over x), ep: 16 (over z, y, core).
Axes of the slice: x: 2, y: 2, z: 4, core: 2. Of those that a mesh axis runs over, the one named last changes fastest.
Arguments:
- block_input: bfloat16 [4096, 2048], P(('grp', 'ep')), may hold values from -6 to 6
- cotangent: bfloat16 [4096, 2048], P(('grp', 'ep')), may hold values from -6 to 6
- routes: int32 [4096, 8], P(('grp', 'ep')), may hold values from 0 to 15, all different within a row; in each aligned block of 128 rows (0 to 127, 128 to 255, ...) at most 66 rows name the same one
- w_query: bfloat16 [2048, 2048], P(('grp', 'ep')), may hold values from -0.125 to 0.125
- w_key: bfloat16 [2048, 2048], P(('grp', 'ep')), may hold values from -0.125 to 0.125
- w_value: bfloat16 [2048, 2048], P(('grp', 'ep')), may hold values from -0.125 to 0.125
- w_output: bfloat16 [2048, 2048], P(('grp', 'ep')), may hold values from -1.5 to 1.5
- w_router: bfloat16 [2048, 16], P(('grp', 'ep')), may hold values from -0.0625 to 0.0625
- gain_attn: bfloat16 [2048], P(('grp', 'ep')), may hold values from 0.25 to 1.75
- gain_query: bfloat16 [2048], P(('grp', 'ep')), may hold values from 0.25 to 1.75
- gain_key: bfloat16 [2048], P(('grp', 'ep')), may hold values from 0.25 to 1.75
- gain_mlp: bfloat16 [2048], P(('grp', 'ep')), may hold values from 0.25 to 1.75
- w_gate: bfloat16 [16, 2048, 1024], P('ep'), may hold values from -0.125 to 0.125
- w_up: bfloat16 [16, 2048, 1024], P('ep'), may hold values from -0.125 to 0.125
- w_down: bfloat16 [16, 1024, 2048], P('ep'), may hold values from -1.5 to 1.5
Outputs:
- block_output: bfloat16 [4096, 2048], P(('grp', 'ep'))
- input_grad: float32 [4096, 2048], P(('grp', 'ep'))
- grad_query: float32 [2048, 2048], P(('grp', 'ep'))
- grad_key: float32 [2048, 2048], P(('grp', 'ep'))
- grad_value: float32 [2048, 2048], P(('grp', 'ep'))
- grad_output: float32 [2048, 2048], P(('grp', 'ep'))
- grad_router: float32 [2048, 16], P(('grp', 'ep'))
- grad_gain_attn: float32 [2048], P(('grp', 'ep'))
- grad_gain_query: float32 [2048], P(('grp', 'ep'))
- grad_gain_key: float32 [2048], P(('grp', 'ep'))
- grad_gain_mlp: float32 [2048], P(('grp', 'ep'))
- grad_gate: float32 [16, 2048, 1024], P('ep')
- grad_up: float32 [16, 2048, 1024], P('ep')
- grad_down: float32 [16, 1024, 2048], P('ep')
Inputs may be any that keep to these rules, and one draw needn't show every extreme that they name: `routes`: each token names 8 different experts. Among the rows of one device (aligned blocks of 128 rows) no expert is named by more than 66 rows, a bound that some block reaches.
All inputs are finite; a program needn't handle non-finite values.
Results may differ from a plain program's by a relative error of at most 0.02.
Values may be sent and summed in bfloat16 or wider, within the bound.
A program may use at most 320 MiB of HBM per device.

v0:
```python
import math

import jax
import jax.numpy as jnp
from jax import lax
from jax.sharding import PartitionSpec as P

HEAD_DIM = 128


eps = 1e-05
theta_base = 10000.0


def rms_scale(values, gain_vec):
    return values * lax.rsqrt(jnp.mean(values * values, axis=-1, keepdims=True) + eps) * gain_vec


def rotate(values, position):
    token_count = values.shape[0]
    by_head = values.reshape(token_count, -1, HEAD_DIM)
    half_dim = HEAD_DIM // 2
    frequency = theta_base ** (-2.0 * jnp.arange(half_dim, dtype=jnp.float32) / HEAD_DIM)
    angles = position.astype(jnp.float32)[:, None] * frequency[None, :]
    cosine = jnp.cos(angles)[:, None, :]
    sine_part = jnp.sin(angles)[:, None, :]
    former = by_head[..., :half_dim]
    latter = by_head[..., half_dim:]
    turned = jnp.concatenate(
        [former * cosine - latter * sine_part, latter * cosine + former * sine_part], axis=-1
    )
    return turned.reshape(token_count, -1)


def masked_scores(query, keys, allowed, scale):
    raw_scores = jnp.einsum("qhd,khd->hqk", query, keys, preferred_element_type=jnp.float32) * scale
    return jnp.where(allowed[None], raw_scores, -1e30)


def attend(query, keys, values, allowed, scale, head_group):
    outputs = []
    log_totals = []
    for head_start in range(0, query.shape[1], head_group):
        head_slice = slice(head_start, head_start + head_group)
        scores = masked_scores(query[:, head_slice], keys[:, head_slice], allowed, scale)
        largest = jnp.max(scores, axis=-1, keepdims=True)
        exponent = jnp.exp(scores - largest)
        summed = jnp.sum(exponent, axis=-1, keepdims=True)
        weights = (exponent / summed).astype(jnp.bfloat16)
        outputs.append(
            jnp.einsum(
                "hqk,khd->qhd", weights, values[:, head_slice], preferred_element_type=jnp.float32
            )
        )
        log_totals.append(largest + jnp.log(summed))
    return (jnp.concatenate(outputs, axis=1), jnp.concatenate(log_totals, axis=0))


def attend_back(query, keys, values, grad_out, log_totals, allowed, scale, head_group):
    query_grads = []
    key_grads = []
    value_grads = []
    for head_start in range(0, query.shape[1], head_group):
        head_slice = slice(head_start, head_start + head_group)
        query_part = query[:, head_slice]
        keys_part = keys[:, head_slice]
        grad_part = grad_out[:, head_slice]
        scores = masked_scores(query_part, keys_part, allowed, scale)
        weights = jnp.where(allowed[None], jnp.exp(scores - log_totals[head_slice]), 0.0)
        grad_weights = jnp.einsum(
            "qhd,khd->hqk", grad_part, values[:, head_slice], preferred_element_type=jnp.float32
        )
        inner = jnp.sum(weights * grad_weights, axis=-1, keepdims=True)
        grad_scores = (weights * (grad_weights - inner)).astype(jnp.bfloat16)
        query_grads.append(
            jnp.einsum("hqk,khd->qhd", grad_scores, keys_part, preferred_element_type=jnp.float32)
            * scale
        )
        key_grads.append(
            jnp.einsum("hqk,qhd->khd", grad_scores, query_part, preferred_element_type=jnp.float32)
            * scale
        )
        value_grads.append(
            jnp.einsum(
                "hqk,qhd->khd",
                weights.astype(jnp.bfloat16),
                grad_part,
                preferred_element_type=jnp.float32,
            )
        )
    return (
        jnp.concatenate(query_grads, axis=1),
        jnp.concatenate(key_grads, axis=1),
        jnp.concatenate(value_grads, axis=1),
    )


def per_device(
    block_input,
    cotangent,
    routes,
    w_query,
    w_key,
    w_value,
    w_output,
    w_router,
    gain_attn,
    gain_query,
    gain_key,
    gain_mlp,
    w_gate,
    w_up,
    w_down,
):
    row_count, model_width = block_input.shape
    top_count = routes.shape[1]
    ep_count = lax.axis_size("ep")
    my_index = lax.axis_index("ep")
    half_count = ep_count // 2
    prompt_len = row_count * half_count
    capacity = min(row_count, row_count * top_count * 33 // (32 * ep_count))
    head_count = model_width // HEAD_DIM
    head_group = math.gcd(4, head_count)
    scale = HEAD_DIM ** (-0.5)
    gathered = (
        lax.all_gather(w_query, ("grp", "ep"), axis=0, tiled=True),
        lax.all_gather(w_key, ("grp", "ep"), axis=0, tiled=True),
        lax.all_gather(w_value, ("grp", "ep"), axis=0, tiled=True),
        lax.all_gather(w_output, ("grp", "ep"), axis=0, tiled=True),
        lax.all_gather(w_router, ("grp", "ep"), axis=0, tiled=True),
        lax.all_gather(gain_attn, ("grp", "ep"), axis=0, tiled=True),
        lax.all_gather(gain_query, ("grp", "ep"), axis=0, tiled=True),
        lax.all_gather(gain_key, ("grp", "ep"), axis=0, tiled=True),
        lax.all_gather(gain_mlp, ("grp", "ep"), axis=0, tiled=True),
    )
    full_query, full_key, full_value, full_output, full_router = (
        gathered[0],
        gathered[1],
        gathered[2],
        gathered[3],
        gathered[4],
    )
    gain_first = gathered[5].astype(jnp.float32)
    gain_qnorm = gathered[6].astype(jnp.float32)
    gain_knorm = gathered[7].astype(jnp.float32)
    gain_second = gathered[8].astype(jnp.float32)
    offsets = jnp.arange(row_count, dtype=jnp.int32)
    in_prompt = my_index < half_count
    position = jnp.where(in_prompt, my_index * row_count + offsets, prompt_len + offsets)
    key_position = jnp.concatenate([jnp.arange(prompt_len, dtype=jnp.int32), prompt_len + offsets])
    from_prompt = jnp.arange(prompt_len + row_count, dtype=jnp.int32) < prompt_len
    allowed = (key_position[None, :] <= position[:, None]) & (
        from_prompt[None, :] | jnp.logical_not(in_prompt)
    )

    def prepare(linear, gain_vec):
        return rotate(rms_scale(linear, gain_vec), position)

    inputs = block_input.astype(jnp.float32)
    normed = rms_scale(inputs, gain_first).astype(jnp.bfloat16)
    query_lin = jnp.dot(normed, full_query, preferred_element_type=jnp.float32)
    key_lin = jnp.dot(normed, full_key, preferred_element_type=jnp.float32)
    value_lin = jnp.dot(normed, full_value, preferred_element_type=jnp.float32)
    query_low = prepare(query_lin, gain_qnorm).astype(jnp.bfloat16)
    key_low = prepare(key_lin, gain_knorm).astype(jnp.bfloat16)
    value_low = value_lin.astype(jnp.bfloat16)
    shared = (
        lax.all_gather(key_low, "ep", axis=0, tiled=True),
        lax.all_gather(value_low, "ep", axis=0, tiled=True),
    )
    keys = jnp.concatenate([shared[0][:prompt_len], key_low]).reshape(-1, head_count, HEAD_DIM)
    values = jnp.concatenate([shared[1][:prompt_len], value_low]).reshape(-1, head_count, HEAD_DIM)
    query = query_low.reshape(row_count, head_count, HEAD_DIM)
    attn_out, log_totals = attend(query, keys, values, allowed, scale, head_group)
    attended = attn_out.reshape(row_count, model_width).astype(jnp.bfloat16)
    residual = inputs + jnp.dot(attended, full_output, preferred_element_type=jnp.float32)
    normed_mlp = rms_scale(residual, gain_second).astype(jnp.bfloat16)
    logits = jnp.dot(normed_mlp, full_router, preferred_element_type=jnp.float32)
    probs = jax.nn.softmax(logits, axis=-1)
    picks = routes[:, :, None] == jnp.arange(ep_count, dtype=jnp.int32)[None, None, :]
    gates = jnp.sum(jnp.where(picks, probs[:, None, :], 0.0), axis=-1)
    hot_table = picks.reshape(-1, ep_count).astype(jnp.int32)
    before = jnp.cumsum(hot_table, axis=0) - hot_table
    slot_index = jnp.sum(before * hot_table, axis=1)
    target = routes.reshape(-1) * capacity + slot_index
    sentinel = row_count * top_count
    source = (
        jnp.full((ep_count * capacity,), sentinel, jnp.int32)
        .at[target]
        .set(jnp.arange(sentinel, dtype=jnp.int32))
    )
    token_of = source // top_count
    padded_rows = jnp.concatenate([normed_mlp, jnp.zeros((1, model_width), jnp.bfloat16)])
    outgoing = padded_rows[token_of].reshape(ep_count, capacity, model_width)
    arrived = lax.all_to_all(outgoing, "ep", split_axis=0, concat_axis=0, tiled=True)
    units = arrived.reshape(-1, model_width)
    gate_w = w_gate[0]
    up_w = w_up[0]
    down_w = w_down[0]
    gate_pre = jnp.dot(units, gate_w, preferred_element_type=jnp.float32)
    up_pre = jnp.dot(units, up_w, preferred_element_type=jnp.float32)
    hidden = (jax.nn.silu(gate_pre) * up_pre).astype(jnp.bfloat16)
    expert_result = jnp.dot(hidden, down_w, preferred_element_type=jnp.float32).astype(jnp.bfloat16)
    returned = lax.all_to_all(
        expert_result.reshape(ep_count, capacity, model_width),
        "ep",
        split_axis=0,
        concat_axis=0,
        tiled=True,
    )
    picked = (
        returned.reshape(-1, model_width)[target]
        .reshape(row_count, top_count, model_width)
        .astype(jnp.float32)
    )
    output_full = residual + jnp.sum(gates[:, :, None] * picked, axis=1)
    block_output = output_full.astype(jnp.bfloat16)
    back_query, back_key, back_value, back_output, back_router = (
        full_query,
        full_key,
        full_value,
        full_output,
        full_router,
    )
    grad_top = cotangent.astype(jnp.float32)
    grad_gates = jnp.sum(grad_top[:, None, :] * picked, axis=-1)
    grad_expert = (
        (gates[:, :, None] * grad_top[:, None, :]).astype(jnp.bfloat16).reshape(-1, model_width)
    )
    padded_grads = jnp.concatenate([grad_expert, jnp.zeros((1, model_width), jnp.bfloat16)])
    grad_outgoing = padded_grads[source].reshape(ep_count, capacity, model_width)
    grad_arrived = lax.all_to_all(
        grad_outgoing, "ep", split_axis=0, concat_axis=0, tiled=True
    ).reshape(-1, model_width)
    grad_hidden = jnp.einsum("nd,fd->nf", grad_arrived, down_w, preferred_element_type=jnp.float32)
    sigma = jax.nn.sigmoid(gate_pre)
    grad_gate_pre = (grad_hidden * up_pre * sigma * (1.0 + gate_pre * (1.0 - sigma))).astype(
        jnp.bfloat16
    )
    grad_up_pre = (grad_hidden * gate_pre * sigma).astype(jnp.bfloat16)
    local_down = jnp.einsum("nf,nd->fd", hidden, grad_arrived, preferred_element_type=jnp.float32)
    local_gate = jnp.einsum("nd,nf->df", units, grad_gate_pre, preferred_element_type=jnp.float32)
    local_up = jnp.einsum("nd,nf->df", units, grad_up_pre, preferred_element_type=jnp.float32)
    grad_units = jnp.einsum("nf,df->nd", grad_gate_pre, gate_w, preferred_element_type=jnp.float32)
    grad_units = grad_units + jnp.einsum(
        "nf,df->nd", grad_up_pre, up_w, preferred_element_type=jnp.float32
    )
    grad_units = grad_units.astype(jnp.bfloat16).reshape(ep_count, capacity, model_width)
    grad_returned = lax.all_to_all(
        grad_units, "ep", split_axis=0, concat_axis=0, tiled=True
    ).reshape(-1, model_width)
    grad_normed_mlp = jnp.sum(
        grad_returned[target].reshape(row_count, top_count, model_width).astype(jnp.float32), axis=1
    )
    expert_sums = (
        lax.psum(local_gate[None].astype(jnp.bfloat16), "grp").astype(jnp.float32),
        lax.psum(local_up[None].astype(jnp.bfloat16), "grp").astype(jnp.float32),
        lax.psum(local_down[None].astype(jnp.bfloat16), "grp").astype(jnp.float32),
    )
    grad_probs = jnp.sum(jnp.where(picks, grad_gates[:, :, None], 0.0), axis=1)
    grad_logits = (
        probs * (grad_probs - jnp.sum(probs * grad_probs, axis=-1, keepdims=True))
    ).astype(jnp.bfloat16)
    local_router = jnp.einsum(
        "rd,re->de", normed_mlp, grad_logits, preferred_element_type=jnp.float32
    )
    grad_normed_mlp = grad_normed_mlp + jnp.einsum(
        "re,de->rd", grad_logits, back_router, preferred_element_type=jnp.float32
    )
    unused_mlp, second_back = jax.vjp(rms_scale, residual, gain_second)
    grad_from_mlp, local_gain_mlp = second_back(grad_normed_mlp)
    grad_residual = grad_top + grad_from_mlp
    grad_proj = grad_residual.astype(jnp.bfloat16)
    local_output = jnp.einsum("rd,re->de", attended, grad_proj, preferred_element_type=jnp.float32)
    grad_attended = jnp.einsum(
        "re,de->rd", grad_proj, back_output, preferred_element_type=jnp.float32
    )
    grad_attended = grad_attended.astype(jnp.bfloat16).reshape(row_count, head_count, HEAD_DIM)
    grad_query_rot, grad_keys, grad_values = attend_back(
        query, keys, values, grad_attended, log_totals, allowed, scale, head_group
    )
    grad_keys = grad_keys.reshape(-1, model_width)
    grad_values = grad_values.reshape(-1, model_width)
    padding = jnp.zeros((ep_count * row_count - prompt_len, model_width), jnp.float32)
    key_share, value_share = (
        lax.psum_scatter(
            jnp.concatenate([grad_keys[:prompt_len], padding]).astype(jnp.bfloat16),
            "ep",
            scatter_dimension=0,
            tiled=True,
        ).astype(jnp.float32),
        lax.psum_scatter(
            jnp.concatenate([grad_values[:prompt_len], padding]).astype(jnp.bfloat16),
            "ep",
            scatter_dimension=0,
            tiled=True,
        ).astype(jnp.float32),
    )
    grad_key_rot = key_share + grad_keys[prompt_len:]
    grad_value_lin = (value_share + grad_values[prompt_len:]).astype(jnp.bfloat16)
    unused_query, query_back = jax.vjp(prepare, query_lin, gain_qnorm)
    grad_query_lin, local_gain_query = query_back(grad_query_rot.reshape(row_count, model_width))
    unused_key, key_back = jax.vjp(prepare, key_lin, gain_knorm)
    grad_key_lin, local_gain_key = key_back(grad_key_rot)
    grad_query_low = grad_query_lin.astype(jnp.bfloat16)
    grad_key_low = grad_key_lin.astype(jnp.bfloat16)
    local_query = jnp.einsum(
        "rd,re->de", normed, grad_query_low, preferred_element_type=jnp.float32
    )
    local_key = jnp.einsum("rd,re->de", normed, grad_key_low, preferred_element_type=jnp.float32)
    local_value = jnp.einsum(
        "rd,re->de", normed, grad_value_lin, preferred_element_type=jnp.float32
    )
    grad_normed = jnp.einsum(
        "re,de->rd", grad_query_low, back_query, preferred_element_type=jnp.float32
    )
    grad_normed = grad_normed + jnp.einsum(
        "re,de->rd", grad_key_low, back_key, preferred_element_type=jnp.float32
    )
    grad_normed = grad_normed + jnp.einsum(
        "re,de->rd", grad_value_lin, back_value, preferred_element_type=jnp.float32
    )
    unused_first, first_back = jax.vjp(rms_scale, inputs, gain_first)
    grad_from_attn, local_gain_attn = first_back(grad_normed)
    input_grad = grad_residual + grad_from_attn
    summed_grads = (
        lax.psum_scatter(local_query, ("grp", "ep"), scatter_dimension=0, tiled=True),
        lax.psum_scatter(local_key, ("grp", "ep"), scatter_dimension=0, tiled=True),
        lax.psum_scatter(local_value, ("grp", "ep"), scatter_dimension=0, tiled=True),
        lax.psum_scatter(local_output, ("grp", "ep"), scatter_dimension=0, tiled=True),
        lax.psum_scatter(local_router, ("grp", "ep"), scatter_dimension=0, tiled=True),
        lax.psum_scatter(local_gain_attn, ("grp", "ep"), scatter_dimension=0, tiled=True),
        lax.psum_scatter(local_gain_query, ("grp", "ep"), scatter_dimension=0, tiled=True),
        lax.psum_scatter(local_gain_key, ("grp", "ep"), scatter_dimension=0, tiled=True),
        lax.psum_scatter(local_gain_mlp, ("grp", "ep"), scatter_dimension=0, tiled=True),
    )
    return (
        block_output,
        input_grad,
        summed_grads[0],
        summed_grads[1],
        summed_grads[2],
        summed_grads[3],
        summed_grads[4],
        summed_grads[5],
        summed_grads[6],
        summed_grads[7],
        summed_grads[8],
        expert_sums[0],
        expert_sums[1],
        expert_sums[2],
    )


def solution(mesh):
    return jax.shard_map(
        per_device,
        mesh=mesh,
        in_specs=(
            P(("grp", "ep"), None),
            P(("grp", "ep"), None),
            P(("grp", "ep"), None),
            P(("grp", "ep"), None),
            P(("grp", "ep"), None),
            P(("grp", "ep"), None),
            P(("grp", "ep"), None),
            P(("grp", "ep"), None),
            P(("grp", "ep")),
            P(("grp", "ep")),
            P(("grp", "ep")),
            P(("grp", "ep")),
            P("ep", None, None),
            P("ep", None, None),
            P("ep", None, None),
        ),
        out_specs=(
            P(("grp", "ep"), None),
            P(("grp", "ep"), None),
            P(("grp", "ep"), None),
            P(("grp", "ep"), None),
            P(("grp", "ep"), None),
            P(("grp", "ep"), None),
            P(("grp", "ep"), None),
            P(("grp", "ep")),
            P(("grp", "ep")),
            P(("grp", "ep")),
            P(("grp", "ep")),
            P("ep", None, None),
            P("ep", None, None),
            P("ep", None, None),
        ),
        check_vma=False,
    )
```

profile of v0, /device:TPU:0, one launch (start us, length us, event | category | flops | bytes accessed | tf_op | source)
XLA Modules:
  0.0 2486.2 jit_solution(13487281524490163754)
XLA Ops:
  12.9 42.6 %all-reduce.17 = (bf16[2048]{0:T(1024)(128)(2,1)S(1)}, bf16[2048]{0:T(1024)(128)(2,1)S(1)}, bf16[2048]{0:T(1024)(128)(2,1)S(1)}, bf16[2048]{0:T(1024)(128)(2,1)S(1)}) all-reduce(bf16[2048]{0:T(1024)(128)(2,1)S(1)} %dynamic-update-slice, bf16[2048]{0:T(1024)(128)(2,1)S(1)} %dynamic-update-slice.1, ...), channel_id=1, replica_groups=mesh['grp'=2,'ep'=16] {'grp','ep'}, use_global_device_ids=true, to_apply=%add.8 | all-reduce | flops 8192 | bytes 32768
  56.8 34.5 %all-gather.8.cloned.1.call-done = bf16[2048,2048]{1,0:T(8,128)(2,1)} async-done(((bf16[64,2048]{1,0:T(8,128)(2,1)}), bf16[2048,2048]{1,0:T(8,128)(2,1)}) %all-gather.8.cloned.1.call-update) | async-done | bytes 8388624 | tf_op jit(solution)/shard_map/all_gather | solution.py:128
  97.4 72.9 %all-gather.14.cloned.1.call-done = bf16[2048,2048]{1,0:T(8,128)(2,1)} async-done(((bf16[64,2048]{1,0:T(8,128)(2,1)}), bf16[2048,2048]{1,0:T(8,128)(2,1)}) %all-gather.14.cloned.1.call-update) | async-done | bytes 8388624 | tf_op jit(solution)/shard_map/all_gather | solution.py:127
  176.4 73.0 %all-gather.12.cloned.1.call-done = bf16[2048,2048]{1,0:T(8,128)(2,1)} async-done(((bf16[64,2048]{1,0:T(8,128)(2,1)}), bf16[2048,2048]{1,0:T(8,128)(2,1)}) %all-gather.12.cloned.1.call-update) | async-done | bytes 8388624 | tf_op jit(solution)/shard_map/all_gather | solution.py:126
  269.6 56.0 %all-gather.10.cloned.1.call-done = bf16[2048,2048]{1,0:T(8,128)(2,1)} async-done(((bf16[128,2048]{1,0:T(8,128)(2,1)}), bf16[2048,2048]{1,0:T(8,128)(2,1)}) %all-gather.10.cloned.1.call-update) | async-done | bytes 8388624 | tf_op jit(solution)/shard_map/all_gather | solution.py:169
  337.1 67.5 %all-gather.16.cloned.1.call-done = bf16[2048,2048]{0,1:T(8,128)(2,1)} async-done(((bf16[128,2048]{0,1:T(8,128)(2,1)}), bf16[2048,2048]{0,1:T(8,128)(2,1)}) %all-gather.16.cloned.1.call-update) | async-done | bytes 8388624 | tf_op jit(solution)/shard_map/all_gather | solution.py:168
  417.6 65.4 %all-gather.18.cloned.1.call-done = bf16[2048,2048]{1,0:T(8,128)(2,1)} async-done(((bf16[64,2048]{1,0:T(8,128)(2,1)}), bf16[2048,2048]{1,0:T(8,128)(2,1)}) %all-gather.18.cloned.1.call-update) | async-done | bytes 8388624 | tf_op jit(solution)/shard_map/all_gather | solution.py:129
  504.9 131.8 %all-gather = bf16[32,64,16]{1,2,0:T(8,128)(2,1)S(1)} all-gather(bf16[1,64,16]{1,2,0:T(8,128)(2,1)S(1)} %bitcast.233), channel_id=1, replica_groups=mesh['grp'=2,'ep'=16] {'grp','ep'}, dimensions={0}, use_global_device_ids=true | all-gather | bytes 67584 | tf_op jit(solution)/shard_map/all_gather | solution.py:130
  640.8 13.3 gather_fusion.2
  669.2 10.3 fusion.12
  685.9 64.8 %all-to-all-done.2 = bf16[16,66,2048]{2,1,0:T(8,128)(2,1)} async-done(((bf16[16,66,2048]{2,1,0:T(8,128)(2,1)}), bf16[16,66,2048]{2,1,0:T(8,128)(2,1)}, u32[]{:S(2)}, u32[]{:S(2)}) %all-to-all-start.2) | async-done | bytes 4325408 | tf_op jit(solution)/shard_map/all_to_all | solution.py:232
  756.0 13.7 multiply_convert_fusion
  790.9 21.8 all-to-all-start.3
  812.7 9.6 convolution_convert_fusion
  827.6 71.9 %all-to-all-done.3 = bf16[16,66,2048]{2,1,0:T(8,128)(2,1)} async-done(((bf16[16,66,2048]{2,1,0:T(8,128)(2,1)}), bf16[16,66,2048]{2,1,0:T(8,128)(2,1)}, u32[]{:S(2)}, u32[]{:S(2)}) %all-to-all-start.3) | async-done | bytes 4325408 | tf_op jit(solution)/shard_map/all_to_all | solution.py:249
  899.5 21.8 all-to-all-start.1
  929.4 11.6 gather_fusion.3
  946.0 62.1 %all-to-all-done.1 = bf16[16,66,2048]{2,1,0:T(8,128)(2,1)} async-done(((bf16[16,66,2048]{2,1,0:T(8,128)(2,1)}), bf16[16,66,2048]{2,1,0:T(8,128)(2,1)}, u32[]{:S(2)}, u32[]{:S(2)}) %all-to-all-start.1) | async-done | bytes 4325408 | tf_op jit(solution)/shard_map/all_to_all | solution.py:204
  1013.4 11.6 gather_fusion.1
  1099.4 10.0 convert_bitcast_fusion.2
  1109.4 9.8 convert_bitcast_fusion.1
  1121.6 9.4 convert_bitcast_fusion
  1151.8 41.5 %reduce-scatter.22.cloned.1.call-done = bf16[128,2048]{1,0:T(8,128)(2,1)} async-done(((bf16[2048,2048]{1,0:T(8,128)(2,1)}), bf16[128,2048]{1,0:T(8,128)(2,1)}) %reduce-scatter.22.cloned.1.call-update) | async-done | bytes 524304
  1202.5 9.9 fusion.126
  1229.1 73.3 %reduce-scatter.24.cloned.1.call-done = bf16[128,2048]{1,0:T(8,128)(2,1)} async-done(((bf16[2048,2048]{1,0:T(8,128)(2,1)}), bf16[128,2048]{1,0:T(8,128)(2,1)}) %reduce-scatter.24.cloned.1.call-update) | async-done | bytes 524304
  1313.2 126.0 %reduce-scatter.26.cloned.1.call-done = f32[64,16]{1,0:T(8,128)} async-done(((f32[2048,16]{1,0:T(8,128)}), f32[64,16]{1,0:T(8,128)}) %reduce-scatter.26.cloned.1.call-update) | async-done | bytes 4112
  1440.6 287.7 %all-reduce.21.cloned.1.call-done = (bf16[1,2048,1024]{2,1,0:T(8,128)(2,1)}, bf16[1,2048,1024]{2,1,0:T(8,128)(2,1)}, bf16[1,1024,2048]{2,1,0:T(8,128)(2,1)}) async-done(((bf16[1,2048,1024]{2,1,0:T(8,128)(2,1)}, bf16[1,2048,1024]{2,1,0:T(8,128)(2,1)}, bf16[1,1024,2048]{2,1,0:T(8,128)(2,1)}), (bf16[1,2048,1024]{2,1,0:T(8,128)(2,1)}, bf16[1,2048,1024]{2,1,0:T(8,128)(2,1)}, ...) | async-done | bytes 12582928 | tf_op jit(solution)/shard_map/psum | solution.py:256
  1757.6 44.9 %all-reduce.16 = (f32[2048]{0:T(1024)S(1)}, f32[2048]{0:T(1024)S(1)}, f32[2048]{0:T(1024)S(1)}, f32[2048]{0:T(1024)S(1)}) all-reduce(f32[2048]{0:T(1024)S(1)} %get-tuple-element.22, f32[2048]{0:T(1024)S(1)} %get-tuple-element.20, f32[2048]{0:T(1024)S(1)} %get-tuple-element.18, ...), channel_id=9, replica_groups=mesh['grp'=2,'ep'=16] {'grp','ep'}, use_global_device_ids=true, to_apply=%region_40.41.clone | all-reduce | flops 8192 | bytes 65536
  1806.1 109.6 %reduce-scatter.20.cloned.1.call-done = f32[64,2048]{1,0:T(8,128)} async-done(((f32[2048,2048]{1,0:T(8,128)}), f32[64,2048]{1,0:T(8,128)}) %reduce-scatter.20.cloned.1.call-update) | async-done | bytes 524304 | tf_op jit(solution)/shard_map/reduce_scatter | solution.py:330
  1915.7 188.2 %reduce-scatter.14.cloned.1.call-done = f32[64,2048]{1,0:T(8,128)} async-done(((f32[2048,2048]{1,0:T(8,128)}), f32[64,2048]{1,0:T(8,128)}) %reduce-scatter.14.cloned.1.call-update) | async-done | bytes 524304 | tf_op jit(solution)/shard_map/reduce_scatter | solution.py:327
  2103.9 187.7 %reduce-scatter.16.cloned.1.call-done = f32[64,2048]{1,0:T(8,128)} async-done(((f32[2048,2048]{1,0:T(8,128)}), f32[64,2048]{1,0:T(8,128)}) %reduce-scatter.16.cloned.1.call-update) | async-done | bytes 524304 | tf_op jit(solution)/shard_map/reduce_scatter | solution.py:328
  2291.6 187.6 %reduce-scatter.18.cloned.1.call-done = f32[64,2048]{1,0:T(8,128)} async-done(((f32[2048,2048]{1,0:T(8,128)}), f32[64,2048]{1,0:T(8,128)}) %reduce-scatter.18.cloned.1.call-update) | async-done | bytes 524304 | tf_op jit(solution)/shard_map/reduce_scatter | solution.py:329
  (464 shorter events, 328.4 us)
Async XLA Ops:
  7.2 84.1 %all-gather.8.cloned.1.call-start = ((), (), s32[]{:S(2)}) async-start(), calls=%async_computation.11 | async-start | bytes 8650752 | tf_op jit(solution)/shard_map/all_gather | solution.py:128
  7.9 162.4 %all-gather.14.cloned.1.call-start = ((), (), s32[]{:S(2)}) async-start(), calls=%async_computation.14 | async-start | bytes 8650752 | tf_op jit(solution)/shard_map/all_gather | solution.py:127
  8.7 240.8 %all-gather.12.cloned.1.call-start = ((), (), s32[]{:S(2)}) async-start(), calls=%async_computation.13 | async-start | bytes 8650752 | tf_op jit(solution)/shard_map/all_gather | solution.py:126
  9.4 316.2 %all-gather.10.cloned.1.call-start = ((), (), s32[]{:S(2)}) async-start(), calls=%async_computation.12 | async-start | bytes 8912896 | tf_op jit(solution)/shard_map/all_gather | solution.py:169
  55.5 193.9 %copy-start.58 = (f32[2048]{0:T(1024)}, f32[2048]{0:T(1024)S(1)}, u32[]{:S(2)}) copy-start(f32[2048]{0:T(1024)S(1)} %convert_element_type.182) | copy-start | bytes 24580
  56.7 192.7 %copy-start.79 = (f32[128]{0:T(128)}, f32[128]{0:T(128)S(1)}, u32[]{:S(2)}) copy-start(f32[128]{0:T(128)S(1)} %fusion.114) | copy-start | bytes 1540
  56.7 113.6 %copy-start = (bf16[128,2048]{1,0:T(8,128)(2,1)S(1)}, bf16[128,2048]{1,0:T(8,128)(2,1)}, u32[]{:S(2)}) copy-start(bf16[128,2048]{1,0:T(8,128)(2,1)} %param.15) | copy-start | bytes 1572868
  97.0 307.6 %all-gather.16.cloned.1.call-start = ((), (), s32[]{:S(2)}) async-start(), calls=%async_computation.15 | async-start | bytes 8912896 | tf_op jit(solution)/shard_map/all_gather | solution.py:168
  97.0 78.1 %copy-start.73 = (f32[2048]{0:T(1024)}, f32[2048]{0:T(1024)S(1)}, u32[]{:S(2)}) copy-start(f32[2048]{0:T(1024)S(1)} %convert_element_type.187) | copy-start | bytes 24580
  97.1 157.2 %copy-start.75 = (f32[2048]{0:T(1024)}, f32[2048]{0:T(1024)S(1)}, u32[]{:S(2)}) copy-start(f32[2048]{0:T(1024)S(1)} %convert_element_type.185) | copy-start | bytes 24580
  97.4 158.1 %copy-start.69 = (f32[128,64]{1,0:T(8,128)}, f32[128,64]{1,0:T(8,128)S(1)}, u32[]{:S(2)}) copy-start(f32[128,64]{1,0:T(8,128)S(1)} %get-tuple-element.74) | copy-start | bytes 98308
  97.4 158.1 %copy-start.71 = (f32[128,64]{1,0:T(8,128)}, f32[128,64]{1,0:T(8,128)S(1)}, u32[]{:S(2)}) copy-start(f32[128,64]{1,0:T(8,128)S(1)} %get-tuple-element.75) | copy-start | bytes 98308
  175.1 79.1 %copy-start.105 = (f32[128]{0:T(128)}, f32[128]{0:T(128)S(1)}, u32[]{:S(2)}) copy-start(f32[128]{0:T(128)S(1)} %get-tuple-element.76) | copy-start | bytes 1540
  257.6 153.6 %copy-start.36 = (bf16[128,16,128]{2,0,1:T(8,128)(2,1)}, bf16[128,16,128]{2,0,1:T(8,128)(2,1)S(1)}, u32[]{:S(2)}) copy-start(bf16[128,16,128]{2,0,1:T(8,128)(2,1)S(1)} %get-tuple-element.95) | copy-start | bytes 1572868
  258.6 224.4 %all-gather.18.cloned.1.call-start = ((), (), s32[]{:S(2)}) async-start(), calls=%async_computation.16 | async-start | bytes 8650752 | tf_op jit(solution)/shard_map/all_gather | solution.py:129
  259.5 228.4 %copy-start.77 = (f32[2048]{0:T(1024)}, f32[2048]{0:T(1024)S(1)}, u32[]{:S(2)}) copy-start(f32[2048]{0:T(1024)S(1)} %convert_element_type.194) | copy-start | bytes 24580
  269.6 141.6 %copy-start.38 = (pred[128,1152]{1,0:T(8,128)(4,1)}, pred[128,1152]{1,0:T(8,128)(4,1)S(1)}, u32[]{:S(2)}) copy-start(pred[128,1152]{1,0:T(8,128)(4,1)S(1)} %compare_and_fusion) | copy-start | bytes 442372
  488.9 148.0 %copy-start.32 = (bf16[128,2048]{1,0:T(8,128)(2,1)}, bf16[128,2048]{1,0:T(8,128)(2,1)S(1)}, u32[]{:S(2)}) copy-start(bf16[128,2048]{1,0:T(8,128)(2,1)S(1)} %multiply_convert_fusion.7) | copy-start | bytes 1572868
  500.1 159.3 %all-to-all-start = ((bf16[16,66,2048]{2,1,0:T(8,128)(2,1)}), bf16[16,66,2048]{2,1,0:T(8,128)(2,1)}, u32[]{:S(2)}, u32[]{:S(2)}) async-start(bf16[16,66,2048]{2,1,0:T(8,128)(2,1)} %reshape.406), calls=%async_computation | async-start | bytes 9437184 | tf_op jit(solution)/shard_map/all_to_all | solution.py:195
  659.4 91.3 %all-to-all-start.2 = ((bf16[16,66,2048]{2,1,0:T(8,128)(2,1)}), bf16[16,66,2048]{2,1,0:T(8,128)(2,1)}, u32[]{:S(2)}, u32[]{:S(2)}) async-start(bf16[16,66,2048]{2,1,0:T(8,128)(2,1)} %reshape.410), calls=%async_computation.2 | async-start | bytes 9437184 | tf_op jit(solution)/shard_map/all_to_all | solution.py:232
  790.9 108.6 %all-to-all-start.3 = ((bf16[16,66,2048]{2,1,0:T(8,128)(2,1)}), bf16[16,66,2048]{2,1,0:T(8,128)(2,1)}, u32[]{:S(2)}, u32[]{:S(2)}) async-start(bf16[16,66,2048]{2,1,0:T(8,128)(2,1)} %reshape.412), calls=%async_computation.3 | async-start | bytes 9437184 | tf_op jit(solution)/shard_map/all_to_all | solution.py:249
  827.6 93.8 %copy-start.93 = (s32[1024,1]{0,1:T(1,128)S(1)}, s32[1024,1]{0,1:T(1,128)}, u32[]{:S(2)}) copy-start(s32[1024,1]{0,1:T(1,128)} %copy-done.92) | copy-start | bytes 12292
  899.5 108.6 %all-to-all-start.1 = ((bf16[16,66,2048]{2,1,0:T(8,128)(2,1)}), bf16[16,66,2048]{2,1,0:T(8,128)(2,1)}, u32[]{:S(2)}, u32[]{:S(2)}) async-start(bf16[16,66,2048]{2,1,0:T(8,128)(2,1)} %reshape.408), calls=%async_computation.1 | async-start | bytes 9437184 | tf_op jit(solution)/shard_map/all_to_all | solution.py:204
  921.3 272.0 %reduce-scatter.22.cloned.1.call-start = ((), (), s32[]{:S(2)}) async-start(), calls=%async_computation.21 | async-start | bytes 8912896
  1033.7 97.5 %copy-start.25 = (f32[128,2048]{1,0:T(8,128)}, f32[128,2048]{1,0:T(8,128)S(1)}, u32[]{:S(2)}) copy-start(f32[128,2048]{1,0:T(8,128)S(1)} %get-tuple-element.54) | copy-start | bytes 3145732
  1071.6 230.8 %reduce-scatter.24.cloned.1.call-start = ((), (), s32[]{:S(2)}) async-start(), calls=%async_computation.22 | async-start | bytes 8912896
  1097.6 341.6 %reduce-scatter.26.cloned.1.call-start = ((), (), s32[]{:S(2)}) async-start(), calls=%async_computation.23 | async-start | bytes 1081344
  1120.6 607.7 %all-reduce.21.cloned.1.call-start = ((), (), s32[]{:S(2)}) async-start(), calls=%async_computation.24 | async-start | bytes 25165824 | tf_op jit(solution)/shard_map/psum | solution.py:256
  1131.1 784.6 %reduce-scatter.20.cloned.1.call-start = ((), (), s32[]{:S(2)}) async-start(), calls=%async_computation.20 | async-start | bytes 17301504 | tf_op jit(solution)/shard_map/reduce_scatter | solution.py:330
  1140.2 963.6 %reduce-scatter.14.cloned.1.call-start = ((), (), s32[]{:S(2)}) async-start(), calls=%async_computation.17 | async-start | bytes 17301504 | tf_op jit(solution)/shard_map/reduce_scatter | solution.py:327
  1212.5 1079.1 %reduce-scatter.16.cloned.1.call-start = ((), (), s32[]{:S(2)}) async-start(), calls=%async_computation.18 | async-start | bytes 17301504 | tf_op jit(solution)/shard_map/reduce_scatter | solution.py:328
  1225.3 1254.0 %reduce-scatter.18.cloned.1.call-start = ((), (), s32[]{:S(2)}) async-start(), calls=%async_computation.19 | async-start | bytes 17301504 | tf_op jit(solution)/shard_map/reduce_scatter | solution.py:329
  (113 other events, 769.3 us)
Sparse Core Ops, SparseCore 0:
  10.9 80.3 all-gather.7
  94.2 76.1 all-gather.13
  173.2 76.1 all-gather.11
  252.0 73.5 all-gather.9
  328.2 76.3 all-gather.15
  407.3 75.7 all-gather.17
  1071.7 121.5 reduce-scatter.21
  1197.9 104.3 reduce-scatter.23
  1304.6 134.5 reduce-scatter.25
  1442.6 285.6 all-reduce.20
  1731.3 184.3 reduce-scatter.19
  1918.5 185.3 reduce-scatter.13
  2106.8 184.7 reduce-scatter.15
  2294.4 184.7 reduce-scatter.17
where the time goes:
time: 2500 us; the launch traced here: 2490 us
  waiting for transfers between devices  1770 us (71%)
  blocking collectives  219 us (9%)
  matrix products  185 us (7%)
  local copies, waits for them, and re-layouts  174 us (7%)
  other arithmetic  65.5 us (3%)
  starting transfers between devices  54.2 us (2%)
    psum x1, waiting for transfers between devices, per_device(): lax.psum(local_gate[None].astype(jnp.bfloat16), 'grp').astype(jnp.float32)  288 us
    unnamed x17, waiting for transfers between devices  243 us
    reduce_scatter x1, waiting for transfers between devices, per_device(): lax.psum_scatter(local_query, ('grp', 'ep'), scatter_dimension=0, tiled=T...  188 us
    reduce_scatter x1, waiting for transfers between devices, per_device(): lax.psum_scatter(local_key, ('grp', 'ep'), scatter_dimension=0, tiled=True)  188 us
    reduce_scatter x1, waiting for transfers between devices, per_device(): lax.psum_scatter(local_value, ('grp', 'ep'), scatter_dimension=0, tiled=T...  188 us
    all_gather x1, blocking collectives, per_device(): lax.all_gather(w_router, ('grp', 'ep'), axis=0, tiled=True)  132 us
    reduce_scatter x1, waiting for transfers between devices, per_device(): lax.psum_scatter(local_output, ('grp', 'ep'), scatter_dimension=0, tiled=...  110 us
    unnamed x2, blocking collectives  87.5 us
  transfers between devices with their start and end apart: 18, of which 17 were waited for; matrix products, arithmetic and copies ran while one was open for 11% of the time, Pallas kernels for 0%

commit v1 on v0

--- a/solution.py
+++ b/solution.py
@@ -3,16 +3,803 @@
 import jax
 import jax.numpy as jnp
 from jax import lax
+from jax.experimental import pallas as pl
+from jax.experimental.pallas import tpu as pltpu
 from jax.sharding import PartitionSpec as P
 
 HEAD_DIM = 128
+MESH = pl.DeviceIdType.MESH
+BF = jnp.bfloat16
+F32 = jnp.float32
 
 
 eps = 1e-05
 theta_base = 10000.0
 
 
+def mm(a, b):
+    return jnp.dot(a, b, preferred_element_type=F32)
+
+
+def mm_nt(a, b):
+    return lax.dot_general(a, b, (((1,), (1,)), ((), ())), preferred_element_type=F32)
+
+
+def mm_tn(a, b):
+    return lax.dot_general(a, b, (((0,), (0,)), ((), ())), preferred_element_type=F32)
+
+
+class Place:
+    def __init__(self, ep_count):
+        self.grp = lax.axis_index("grp")
+        self.ep = lax.axis_index("ep")
+        self.count = ep_count
+        self.ring = ep_count // 2
+        self.half = self.ring // 2
+        self.core = self.ep % 2
+        y = (self.ep // 2) % 2
+        z = self.ep // 4
+        self.place = z + y * (self.ring - 1 - 2 * z)
+
+    def index(self, place, core):
+        y = place // self.half
+        z = place + y * (self.ring - 1 - 2 * place)
+        return (z * 2 + y) * 2 + core
+
+    def at(self, offset):
+        return (self.place + offset + self.ring) % self.ring
+
+    def chip(self, offset):
+        return self.index(self.at(offset), self.core)
+
+    def right(self):
+        return (self.grp, self.chip(1))
+
+    def left(self):
+        return (self.grp, self.chip(-1))
+
+    def sibling(self):
+        return (self.grp, self.index(self.place, 1 - self.core))
+
+    def across(self):
+        return (1 - self.grp, self.ep)
+
+    def peer(self, offset):
+        return (self.grp, (self.ep + offset + self.count) % self.count)
+
+
+def greet(devices):
+    barrier = pltpu.get_barrier_semaphore()
+    for device in devices:
+        pl.semaphore_signal(barrier, inc=1, device_id=device, device_id_type=MESH)
+    pl.semaphore_wait(barrier, len(devices))
+
+
+def remote(src, dst, send, recv, device):
+    return pltpu.make_async_remote_copy(
+        src_ref=src, dst_ref=dst, send_sem=send, recv_sem=recv, device_id=device, device_id_type=MESH
+    )
+
+
+class Gather:
+    def __init__(self, here, src, dst, sems):
+        self.here, self.src, self.dst = here, src, dst
+        self.ring_send, self.ring_recv, self.side_send, self.side_recv, self.own_sem = sems
+        self.rows = dst.shape[1] // 2
+        self.far = here.ring // 2
+        self.started = []
+
+    @staticmethod
+    def scratch(ep_count):
+        far = ep_count // 4
+        ring = pltpu.SemaphoreType.DMA((2, far, 2))
+        side = pltpu.SemaphoreType.DMA((2, far + 1, 2))
+        return [ring, ring, side, side, pltpu.SemaphoreType.DMA]
+
+    def block(self, index, part):
+        return self.dst.at[index, pl.ds(part * self.rows, self.rows)]
+
+    def go(self, copy):
+        copy.start()
+        self.started.append(copy)
+
+    def hops(self, way, part):
+        return self.far if way == part else self.far - 1
+
+    def ring_copy(self, way, step, part, src, index):
+        device = self.here.right() if way == 0 else self.here.left()
+        return remote(
+            src, self.block(index, part), self.ring_send.at[way, step, part], self.ring_recv.at[way, step, part], device
+        )
+
+    def side_copy(self, way, step, part, src, index):
+        return remote(
+            src,
+            self.block(index, part),
+            self.side_send.at[way, step, part],
+            self.side_recv.at[way, step, part],
+            self.here.sibling(),
+        )
+
+    def start(self):
+        here = self.here
+        for part in range(2):
+            src = self.src.at[pl.ds(part * self.rows, self.rows)]
+            for way in range(2):
+                if self.hops(way, part) > 0:
+                    self.go(self.ring_copy(way, 0, part, src, here.ep))
+            self.go(self.side_copy(0, 0, part, src, here.ep))
+        self.own = pltpu.make_async_copy(self.src, self.dst.at[here.ep], self.own_sem)
+        self.own.start()
+
+    def step(self, step):
+        here = self.here
+        for part in range(2):
+            for way in range(2):
+                if step < self.hops(way, part):
+                    index = here.chip(-1 - step if way == 0 else 1 + step)
+                    src = self.block(index, part)
+                    self.ring_copy(way, step, part, src, index).wait_recv()
+                    if step + 1 < self.hops(way, part):
+                        self.go(self.ring_copy(way, step + 1, part, src, index))
+                    self.go(self.side_copy(way, step + 1, part, src, index))
+
+    def side(self, step):
+        here = self.here
+        for part in range(2):
+            for way in range(2):
+                if (step < 0 and way == 0) or (0 <= step < self.hops(way, part)):
+                    offset = 0 if step < 0 else (-1 - step if way == 0 else 1 + step)
+                    index = here.index(here.at(offset), 1 - here.core)
+                    self.side_copy(way, step + 1, part, self.block(index, part), index).wait_recv()
+
+    def finish(self):
+        self.own.wait()
+        for copy in self.started:
+            copy.wait_send()
+
+
+class Exchange:
+    def __init__(self, here, src, dst, sems):
+        self.here, self.src, self.dst = here, src, dst
+        self.send, self.recv, self.own_sem = sems
+
+    @staticmethod
+    def scratch(ep_count):
+        return [
+            pltpu.SemaphoreType.DMA((ep_count,)),
+            pltpu.SemaphoreType.DMA((ep_count,)),
+            pltpu.SemaphoreType.DMA,
+        ]
+
+    def start(self):
+        here = self.here
+        self.own = pltpu.make_async_copy(self.src(here.ep), self.dst(here.ep), self.own_sem)
+        self.own.start()
+        self.copies = []
+        for offset in range(1, here.count):
+            device = here.peer(offset)
+            copy = remote(self.src(device[1]), self.dst(here.ep), self.send.at[offset], self.recv.at[offset], device)
+            copy.start()
+            self.copies.append(copy)
+
+    def arrive(self):
+        here = self.here
+        self.own.wait()
+        for offset in range(1, here.count):
+            source = here.peer(-offset)[1]
+            remote(
+                self.dst(source), self.dst(source), self.send.at[offset], self.recv.at[offset], here.peer(offset)
+            ).wait_recv()
+
+    def finish(self):
+        for copy in self.copies:
+            copy.wait_send()
+
+
+def ring_devices(here):
+    return [here.right(), here.left(), here.sibling()]
+
+
+def plane_devices(here):
+    return [here.peer(offset) for offset in range(1, here.count)]
+
+
+def comm_call(kernel, out_shape, scratch, name, collective_id, operands, vmem=False):
+    space = pltpu.VMEM if vmem else pl.ANY
+    spec = pl.BlockSpec(memory_space=space)
+    out_spec = [spec] * len(out_shape) if isinstance(out_shape, (list, tuple)) else spec
+    return pl.pallas_call(
+        kernel,
+        out_shape=out_shape,
+        in_specs=[spec] * len(operands),
+        out_specs=out_spec,
+        scratch_shapes=scratch,
+        compiler_params=pltpu.CompilerParams(
+            collective_id=collective_id, has_side_effects=True, vmem_limit_bytes=56 << 20
+        ),
+        name=name,
+    )(*operands)
+
+
+def split(refs, *sizes):
+    groups, start = [], 0
+    for size in sizes:
+        groups.append(refs[start : start + size])
+        start += size
+    return groups
+
+
+def gather_inputs(ep_count, rows_block, weights, small):
+    rows, width = rows_block.shape
+    kinds, depth, columns = weights.shape
+    mine = columns // ep_count
+    small_rows = small.shape[0]
+
+    def kernel(x_ref, w_ref, s_ref, x_out, w_out, s_out, *scratch):
+        gather_sems, w_sems, s_sems, cross = split(scratch, 5, 3, 3, 4)
+        here = Place(ep_count)
+        greet(plane_devices(here) + [here.across()])
+        first = pltpu.make_async_copy(s_ref, s_out.at[here.grp, here.ep], cross[0].at[2])
+        first.start()
+        swap = remote(s_ref, s_out.at[here.grp, here.ep], cross[1].at[0], cross[2].at[0], here.across())
+        swap.start()
+        gather = Gather(here, x_ref, x_out, gather_sems)
+        gather.start()
+        columns_of = Exchange(
+            here,
+            lambda e: w_ref.at[:, :, pl.ds(pl.multiple_of(e * mine, mine), mine)],
+            lambda e: w_out.at[here.grp, e],
+            w_sems,
+        )
+        columns_of.start()
+        first.wait()
+        remote(
+            s_ref, s_out.at[1 - here.grp, here.ep], cross[1].at[0], cross[2].at[0], here.across()
+        ).wait_recv()
+        swap.wait_send()
+        spread = Exchange(here, lambda e: s_out.at[:, here.ep], lambda e: s_out.at[:, e], s_sems)
+        copies = []
+        for offset in range(1, here.count):
+            copy = remote(
+                s_out.at[:, here.ep], s_out.at[:, here.ep], s_sems[0].at[offset], s_sems[1].at[offset], here.peer(offset)
+            )
+            copy.start()
+            copies.append(copy)
+        gather.step(0)
+        columns_of.arrive()
+        over = remote(w_out.at[here.grp], w_out.at[here.grp], cross[1].at[1], cross[2].at[1], here.across())
+        over.start()
+        for step in range(1, gather.far):
+            gather.step(step)
+        for offset in range(1, here.count):
+            source = here.peer(-offset)[1]
+            remote(
+                s_out.at[:, source], s_out.at[:, source], s_sems[0].at[offset], s_sems[1].at[offset], here.peer(offset)
+            ).wait_recv()
+        for step in range(-1, gather.far):
+            gather.side(step)
+        remote(
+            w_out.at[1 - here.grp], w_out.at[1 - here.grp], cross[1].at[1], cross[2].at[1], here.across()
+        ).wait_recv()
+        gather.finish()
+        columns_of.finish()
+        over.wait_send()
+        for copy in copies:
+            copy.wait_send()
+
+    dma = pltpu.SemaphoreType.DMA
+    return comm_call(
+        kernel,
+        [
+            jax.ShapeDtypeStruct((ep_count, rows, width), rows_block.dtype),
+            jax.ShapeDtypeStruct((2, ep_count, kinds, depth, mine), weights.dtype),
+            jax.ShapeDtypeStruct((2, ep_count, small_rows, small.shape[1]), small.dtype),
+        ],
+        Gather.scratch(ep_count)
+        + Exchange.scratch(ep_count)
+        + Exchange.scratch(ep_count)
+        + [dma((3,)), dma((2,)), dma((2,)), dma((1,))],
+        "gather_inputs",
+        1,
+        [rows_block, weights, small],
+    )
+
+
+def gather_both(ep_count, block, name, collective_id):
+    rows, width = block.shape
+
+    def kernel(x_ref, own_ref, other_ref, *scratch):
+        gather_sems, cross = split(scratch, 5, 4)
+        across_send, across_recv, hand_send, hand_recv = cross
+        here = Place(ep_count)
+        greet(ring_devices(here) + [here.across()])
+        gather = Gather(here, x_ref, own_ref, gather_sems)
+        gather.start()
+        sent = []
+        places = [0]
+
+        def cross_copy(slot, index, src):
+            return remote(src, other_ref.at[index], across_send.at[slot], across_recv.at[slot], here.across())
+
+        def hand_copy(slot, index):
+            return remote(
+                other_ref.at[index], other_ref.at[index], hand_send.at[slot], hand_recv.at[slot], here.sibling()
+            )
+
+        def start(copy):
+            copy.start()
+            sent.append(copy)
+
+        start(cross_copy(0, here.ep, x_ref))
+        slots = [(0, 0)]
+        for step in range(gather.far):
+            gather.step(step)
+            for way in range(2):
+                if step < gather.far - 1 or way == 0:
+                    offset = -1 - step if way == 0 else 1 + step
+                    slots.append((len(slots), offset))
+                    index = here.chip(offset)
+                    start(cross_copy(slots[-1][0], index, own_ref.at[index]))
+        for step in range(-1, gather.far):
+            gather.side(step)
+        for slot, offset in slots:
+            index = here.chip(offset)
+            cross_copy(slot, index, other_ref.at[index]).wait_recv()
+            start(hand_copy(slot, index))
+        for slot, offset in slots:
+            hand_copy(slot, here.index(here.at(offset), 1 - here.core)).wait_recv()
+        gather.finish()
+        for copy in sent:
+            copy.wait_send()
+
+    dma = pltpu.SemaphoreType.DMA
+    shape = jax.ShapeDtypeStruct((ep_count, rows, width), block.dtype)
+    slots = dma((ep_count // 2,))
+    return comm_call(
+        kernel, [shape, shape], Gather.scratch(ep_count) + [slots] * 4, name, collective_id, [block]
+    )
+
+
+def exchange(ep_count, tiles, name, collective_id):
+    def kernel(src, dst, *sems):
+        here = Place(ep_count)
+        greet(plane_devices(here))
+        swap = Exchange(here, lambda e: src.at[e], lambda e: dst.at[e], sems)
+        swap.start()
+        swap.arrive()
+        swap.finish()
+
+    return comm_call(
+        kernel,
+        jax.ShapeDtypeStruct(tiles.shape, tiles.dtype),
+        Exchange.scratch(ep_count),
+        name,
+        collective_id,
+        [tiles],
+    )
+
+
+def spread(ep_count, tile, name, collective_id):
+    def kernel(src, dst, *sems):
+        here = Place(ep_count)
+        greet(plane_devices(here))
+        swap = Exchange(here, lambda e: src, lambda e: dst.at[e], sems)
+        swap.start()
+        swap.arrive()
+        swap.finish()
+
+    return comm_call(
+        kernel,
+        jax.ShapeDtypeStruct((ep_count,) + tile.shape, tile.dtype),
+        Exchange.scratch(ep_count),
+        name,
+        collective_id,
+        [tile],
+    )
+
+
+def scatter_sum(ep_count, blocks, name, collective_id):
+    rows, width = blocks.shape[1:]
+    part_rows = rows // 2
+    far = ep_count // 4
+
+    def hops(way, part):
+        return far if way == part else far - 1
+
+    def kernel(src, out, joint, travel, landed, side_send, side_recv, ring_send, ring_recv):
+        here = Place(ep_count)
+        greet(ring_devices(here))
+        offsets = [far] + [sign * k for k in range(far - 1, 0, -1) for sign in (1, -1)] + [0]
+        sides = []
+        for slot, offset in enumerate(offsets):
+            index = here.index(here.at(offset), 1 - here.core)
+            copy = remote(src.at[index], joint.at[slot], side_send.at[slot], side_recv.at[slot], here.sibling())
+            copy.start()
+            sides.append(copy)
+        waited = set()
+
+        def term(offset, part):
+            offset = far if offset == -far else offset
+            slot = offsets.index(offset)
+            if slot not in waited:
+                waited.add(slot)
+                sides[slot].wait_recv()
+            index = here.chip(offset)
+            at = pl.ds(part * part_rows, part_rows)
+            return src[index, at].astype(F32) + joint[slot, at].astype(F32)
+
+        sends = []
+
+        def ring_copy(way, step, part):
+            at = pl.ds(part * part_rows, part_rows)
+            return remote(
+                travel.at[way, step, at],
+                landed.at[way, step, at],
+                ring_send.at[way, step, part],
+                ring_recv.at[way, step, part],
+                here.right() if way == 0 else here.left(),
+            )
+
+        for step in range(far):
+            for part in range(2):
+                for way in range(2):
+                    count = hops(way, part)
+                    if step < count:
+                        distance = count - step
+                        value = term(distance if way == 0 else -distance, part)
+                        at = pl.ds(part * part_rows, part_rows)
+                        if step > 0:
+                            ring_copy(way, step - 1, part).wait_recv()
+                            value = value + landed[way, step - 1, at].astype(F32)
+                        travel[way, step, at] = value.astype(travel.dtype)
+                        copy = ring_copy(way, step, part)
+                        copy.start()
+                        sends.append(copy)
+        for part in range(2):
+            value = term(0, part)
+            at = pl.ds(part * part_rows, part_rows)
+            for way in range(2):
+                count = hops(way, part)
+                ring_copy(way, count - 1, part).wait_recv()
+                value = value + landed[way, count - 1, at].astype(F32)
+            out[at] = value
+        for copy in sides + sends:
+            copy.wait_send()
+
+    dma = pltpu.SemaphoreType.DMA
+    ring = ep_count // 2
+    return comm_call(
+        kernel,
+        jax.ShapeDtypeStruct((rows, width), F32),
+        [
+            pltpu.VMEM((ring, rows, width), blocks.dtype),
+            pltpu.VMEM((2, far, rows, width), blocks.dtype),
+            pltpu.VMEM((2, far, rows, width), blocks.dtype),
+            dma((ring,)),
+            dma((ring,)),
+            dma((2, far, 2)),
+            dma((2, far, 2)),
+        ],
+        name,
+        collective_id,
+        [blocks],
+        vmem=True,
+    )
+
+
 def rms_scale(values, gain_vec):
+    return values * lax.rsqrt(jnp.mean(values * values, axis=-1, keepdims=True) + eps) * gain_vec
+
+
+def angles_of(position):
+    half_dim = HEAD_DIM // 2
+    frequency = theta_base ** (-2.0 * jnp.arange(half_dim, dtype=F32) / HEAD_DIM)
+    angles = position.astype(F32)[:, None] * frequency[None, :]
+    return jnp.cos(angles), jnp.sin(angles)
+
+
+def turn(values, cosine, sine):
+    half_dim = HEAD_DIM // 2
+    former, latter = values[:, :half_dim], values[:, half_dim:]
+    return jnp.concatenate([former * cosine - latter * sine, latter * cosine + former * sine], axis=-1)
+
+
+def attend(query, key, value, prompt_len, length, scale):
+    causal = jnp.tril(jnp.ones((prompt_len, prompt_len), jnp.bool_))
+    small_causal = jnp.tril(jnp.ones((length, length), jnp.bool_))
+    q_p, k_p, v_p = query[:prompt_len], key[:prompt_len], value[:prompt_len]
+    q_c, k_c, v_c = query[prompt_len:], key[prompt_len:], value[prompt_len:]
+    s_p = jnp.where(causal, mm_nt(q_p, k_p) * scale, -1e30)
+    top = jnp.max(s_p, axis=-1, keepdims=True)
+    e_p = jnp.exp(s_p - top)
+    total = jnp.sum(e_p, axis=-1, keepdims=True)
+    out_p = mm((e_p / total).astype(BF), v_p)
+    log_p = top + jnp.log(total)
+    shape = (-1, length, query.shape[1])
+    s_c = mm_nt(q_c, k_p) * scale
+    s_o = jnp.einsum("nqd,nkd->nqk", q_c.reshape(shape), k_c.reshape(shape), preferred_element_type=F32) * scale
+    s_o = jnp.where(small_causal, s_o, -1e30).reshape(-1, length)
+    top = jnp.maximum(jnp.max(s_c, axis=-1, keepdims=True), jnp.max(s_o, axis=-1, keepdims=True))
+    e_c = jnp.exp(s_c - top)
+    e_o = jnp.exp(s_o - top)
+    total = jnp.sum(e_c, axis=-1, keepdims=True) + jnp.sum(e_o, axis=-1, keepdims=True)
+    out_c = mm((e_c / total).astype(BF), v_p)
+    own = jnp.einsum(
+        "nqk,nkd->nqd",
+        (e_o / total).astype(BF).reshape(-1, length, length),
+        v_c.reshape(shape),
+        preferred_element_type=F32,
+    )
+    out_c = out_c + own.reshape(out_c.shape)
+    log_c = top + jnp.log(total)
+    return jnp.concatenate([out_p, out_c]), jnp.concatenate([log_p, log_c])
+
+
+def attend_back(query, key, value, grad, logs, prompt_len, length, scale):
+    causal = jnp.tril(jnp.ones((prompt_len, prompt_len), jnp.bool_))
+    small_causal = jnp.tril(jnp.ones((length, length), jnp.bool_))
+    q_p, k_p, v_p, g_p, l_p = (a[:prompt_len] for a in (query, key, value, grad, logs))
+    q_c, k_c, v_c, g_c, l_c = (a[prompt_len:] for a in (query, key, value, grad, logs))
+    shape = (-1, length, query.shape[1])
+    w_p = jnp.where(causal, jnp.exp(mm_nt(q_p, k_p) * scale - l_p), 0.0)
+    d_p = mm_nt(g_p, v_p)
+    ds_p = (w_p * (d_p - jnp.sum(w_p * d_p, axis=-1, keepdims=True))).astype(BF)
+    w_c = jnp.exp(mm_nt(q_c, k_p) * scale - l_c)
+    d_c = mm_nt(g_c, v_p)
+    q_n, k_n, v_n, g_n = (a.reshape(shape) for a in (q_c, k_c, v_c, g_c))
+    s_o = jnp.einsum("nqd,nkd->nqk", q_n, k_n, preferred_element_type=F32) * scale
+    w_o = jnp.where(small_causal, jnp.exp(s_o - l_c.reshape(-1, length, 1)), 0.0)
+    d_o = jnp.einsum("nqd,nkd->nqk", g_n, v_n, preferred_element_type=F32)
+    inner = jnp.sum(w_c * d_c, axis=-1, keepdims=True) + jnp.sum(w_o * d_o, axis=-1).reshape(-1, 1)
+    ds_c = (w_c * (d_c - inner)).astype(BF)
+    ds_o = (w_o * (d_o - inner.reshape(-1, length, 1))).astype(BF)
+
+    def over(eq, a, b):
+        return jnp.einsum(eq, a, b, preferred_element_type=F32)
+
+    dq_p = mm(ds_p, k_p)
+    dq_c = mm(ds_c, k_p) + over("nqk,nkd->nqd", ds_o, k_n).reshape(q_c.shape)
+    dk_p = mm_tn(ds_p, q_p) + mm_tn(ds_c, q_c)
+    dk_c = over("nqk,nqd->nkd", ds_o, q_n).reshape(q_c.shape)
+    dv_p = mm_tn(w_p.astype(BF), g_p) + mm_tn(w_c.astype(BF), g_c)
+    dv_c = over("nqk,nqd->nkd", w_o.astype(BF), g_n).reshape(q_c.shape)
+    return (
+        jnp.concatenate([dq_p, dq_c]) * scale,
+        jnp.concatenate([dk_p, dk_c]) * scale,
+        jnp.concatenate([dv_p, dv_c]),
+    )
+
+
+def per_device(
+    block_input,
+    cotangent,
+    routes,
+    w_query,
+    w_key,
+    w_value,
+    w_output,
+    w_router,
+    gain_attn,
+    gain_query,
+    gain_key,
+    gain_mlp,
+    w_gate,
+    w_up,
+    w_down,
+):
+    rows, width = block_input.shape
+    top_count = routes.shape[1]
+    ep_count = lax.axis_size("ep")
+    grp_count = lax.axis_size("grp")
+    me = lax.axis_index("ep")
+    my_group = lax.axis_index("grp")
+    tokens = rows * ep_count
+    prompt_len = tokens // 2
+    capacity = min(rows, rows * top_count * 33 // (32 * ep_count))
+    cols = width // ep_count
+    scale = HEAD_DIM ** (-0.5)
+    depth = w_query.shape[0]
+
+    chosen = jnp.any(routes[:, :, None] == jnp.arange(ep_count, dtype=jnp.int32), axis=1)
+    per_row = 128
+    router_rows = depth * ep_count // per_row
+    gains = jnp.concatenate([gain_attn, gain_query, gain_key, gain_mlp])
+    gain_rows = gains.shape[0] // per_row
+    small = jnp.concatenate(
+        [
+            w_router.reshape(router_rows, per_row),
+            gains.reshape(gain_rows, per_row),
+            jnp.zeros((16 - router_rows - gain_rows, per_row), BF),
+            chosen.T.astype(BF),
+        ]
+    )
+    weights = jnp.stack([w_query, w_key, w_value])
+    full_output = lax.all_gather(w_output, ("grp", "ep"), axis=0, tiled=True)
+    cot_both = lax.all_gather(cotangent, ("grp", "ep"), axis=0, tiled=True)
+
+    x_all, w_cols, smalls = gather_inputs(ep_count, block_input, weights, small)
+    x_all = x_all.reshape(tokens, width)
+    w_q, w_k, w_v = (w_cols[:, :, i].reshape(width, cols) for i in range(3))
+    smalls = smalls.reshape(grp_count * ep_count, small.shape[0], per_row)
+    full_router = smalls[:, :router_rows].reshape(width, ep_count)
+    gains = smalls[:, router_rows : router_rows + gain_rows].reshape(-1, 4, depth).transpose(1, 0, 2).reshape(4, width)
+    gain_first, gain_qnorm, gain_knorm, gain_second = (gains[i].astype(F32) for i in range(4))
+    chosen_all = smalls[:, 16:].reshape(grp_count, ep_count, ep_count, rows)
+
+    token = jnp.arange(tokens, dtype=jnp.int32)
+    position = jnp.where(token < prompt_len, token, prompt_len + (token - prompt_len) % rows)
+    cosine, sine = angles_of(position)
+    x_wide = x_all.astype(F32)
+    normed_all = rms_scale(x_wide, gain_first).astype(BF)
+    q_lin = mm(normed_all, w_q)
+    k_lin = mm(normed_all, w_k)
+    value = mm(normed_all, w_v).astype(BF)
+    squares = jnp.stack([jnp.sum(q_lin * q_lin, axis=-1), jnp.sum(k_lin * k_lin, axis=-1)])
+    squares = jnp.sum(spread(ep_count, squares.reshape(-1, per_row), "spread_squares", 2), axis=0).reshape(2, tokens)
+    r_q, r_k = (lax.rsqrt(squares[i] / width + eps)[:, None] for i in range(2))
+    gain_q = lax.dynamic_slice(gain_qnorm, (me * cols,), (cols,))
+    gain_k = lax.dynamic_slice(gain_knorm, (me * cols,), (cols,))
+    n_q, n_k = q_lin * r_q, k_lin * r_k
+    query = turn(n_q * gain_q, cosine, sine).astype(BF)
+    key = turn(n_k * gain_k, cosine, sine).astype(BF)
+    attended, logs = attend(query, key, value, prompt_len, rows, scale)
+    tiles = exchange(ep_count, attended.astype(BF).reshape(ep_count, rows, cols), "exchange_attended", 3)
+    att_loc = tiles.transpose(1, 0, 2).reshape(rows, width)
+
+    inputs = block_input.astype(F32)
+    residual = inputs + mm(att_loc, full_output)
+    r_m = lax.rsqrt(jnp.mean(residual * residual, axis=-1, keepdims=True) + eps)
+    n_m = residual * r_m
+    normed_mlp = (n_m * gain_second).astype(BF)
+    own_rows, other_rows = gather_both(ep_count, normed_mlp, "gather_normed", 4)
+
+    pair = 2 * rows
+    slots = -(-2 * capacity // 16) * 16
+    chips = ep_count // 2
+
+    def picks(group):
+        mine = lax.dynamic_index_in_dim(chosen_all, group, 0, keepdims=False)[:, me]
+        mine = mine.reshape(chips, pair)
+        slot = jnp.cumsum(mine.astype(jnp.int32), axis=1) - 1
+        hot = (slot[:, None, :] == jnp.arange(slots, dtype=jnp.int32)[None, :, None]) & (mine[:, None, :] > 0)
+        return hot
+
+    def gate_of(normed_rows):
+        probs = jax.nn.softmax(mm(normed_rows, full_router), axis=-1)
+        return lax.dynamic_index_in_dim(probs, me, 1, keepdims=False)
+
+    def take(hot, values):
+        return jnp.einsum(
+            "csp,cpd->csd", hot, values.reshape(chips, pair, width), preferred_element_type=F32
+        ).astype(BF).reshape(-1, width)
+
+    def give(hot, values):
+        return jnp.einsum(
+            "csp,csd->cpd", hot, values.reshape(chips, slots, width), preferred_element_type=F32
+        ).reshape(tokens, width)
+
+    gate_w, up_w, down_w = w_gate[0], w_up[0], w_down[0]
+    cot_both = cot_both.reshape(grp_count, tokens, width)
+
+    def expert(normed_rows, cot_rows, group):
+        hot = picks(group)
+        hot_low = hot.astype(BF)
+        gate = gate_of(normed_rows)
+        gate_rows = jnp.sum(jnp.where(hot, gate.reshape(chips, 1, pair), 0.0), axis=2).reshape(-1, 1)
+        units = take(hot_low, normed_rows)
+        cot_units = take(hot_low, cot_rows).astype(F32)
+        grad_out = (gate_rows * cot_units).astype(BF)
+        gate_pre = mm(units, gate_w)
+        up_pre = mm(units, up_w)
+        sigma = jax.nn.sigmoid(gate_pre)
+        hidden = (gate_pre * sigma * up_pre).astype(BF)
+        grad_hidden = mm_nt(grad_out, down_w)
+        grad_gate_pre = (grad_hidden * up_pre * sigma * (1.0 + gate_pre * (1.0 - sigma))).astype(BF)
+        grad_up_pre = (grad_hidden * gate_pre * sigma).astype(BF)
+        return hot, hot_low, gate, units, cot_units, grad_out, hidden, grad_gate_pre, grad_up_pre
+
+    own_rows = own_rows.reshape(tokens, width)
+    cot_own = lax.dynamic_index_in_dim(cot_both, my_group, 0, keepdims=False)
+    hot, hot_low, gate, units, cot_units, grad_out, hidden, grad_gate_pre, grad_up_pre = expert(
+        own_rows, cot_own, my_group
+    )
+    result = mm(hidden, down_w).astype(BF)
+    gate_grad_rows = jnp.sum(cot_units * result.astype(F32), axis=-1).reshape(chips, slots, 1)
+    gate_grad = jnp.sum(jnp.where(hot, gate_grad_rows, 0.0), axis=1).reshape(ep_count, 1, rows)
+    grad_units = (mm_nt(grad_gate_pre, gate_w) + mm_nt(grad_up_pre, up_w)).astype(BF)
+    partial_units = give(hot_low, grad_units).astype(BF).reshape(ep_count, rows, width)
+    partial_result = (gate[:, None] * give(hot_low, result)).astype(BF)
+    mixture = lax.psum_scatter(partial_result, "ep", scatter_dimension=0, tiled=True).astype(F32)
+    block_output = (residual + mixture).astype(BF)
+    d_normed_mlp = scatter_sum(ep_count, partial_units, "scatter_units", 5)
+    gate_grads = exchange(
+        ep_count, jnp.broadcast_to(gate_grad, (ep_count, 8, rows)), "exchange_gate_grads", 6
+    )[:, 0]
+
+    _, _, _, units_2, _, grad_out_2, hidden_2, grad_gate_pre_2, grad_up_pre_2 = expert(
+        other_rows.reshape(tokens, width),
+        lax.dynamic_index_in_dim(cot_both, 1 - my_group, 0, keepdims=False),
+        1 - my_group,
+    )
+    grad_gate = (mm_tn(units, grad_gate_pre) + mm_tn(units_2, grad_gate_pre_2))[None]
+    grad_up = (mm_tn(units, grad_up_pre) + mm_tn(units_2, grad_up_pre_2))[None]
+    grad_down = (mm_tn(hidden, grad_out) + mm_tn(hidden_2, grad_out_2))[None]
+
+    probs = jax.nn.softmax(mm(normed_mlp, full_router), axis=-1)
+    d_probs = gate_grads.T
+    d_logits = (probs * (d_probs - jnp.sum(probs * d_probs, axis=-1, keepdims=True))).astype(BF)
+    local_router = mm_tn(normed_mlp, d_logits)
+    d_normed_mlp = d_normed_mlp + mm_nt(d_logits, full_router)
+    local_gain_mlp = jnp.sum(d_normed_mlp * n_m, axis=0)
+    d_n = d_normed_mlp * gain_second
+    d_residual = cotangent.astype(F32) + r_m * (d_n - n_m * jnp.mean(n_m * d_n, axis=-1, keepdims=True))
+    d_proj = d_residual.astype(BF)
+    d_attended = mm_nt(d_proj, full_output).astype(BF)
+    local_output = mm_tn(att_loc, d_proj).astype(BF)
+    grad_output = lax.psum_scatter(local_output, ("grp", "ep"), scatter_dimension=0, tiled=True).astype(F32)
+    d_attended = exchange(
+        ep_count, d_attended.reshape(rows, ep_count, cols).transpose(1, 0, 2), "exchange_d_attended", 7
+    ).reshape(tokens, cols)
+
+    d_query, d_key, d_value = attend_back(query, key, value, d_attended, logs, prompt_len, rows, scale)
+    d_query = turn(d_query, cosine, -sine)
+    d_key = turn(d_key, cosine, -sine)
+    gain_grad_q = jnp.sum(d_query * n_q, axis=0)
+    gain_grad_k = jnp.sum(d_key * n_k, axis=0)
+    d_nq, d_nk = d_query * gain_q, d_key * gain_k
+    dots = jnp.stack([jnp.sum(d_nq * n_q, axis=-1), jnp.sum(d_nk * n_k, axis=-1)])
+    dots = jnp.sum(spread(ep_count, dots.reshape(-1, per_row), "spread_dots", 8), axis=0).reshape(2, tokens) / width
+    d_q_lin = (r_q * (d_nq - n_q * dots[0][:, None])).astype(BF)
+    d_k_lin = (r_k * (d_nk - n_k * dots[1][:, None])).astype(BF)
+    d_v_lin = d_value.astype(BF)
+    d_lin = jnp.concatenate([d_q_lin, d_k_lin, d_v_lin], axis=1)
+    w_all = jnp.concatenate([w_q, w_k, w_v], axis=1)
+    partial_normed = mm_nt(d_lin, w_all).astype(BF).reshape(ep_count, rows, width)
+    d_normed = scatter_sum(ep_count, partial_normed, "scatter_normed", 9)
+    r_a = lax.rsqrt(jnp.mean(inputs * inputs, axis=-1, keepdims=True) + eps)
+    n_a = inputs * r_a
+    local_gain_attn = jnp.sum(d_normed * n_a, axis=0)
+    d_n = d_normed * gain_first
+    input_grad = d_residual + r_a * (d_n - n_a * jnp.mean(n_a * d_n, axis=-1, keepdims=True))
+
+    grad_w = mm_tn(normed_all, d_lin).astype(BF)
+    grad_w = lax.psum_scatter(
+        grad_w.reshape(grp_count, ep_count * depth, 3 * cols), "grp", scatter_dimension=0, tiled=True
+    )
+    grad_w = exchange(ep_count, grad_w.reshape(ep_count, depth, 3 * cols), "exchange_grad_w", 10)
+    grad_w = grad_w.reshape(ep_count, depth, 3, cols).transpose(2, 1, 0, 3).reshape(3, depth, width).astype(F32)
+    grad_router = lax.psum_scatter(local_router, ("grp", "ep"), scatter_dimension=0, tiled=True)
+    zeros = jnp.zeros((width,), F32)
+    gain_sums = jnp.stack(
+        [
+            local_gain_attn,
+            lax.dynamic_update_slice(zeros, gain_grad_q, (me * cols,)),
+            lax.dynamic_update_slice(zeros, gain_grad_k, (me * cols,)),
+            local_gain_mlp,
+        ]
+    )
+    gain_sums = lax.psum(gain_sums, ("grp", "ep"))
+    gain_sums = lax.dynamic_slice(gain_sums, (0, (my_group * ep_count + me) * depth), (4, depth))
+    return (
+        block_output,
+        input_grad,
+        grad_w[0],
+        grad_w[1],
+        grad_w[2],
+        grad_output,
+        grad_router,
+        gain_sums[0],
+        gain_sums[1],
+        gain_sums[2],
+        gain_sums[3],
+        grad_gate,
+        grad_up,
+        grad_down,
+    )
+
+
+def plain_scale(values, gain_vec):
     return values * lax.rsqrt(jnp.mean(values * values, axis=-1, keepdims=True) + eps) * gain_vec
 
 
@@ -37,7 +824,7 @@
     return jnp.where(allowed[None], raw_scores, -1e30)
 
 
-def attend(query, keys, values, allowed, scale, head_group):
+def plain_attend(query, keys, values, allowed, scale, head_group):
     outputs = []
     log_totals = []
     for head_start in range(0, query.shape[1], head_group):
@@ -56,7 +843,7 @@
     return (jnp.concatenate(outputs, axis=1), jnp.concatenate(log_totals, axis=0))
 
 
-def attend_back(query, keys, values, grad_out, log_totals, allowed, scale, head_group):
+def plain_attend_back(query, keys, values, grad_out, log_totals, allowed, scale, head_group):
     query_grads = []
     key_grads = []
     value_grads = []
@@ -95,7 +882,7 @@
     )
 
 
-def per_device(
+def per_device_plain(
     block_input,
     cotangent,
     routes,
@@ -154,10 +941,10 @@
     )
 
     def prepare(linear, gain_vec):
-        return rotate(rms_scale(linear, gain_vec), position)
+        return rotate(plain_scale(linear, gain_vec), position)
 
     inputs = block_input.astype(jnp.float32)
-    normed = rms_scale(inputs, gain_first).astype(jnp.bfloat16)
+    normed = plain_scale(inputs, gain_first).astype(jnp.bfloat16)
     query_lin = jnp.dot(normed, full_query, preferred_element_type=jnp.float32)
     key_lin = jnp.dot(normed, full_key, preferred_element_type=jnp.float32)
     value_lin = jnp.dot(normed, full_value, preferred_element_type=jnp.float32)
@@ -171,10 +958,10 @@
     keys = jnp.concatenate([shared[0][:prompt_len], key_low]).reshape(-1, head_count, HEAD_DIM)
     values = jnp.concatenate([shared[1][:prompt_len], value_low]).reshape(-1, head_count, HEAD_DIM)
     query = query_low.reshape(row_count, head_count, HEAD_DIM)
-    attn_out, log_totals = attend(query, keys, values, allowed, scale, head_group)
+    attn_out, log_totals = plain_attend(query, keys, values, allowed, scale, head_group)
     attended = attn_out.reshape(row_count, model_width).astype(jnp.bfloat16)
     residual = inputs + jnp.dot(attended, full_output, preferred_element_type=jnp.float32)
-    normed_mlp = rms_scale(residual, gain_second).astype(jnp.bfloat16)
+    normed_mlp = plain_scale(residual, gain_second).astype(jnp.bfloat16)
     logits = jnp.dot(normed_mlp, full_router, preferred_element_type=jnp.float32)
     probs = jax.nn.softmax(logits, axis=-1)
     picks = routes[:, :, None] == jnp.arange(ep_count, dtype=jnp.int32)[None, None, :]
@@ -267,7 +1054,7 @@
     grad_normed_mlp = grad_normed_mlp + jnp.einsum(
         "re,de->rd", grad_logits, back_router, preferred_element_type=jnp.float32
     )
-    unused_mlp, second_back = jax.vjp(rms_scale, residual, gain_second)
+    unused_mlp, second_back = jax.vjp(plain_scale, residual, gain_second)
     grad_from_mlp, local_gain_mlp = second_back(grad_normed_mlp)
     grad_residual = grad_top + grad_from_mlp
     grad_proj = grad_residual.astype(jnp.bfloat16)
@@ -276,7 +1063,7 @@
         "re,de->rd", grad_proj, back_output, preferred_element_type=jnp.float32
     )
     grad_attended = grad_attended.astype(jnp.bfloat16).reshape(row_count, head_count, HEAD_DIM)
-    grad_query_rot, grad_keys, grad_values = attend_back(
+    grad_query_rot, grad_keys, grad_values = plain_attend_back(
         query, keys, values, grad_attended, log_totals, allowed, scale, head_group
     )
     grad_keys = grad_keys.reshape(-1, model_width)
@@ -320,7 +1107,7 @@
     grad_normed = grad_normed + jnp.einsum(
         "re,de->rd", grad_value_lin, back_value, preferred_element_type=jnp.float32
     )
-    unused_first, first_back = jax.vjp(rms_scale, inputs, gain_first)
+    unused_first, first_back = jax.vjp(plain_scale, inputs, gain_first)
     grad_from_attn, local_gain_attn = first_back(grad_normed)
     input_grad = grad_residual + grad_from_attn
     summed_grads = (
@@ -353,41 +1140,11 @@
 
 
 def solution(mesh):
+    both = ("grp", "ep")
     return jax.shard_map(
-        per_device,
+        per_device if mesh.shape["grp"] == 2 else per_device_plain,
         mesh=mesh,
-        in_specs=(
-            P(("grp", "ep"), None),
-            P(("grp", "ep"), None),
-            P(("grp", "ep"), None),
-            P(("grp", "ep"), None),
-            P(("grp", "ep"), None),
-            P(("grp", "ep"), None),
-            P(("grp", "ep"), None),
-            P(("grp", "ep"), None),
-            P(("grp", "ep")),
-            P(("grp", "ep")),
-            P(("grp", "ep")),
-            P(("grp", "ep")),
-            P("ep", None, None),
-            P("ep", None, None),
-            P("ep", None, None),
-        ),
-        out_specs=(
-            P(("grp", "ep"), None),
-            P(("grp", "ep"), None),
-            P(("grp", "ep"), None),
-            P(("grp", "ep"), None),
-            P(("grp", "ep"), None),
-            P(("grp", "ep"), None),
-            P(("grp", "ep"), None),
-            P(("grp", "ep")),
-            P(("grp", "ep")),
-            P(("grp", "ep")),
-            P(("grp", "ep")),
-            P("ep", None, None),
-            P("ep", None, None),
-            P("ep", None, None),
-        ),
+        in_specs=(P(both, None),) * 8 + (P(both),) * 4 + (P("ep", None, None),) * 3,
+        out_specs=(P(both, None),) * 7 + (P(both),) * 4 + (P("ep", None, None),) * 3,
         check_vma=False,
     )

time: 2500 us -> 938 us (0.38)
  waiting for transfers between devices: 1770 us -> 70.2 us
  Pallas kernels: 0 us -> 449 us
  blocking collectives: 219 us -> 40.7 us
  local copies, waits for them, and re-layouts: 174 us -> 41.3 us
  matrix products: 185 us -> 239 us
  starting transfers between devices: 54.2 us -> 0.45 us
    reduce_scatter x3 -> x2, waiting for transfers between devices: 564 us -> 0.01 us  [the longest x1 0.01 us: per_device(): lax.psum_scatter(grad_w.reshape(grp_count, ep_count * depth, 3 * cols), '...]
    pallas_call x0 -> x10, Pallas kernels: none -> 449 us  [comm_call(): pl.pallas_call(kernel, out_shape=out_shape, in_specs=[spec] * len(operand...]
    all_gather x6 -> x2, waiting for transfers between devices: 369 us -> 0.01 us  [the longest x1 0.01 us: per_device(): full_output = lax.all_gather(w_output, ('grp', 'ep'), axis=0, tiled=True)]
    psum x1 -> x0, waiting for transfers between devices: 288 us -> none  [per_device(): lax.psum(local_gate[None].astype(jnp.bfloat16), 'grp').astype(jnp.float32)]
    unnamed x17 -> x7, waiting for transfers between devices: 243 us -> 1.45 us
    all_to_all x4 -> x0, waiting for transfers between devices: 199 us -> none  [the longest x1 71.9 us: per_device(): lax.all_to_all(grad_units, 'ep', split_axis=0, concat_axis=0, tiled=True)]
    all_gather x1 -> x0, blocking collectives: 132 us -> none  [per_device(): lax.all_gather(w_router, ('grp', 'ep'), axis=0, tiled=True)]
    unnamed x2 -> x0, blocking collectives: 87.5 us -> none
  transfers between devices with their start and end apart: 18 -> 6, of which waited for: 17 -> 1; matrix products, arithmetic and copies ran while one was open for 11% -> 32% of each run, Pallas kernels for 0% -> 46%
where the time goes in v1:
time: 938 us; the launch traced here: 929 us
  Pallas kernels  449 us (48%)
  matrix products  239 us (25%)
  other arithmetic  72 us (8%)
  waiting for transfers between devices  70.2 us (7%)
  local copies, waits for them, and re-layouts  41.3 us (4%)
  blocking collectives  40.7 us (4%)
  between operations  16.2 us (2%)
    pallas_call x10, Pallas kernels, comm_call(): pl.pallas_call(kernel, out_shape=out_shape, in_specs=[spec] * len(operand...  449 us
    dot_general x12, matrix products, mm_tn(): lax.dot_general(a, b, (((0,), (0,)), ((), ())), preferred_element_type=F32)  83.3 us
    reduce_scatter x1, waiting for transfers between devices, per_device(): lax.psum_scatter(local_output, ('grp', 'ep'), scatter_dimension=0, tiled=...  68.7 us
    dot_general x16, matrix products, mm(): return jnp.dot(a, b, preferred_element_type=F32)  66.5 us
    dot_general x11, matrix products, mm_nt(): lax.dot_general(a, b, (((1,), (1,)), ((), ())), preferred_element_type=F32)  53.3 us
    psum x1, blocking collectives, per_device(): gain_sums = lax.psum(gain_sums, ('grp', 'ep'))  40.7 us
    dot_general x4, matrix products, take(): jnp.einsum('csp,cpd->csd', hot, values.reshape(chips, pair, width), prefe...  21.4 us
  transfers between devices with their start and end apart: 6, of which 1 were waited for; matrix products, arithmetic and copies ran while one was open for 32% of the time, Pallas kernels for 46%

profile of v1, /device:TPU:0, one launch (start us, length us, event | category | flops | bytes accessed | tf_op | source)
XLA Modules:
  0.0 929.3 jit_solution(10020745921646917274)
XLA Ops:
  13.9 113.4 %gather_inputs.1 = (bf16[16,128,2048]{2,1,0:T(8,128)(2,1)}, bf16[2,16,3,64,128]{4,3,2,1,0:T(8,128)(2,1)}, bf16[2,16,32,128]{3,2,1,0:T(8,128)(2,1)}) custom-call(bf16[128,2048]{1,0:T(8,128)(2,1)} %x_ref.1, bf16[3,64,2048]{2,1,0:T(8,128)(2,1)} %pad_maximum_fusion.2.w_ref, bf16[32,128]{1,0:T(8,128)(2,1)} %pad_maximum_fusion.9.s_ref), custom_call_target="tpu_custom_call" | custom-call | tf_op jit(solution)/shard_map/gather_inputs/pallas_call | solution.py:212
  135.8 9.3 %multiply_convert_fusion = bf16[16,128,2048]{2,1,0:T(8,128)(2,1)} fusion(f32[2048]{0:T(1024)S(1)} %reshape.569, f32[16,128]{1,0:T(8,128)S(1)} %get-tuple-element.85, bf16[16,128,2048]{2,1,0:T(8,128)(2,1)} %get-tuple-element.19), kind=kLoop, calls=%fused_computation.5 | loop fusion | flops 16777216 | bytes 16793600 | tf_op jit(solution)/shard_map/convert_element_type | solution.py:634
  145.1 6.4 multiply_reduce_fusion.12
  155.3 12.7 %spread_squares.1 = f32[16,32,128]{2,1,0:T(8,128)} custom-call(f32[32,128]{1,0:T(8,128)} %reshape.540.src), custom_call_target="tpu_custom_call" | custom-call | tf_op jit(solution)/shard_map/spread_squares/pallas_call | solution.py:212
  187.4 26.6 %exchange_attended.1 = bf16[16,128,128]{2,1,0:T(8,128)(2,1)} custom-call(bf16[16,128,128]{2,1,0:T(8,128)(2,1)} %bitcast.286), custom_call_target="tpu_custom_call" | custom-call | tf_op jit(solution)/shard_map/exchange_attended/pallas_call | solution.py:212
  222.9 117.9 %gather_normed.1 = (bf16[16,128,2048]{2,1,0:T(8,128)(2,1)}, bf16[16,128,2048]{2,1,0:T(8,128)(2,1)}) custom-call(bf16[128,2048]{1,0:T(8,128)(2,1)} %multiply_convert_fusion.15.x_ref), custom_call_target="tpu_custom_call" | custom-call | tf_op jit(solution)/shard_map/gather_normed/pallas_call | solution.py:212
  360.4 7.4 multiply_convert_fusion.7
  382.0 9.4 %fusion.1 = bf16[2048,2048]{1,0:T(8,128)(2,1)} fusion(f32[2048]{0:T(1024)S(1)} %reshape.569, f32[2048]{0:T(1024)S(1)} %get-tuple-element.84, bf16[16,128,2048]{2,1,0:T(8,128)(2,1)} %get-tuple-element.19), kind=kLoop, calls=%fused_computation.2 | loop fusion | flops 16777216 | bytes 16793600 | tf_op jit(solution)/shard_map/convert_element_type | solution.py:634
  392.8 7.9 convolution_convert_fusion.4
  400.7 9.7 %constant_dynamic-slice_fusion = (bf16[1,2048,2048]{2,1,0:T(8,128)(2,1)}, bf16[1,2048,2048]{2,1,0:T(8,128)(2,1)S(1)}) fusion(bf16[2,2048,2048]{2,1,0:T(8,128)(2,1)} %bitcast.252, s32[]{:T(128)S(6)} %select_n.156, s32[]{:T(128)S(6)} %select_n.148), kind=kLoop, calls=%fused_computation.278 | loop fusion | bytes 33554440 | tf_op jit(solution)/shard_map/jit(dynamic_index_in_dim)/dynamic_slice | solution.py:722
  416.3 7.8 exchange_gate_grads.1
  428.6 9.6 %multiply_convert_fusion.5 = (bf16[1152,1024]{1,0:T(8,128)(2,1)S(1)}, bf16[1152,1024]{1,0:T(8,128)(2,1)S(1)}) fusion(f32[1152,1024]{1,0:T(8,128)} %copy-done.90, f32[1152,1024]{1,0:T(8,128)} %get-tuple-element.103, bf16[1152,2048]{1,0:T(8,128)(2,1)S(1)} %bitcast.273, bf16[1,1024,2048]{2,1,0:T(8,128)(2,1)S(1)} %copy-done.85), kind=kOutput, calls=%fused_computation.29 | convolution fusion | flops 4847173632 | bytes 23068672 | tf_op jit(solution)/shard_map/dot_general | solution.py:25
  438.3 7.6 fusion.19
  445.9 8.2 add_convert_fusion
  460.0 67.6 %scatter_units.1 = f32[128,2048]{1,0:T(8,128)} custom-call(bf16[16,128,2048]{2,1,0:T(8,128)(2,1)} %bitcast.248), custom_call_target="tpu_custom_call" | custom-call | tf_op jit(solution)/shard_map/scatter_units/pallas_call | solution.py:212
  540.4 12.2 %exchange_d_attended.1 = bf16[16,128,128]{2,1,0:T(8,128)(2,1)} custom-call(bf16[16,128,128]{2,1,0:T(8,128)(2,1)} %bitcast.289), custom_call_target="tpu_custom_call" | custom-call | tf_op jit(solution)/shard_map/exchange_d_attended/pallas_call | solution.py:212
  582.5 12.1 %spread_dots.1 = f32[16,32,128]{2,1,0:T(8,128)} custom-call(f32[32,128]{1,0:T(8,128)} %reshape.560.src), custom_call_target="tpu_custom_call" | custom-call | tf_op jit(solution)/shard_map/spread_dots/pallas_call | solution.py:212
  601.5 9.2 convolution_convert_fusion.7
  611.1 9.7 %fusion.12 = f32[1152,1024]{1,0:T(8,128)} fusion(bf16[1152,2048]{1,0:T(8,128)(2,1)} %bitcast.259, bf16[1,2048,1024]{2,1,0:T(8,128)(2,1)} %param.28), kind=kOutput, calls=%fused_computation.38 | convolution fusion | flops 4831838208 | bytes 13631488 | tf_op jit(solution)/shard_map/dot_general | solution.py:21
  620.9 6.8 fusion.17
  627.7 6.9 convolution_convert_fusion.1
  634.5 56.2 %scatter_normed.1 = f32[128,2048]{1,0:T(8,128)} custom-call(bf16[16,128,2048]{2,1,0:T(8,128)(2,1)} %bitcast.270), custom_call_target="tpu_custom_call" | custom-call | tf_op jit(solution)/shard_map/scatter_normed/pallas_call | solution.py:212
  698.3 40.7 %psum.7 = f32[4,2048]{1,0:T(4,128)S(1)} all-reduce(f32[4,2048]{1,0:T(4,128)S(1)} %pad_maximum_fusion.6), channel_id=1, replica_groups=mesh['grp'=2,'ep'=16] {'grp','ep'}, use_global_device_ids=true, to_apply=%region_39.40 | all-reduce | flops 8192 | bytes 65536 | tf_op jit(solution)/shard_map/psum | solution.py:782
  746.9 7.9 fusion.178
  754.8 7.9 fusion.177
  764.4 8.0 fusion.179
  772.4 7.0 fusion.7
  779.9 13.6 %add_bitcast_fusion = f32[1,1024,2048]{2,1,0:T(8,128)} fusion(f32[1024,2048]{1,0:T(8,128)} %fusion.179, bf16[1152,2048]{1,0:T(8,128)(2,1)S(1)} %fusion.3, f32[1152,1024]{1,0:T(8,128)} %fusion.12, f32[1152,1024]{1,0:T(8,128)} %fusion.17), kind=kOutput, calls=%fused_computation.17 | convolution fusion | flops 4841013248 | bytes 30932992 | tf_op jit(solution)/shard_map/dot_general | solution.py:29
  793.5 12.1 %add_bitcast_fusion.1 = f32[1,2048,1024]{2,1,0:T(8,128)} fusion(f32[2048,1024]{1,0:T(8,128)} %fusion.178, bf16[1152,2048]{1,0:T(8,128)(2,1)S(1)} %bitcast.265, f32[1152,1024]{1,0:T(8,128)S(1)} %copy-done.89, f32[1152,1024]{1,0:T(8,128)} %fusion.17), kind=kOutput, calls=%fused_computation.18 | convolution fusion | flops 4841013248 | bytes 30932992 | tf_op jit(solution)/shard_map/dot_general | solution.py:29
  805.6 14.1 %add_bitcast_fusion.2 = f32[1,2048,1024]{2,1,0:T(8,128)} fusion(f32[2048,1024]{1,0:T(8,128)} %fusion.177, bf16[1152,2048]{1,0:T(8,128)(2,1)S(1)} %bitcast.266, f32[1152,1024]{1,0:T(8,128)} %fusion.17, f32[1152,1024]{1,0:T(8,128)S(1)} %copy-done.89, f32[1152,1024]{1,0:T(8,128)} %fusion.12), kind=kOutput, calls=%fused_computation.19 | convolution fusion | flops 4845731840 | bytes 35651584 | tf_op jit(solution)/shard_map/dot_general | solution.py:29
  821.1 22.9 %exchange_grad_w.1 = bf16[16,64,384]{2,1,0:T(8,128)(2,1)} custom-call(bf16[16,64,384]{2,1,0:T(8,128)(2,1)} %bitcast.297), custom_call_target="tpu_custom_call" | custom-call | tf_op jit(solution)/shard_map/exchange_grad_w/pallas_call | solution.py:212
  851.7 68.7 %reduce-scatter.11.cloned.1.call-done = bf16[64,2048]{1,0:T(8,128)(2,1)} async-done(((bf16[2048,2048]{1,0:T(8,128)(2,1)}), bf16[64,2048]{1,0:T(8,128)(2,1)}) %reduce-scatter.11.cloned.1.call-update) | async-done | bytes 262160 | tf_op jit(solution)/shard_map/reduce_scatter | solution.py:740
  (402 shorter events, 175.7 us)
Async XLA Ops:
  7.2 209.9 %all-gather.3.cloned.1.call-start = ((), (), s32[]{:S(2)}) async-start(), calls=%async_computation.4 | async-start | bytes 8650752 | tf_op jit(solution)/shard_map/all_gather | solution.py:618
  7.9 392.8 %all-gather.5.cloned.1.call-start = ((), (), s32[]{:S(2)}) async-start(), calls=%async_computation.6 | async-start | bytes 17301504 | tf_op jit(solution)/shard_map/all_gather | solution.py:619
  8.7 521.6 %reduce-scatter.7.cloned.1.call-start = ((), (), s32[]{:S(2)}) async-start(), calls=%async_computation.5 | async-start | bytes 8912896 | tf_op jit(solution)/shard_map/reduce_scatter | solution.py:713
  135.8 15.8 %copy-start.39 = (bf16[2,16,1,64,128]{4,3,2,1,0:T(8,128)(2,1)}, bf16[2,16,1,64,128]{4,3,2,1,0:T(8,128)(2,1)S(1)}, u32[]{:S(2)}) copy-start(bf16[2,16,1,64,128]{4,3,2,1,0:T(8,128)(2,1)S(1)} %get-tuple-element.57) | copy-start | bytes 1572868
  135.8 37.1 %copy-start.51 = (bf16[2,16,1,64,128]{4,3,2,1,0:T(8,128)(2,1)}, bf16[2,16,1,64,128]{4,3,2,1,0:T(8,128)(2,1)S(1)}, u32[]{:S(2)}) copy-start(bf16[2,16,1,64,128]{4,3,2,1,0:T(8,128)(2,1)S(1)} %get-tuple-element.58) | copy-start | bytes 1572868
  151.6 17.8 %copy-start.10 = (f32[2048,128]{0,1:T(8,128)}, f32[2048,128]{0,1:T(8,128)S(1)}, u32[]{:S(2)}) copy-start(f32[2048,128]{0,1:T(8,128)S(1)} %get-tuple-element.93) | copy-start | bytes 3145732
  154.5 17.9 %copy-start.8 = (f32[2048,128]{0,1:T(8,128)}, f32[2048,128]{0,1:T(8,128)S(1)}, u32[]{:S(2)}) copy-start(f32[2048,128]{0,1:T(8,128)S(1)} %get-tuple-element.91) | copy-start | bytes 3145732
  172.3 10.6 %copy-start.31 = (bf16[2048,64]{0,1:T(8,128)(2,1)}, bf16[2048,64]{0,1:T(8,128)(2,1)S(1)}, u32[]{:S(2)}) copy-start(bf16[2048,64]{0,1:T(8,128)(2,1)S(1)} %get-tuple-element.82) | copy-start | bytes 786436
  172.3 10.6 %copy-start.33 = (bf16[2048,64]{0,1:T(8,128)(2,1)}, bf16[2048,64]{0,1:T(8,128)(2,1)S(1)}, u32[]{:S(2)}) copy-start(bf16[2048,64]{0,1:T(8,128)(2,1)S(1)} %get-tuple-element.83) | copy-start | bytes 786436
  172.5 10.5 %copy-start.28 = (bf16[1024,128]{0,1:T(8,128)(2,1)}, bf16[1024,128]{0,1:T(8,128)(2,1)S(1)}, u32[]{:S(2)}) copy-start(bf16[1024,128]{0,1:T(8,128)(2,1)S(1)} %get-tuple-element.72) | copy-start | bytes 786436
  186.6 30.5 %copy-start.12 = (bf16[128,2048]{1,0:T(8,128)(2,1)S(1)}, bf16[128,2048]{1,0:T(8,128)(2,1)}, u32[]{:S(2)}) copy-start(bf16[128,2048]{1,0:T(8,128)(2,1)} %x_ref.1) | copy-start | bytes 1572868
  380.6 439.0 %reduce-scatter.13.cloned.1.call-start = ((), (), s32[]{:S(2)}) async-start(), calls=%async_computation.9 | async-start | bytes 1081344
  382.0 10.5 %copy-start.20 = (bf16[128,2048]{1,0:T(8,128)(2,1)S(1)}, bf16[128,2048]{1,0:T(8,128)(2,1)}, u32[]{:S(2)}) copy-start(bf16[128,2048]{1,0:T(8,128)(2,1)} %multiply_convert_fusion.15.x_ref) | copy-start | bytes 1572868
  392.8 17.6 %slice-start.2 = ((s8[4718592]{0:T(1024)(128)(4,1)}), s8[524288]{0:T(1024)(128)(4,1)S(1)}, s32[]{:S(2)}) async-start(s8[4718592]{0:T(1024)(128)(4,1)} %bitcast.250), calls=%async_computation.12 | async-start | bytes 1048576
  400.7 10.0 %slice-start.3 = ((s8[4718592]{0:T(1024)(128)(4,1)}), s8[4194304]{0:T(1024)(128)(4,1)S(1)}, s32[]{:S(2)}) async-start(s8[4718592]{0:T(1024)(128)(4,1)} %bitcast.250), calls=%async_computation.13 | async-start | bytes 8388608
  460.0 70.3 %copy-start.45 = (bf16[128,2048]{1,0:T(8,128)(2,1)S(1)}, bf16[128,2048]{1,0:T(8,128)(2,1)}, u32[]{:S(2)}) copy-start(bf16[128,2048]{1,0:T(8,128)(2,1)} %param.16) | copy-start | bytes 1572868
  539.1 14.6 %copy-start.19 = (f32[8,128,128]{1,2,0:T(8,128)S(1)}, f32[8,128,128]{1,2,0:T(8,128)}, u32[]{:S(2)}) copy-start(f32[8,128,128]{1,2,0:T(8,128)} %copy-done.18) | copy-start | bytes 1572868
  539.1 14.6 %copy-start.58 = (pred[128,128]{0,1:T(8,128)(4,1)S(1)}, pred[128,128]{0,1:T(8,128)(4,1)}, u32[]{:S(2)}) copy-start(pred[128,128]{0,1:T(8,128)(4,1)} %copy-done.57) | copy-start | bytes 49156
  539.1 14.6 %copy-start.71 = (f32[8,128]{1,0:T(8,128)S(1)}, f32[8,128]{1,0:T(8,128)}, u32[]{:S(2)}) copy-start(f32[8,128]{1,0:T(8,128)} %get-tuple-element.44) | copy-start | bytes 12292
  539.1 16.0 %copy-start.48 = (bf16[2048,128]{1,0:T(8,128)(2,1)S(1)}, bf16[2048,128]{1,0:T(8,128)(2,1)}, u32[]{:S(2)}) copy-start(bf16[2048,128]{1,0:T(8,128)(2,1)} %copy-done.47) | copy-start | bytes 1572868
  539.1 16.0 %copy-start.70 = (f32[1024]{0:T(1024)S(1)}, f32[1024]{0:T(1024)}, u32[]{:S(2)}) copy-start(f32[1024]{0:T(1024)} %get-tuple-element.42) | copy-start | bytes 12292
  540.4 14.7 %copy-start.2 = (f32[1024,1024]{0,1:T(8,128)S(1)}, f32[1024,1024]{0,1:T(8,128)}, u32[]{:S(2)}) copy-start(f32[1024,1024]{0,1:T(8,128)} %copy-done.1) | copy-start | bytes 12582916
  601.4 219.6 %reduce-scatter.9.cloned.1.call-start = ((), (), s32[]{:S(2)}) async-start(), calls=%async_computation.7 | async-start | bytes 2359296 | tf_op jit(solution)/shard_map/reduce_scatter | solution.py:767
  601.5 19.2 %slice-start.6 = ((s8[4718592]{0:T(1024)(128)(4,1)}), s8[524288]{0:T(1024)(128)(4,1)S(1)}, s32[]{:S(2)}) async-start(s8[4718592]{0:T(1024)(128)(4,1)} %bitcast.260), calls=%async_computation.16 | async-start | bytes 1048576
  610.8 309.7 %reduce-scatter.11.cloned.1.call-start = ((), (), s32[]{:S(2)}) async-start(), calls=%async_computation.8 | async-start | bytes 8650752 | tf_op jit(solution)/shard_map/reduce_scatter | solution.py:740
  611.0 9.7 %slice-start.7 = ((s8[4718592]{0:T(1024)(128)(4,1)}), s8[4194304]{0:T(1024)(128)(4,1)S(1)}, s32[]{:S(2)}) async-start(s8[4718592]{0:T(1024)(128)(4,1)} %bitcast.260), calls=%async_computation.17 | async-start | bytes 8388608
  634.5 56.2 %copy-start.16 = (bf16[128,16,128]{0,2,1:T(8,128)(2,1)S(1)}, bf16[128,16,128]{0,2,1:T(8,128)(2,1)}, u32[]{:S(2)}) copy-start(bf16[128,16,128]{0,2,1:T(8,128)(2,1)} %copy-done.15) | copy-start | bytes 1572868
  697.7 47.8 %slice-start.4 = ((s8[4718592]{0:T(1024)(128)(4,1)}), s8[524288]{0:T(1024)(128)(4,1)S(1)}, s32[]{:S(2)}) async-start(s8[4718592]{0:T(1024)(128)(4,1)} %bitcast.255), calls=%async_computation.14 | async-start | bytes 1048576
  746.9 15.8 %slice-start = ((s8[4718592]{0:T(1024)(128)(4,1)}), s8[4194304]{0:T(1024)(128)(4,1)S(1)}, s32[]{:S(2)}) async-start(s8[4718592]{0:T(1024)(128)(4,1)} %bitcast.245), calls=%async_computation.10 | async-start | bytes 8388608
  779.3 14.1 %slice-start.8 = ((s8[4718592]{0:T(1024)(128)(4,1)}), s8[524288]{0:T(1024)(128)(4,1)S(1)}, s32[]{:S(2)}) async-start(s8[4718592]{0:T(1024)(128)(4,1)} %bitcast.263), calls=%async_computation.18 | async-start | bytes 1048576
  779.9 13.6 %slice-start.9 = ((s8[4718592]{0:T(1024)(128)(4,1)}), s8[4194304]{0:T(1024)(128)(4,1)S(1)}, s32[]{:S(2)}) async-start(s8[4718592]{0:T(1024)(128)(4,1)} %bitcast.263), calls=%async_computation.19 | async-start | bytes 8388608
  779.9 13.6 %copy-start.89 = (f32[1152,1024]{1,0:T(8,128)S(1)}, f32[1152,1024]{1,0:T(8,128)}, u32[]{:S(2)}) copy-start(f32[1152,1024]{1,0:T(8,128)} %fusion.7) | copy-start | bytes 14155780
  (79 other events, 366.7 us)
Sparse Core Ops, SparseCore 0:
  10.9 106.1 all-gather.2
  119.9 136.2 all-gather.4
  380.7 117.5 reduce-scatter.6
  601.6 139.2 reduce-scatter.12
  743.0 22.3 reduce-scatter.8
  767.5 152.8 reduce-scatter.10

commit v2 on v1

--- a/solution.py
+++ b/solution.py
@@ -153,8 +153,10 @@
                     index = here.index(here.at(offset), 1 - here.core)
                     self.side_copy(way, step + 1, part, self.block(index, part), index).wait_recv()
 
+    def settle(self):
+        self.own.wait()
+
     def finish(self):
-        self.own.wait()
         for copy in self.started:
             copy.wait_send()
 
@@ -195,6 +197,10 @@
     def finish(self):
         for copy in self.copies:
             copy.wait_send()
+
+
+def far_devices(here):
+    return [(1 - here.grp, (here.ep + offset) % here.count) for offset in range(here.count)]
 
 
 def ring_devices(here):
@@ -282,6 +288,7 @@
         remote(
             w_out.at[1 - here.grp], w_out.at[1 - here.grp], cross[1].at[1], cross[2].at[1], here.across()
         ).wait_recv()
+        gather.settle()
         gather.finish()
         columns_of.finish()
         over.wait_send()
@@ -349,6 +356,7 @@
             start(hand_copy(slot, index))
         for slot, offset in slots:
             hand_copy(slot, here.index(here.at(offset), 1 - here.core)).wait_recv()
+        gather.settle()
         gather.finish()
         for copy in sent:
             copy.wait_send()
@@ -486,6 +494,707 @@
         [blocks],
         vmem=True,
     )
+
+
+class Sums:
+    def __init__(self, here, buffers, sems):
+        self.here = here
+        self.mine, self.theirs, self.joint, self.first, self.landed = buffers
+        self.side_send, self.side_recv, self.ring_send, self.ring_recv = sems
+        self.far = here.ring // 2
+        self.offsets = ring_offsets(here.ring)
+        self.part_rows = self.mine.shape[1] // 2
+        self.waited, self.copies = set(), []
+
+    @staticmethod
+    def scratch(ep_count, rows, width, dtype=BF):
+        ring, far = ep_count // 2, ep_count // 4
+        dma = pltpu.SemaphoreType.DMA
+        buffers = [pltpu.VMEM((ring, rows, width), dtype) for _ in range(3)]
+        buffers += [pltpu.VMEM((2, rows, width), dtype), pltpu.VMEM((2, far, rows, width), dtype)]
+        return buffers, [dma((ring,)), dma((ring,)), dma((2, far, 2)), dma((2, far, 2))]
+
+    def side_copy(self, slot):
+        return remote(
+            self.theirs.at[slot],
+            self.joint.at[slot],
+            self.side_send.at[slot],
+            self.side_recv.at[slot],
+            self.here.sibling(),
+        )
+
+    def give(self, slot):
+        copy = self.side_copy(slot)
+        copy.start()
+        self.copies.append(copy)
+
+    def hops(self, way, part):
+        return self.far if way == part else self.far - 1
+
+    def rows(self, part):
+        return pl.ds(part * self.part_rows, self.part_rows)
+
+    def term(self, offset, part):
+        slot = self.offsets.index(self.far if offset == -self.far else offset)
+        if slot not in self.waited:
+            self.waited.add(slot)
+            self.side_copy(slot).wait_recv()
+        at = self.rows(part)
+        return self.mine[slot, at].astype(F32) + self.joint[slot, at].astype(F32)
+
+    def ring_copy(self, way, step, part):
+        at = self.rows(part)
+        src = self.first.at[way, at] if step == 0 else self.landed.at[way, step - 1, at]
+        return remote(
+            src,
+            self.landed.at[way, step, at],
+            self.ring_send.at[way, step, part],
+            self.ring_recv.at[way, step, part],
+            self.here.right() if way == 0 else self.here.left(),
+        )
+
+    def step(self, step):
+        for part in range(2):
+            for way in range(2):
+                count = self.hops(way, part)
+                if step < count:
+                    distance = count - step
+                    value = self.term(distance if way == 0 else -distance, part)
+                    at = self.rows(part)
+                    if step == 0:
+                        self.first[way, at] = value.astype(self.first.dtype)
+                    else:
+                        self.ring_copy(way, step - 1, part).wait_recv()
+                        value = value + self.landed[way, step - 1, at].astype(F32)
+                        self.landed[way, step - 1, at] = value.astype(self.landed.dtype)
+                    copy = self.ring_copy(way, step, part)
+                    copy.start()
+                    self.copies.append(copy)
+
+    def finish(self, put):
+        for part in range(2):
+            value = self.term(0, part)
+            at = self.rows(part)
+            for way in range(2):
+                count = self.hops(way, part)
+                self.ring_copy(way, count - 1, part).wait_recv()
+                value = value + self.landed[way, count - 1, at].astype(F32)
+            put(at, value)
+        for copy in self.copies:
+            copy.wait_send()
+
+
+def ring_offsets(ring):
+    far = ring // 2
+    return [0] + [sign * k for k in range(1, far) for sign in (1, -1)] + [far]
+
+
+def experts(ep_count, block, cots, hots, hots_t, router, gate_w, up_w, down_w, name, collective_id):
+    rows, width = block.shape
+    hidden_width = gate_w.shape[1]
+    slots = hots.shape[2]
+    pair = 2 * rows
+    ring = ep_count // 2
+    offsets = ring_offsets(ring)
+    batches = [[0]] + [[2 * k - 1, 2 * k] for k in range(1, ring // 2)] + [[ring - 1]]
+    tile, wide = 512, 1024
+    far = ring // 2
+
+    def kernel(*refs):
+        ins, outs, scratch = split(refs, 8, 10, len(refs) - 18)
+        block_ref, cot_ref, hot_ref, hot_t_ref, router_ref, gate_ref, up_ref, down_ref = ins
+        own_ref, other_ref, u_out, e_out, h_out, g_out, p_out, r_out, sum_out, dot_out = outs
+        gather_sems, cross, bufs, stage, sum_bufs, sum_sems, dot_sems, load_sems = split(scratch, 5, 4, 5, 9, 5, 4, 3, 4)
+        across_send, across_recv, hand_send, hand_recv = cross
+        gate_v, up_v, down_v, rows_v, cot_v = bufs
+        u_s, e_s, h_s, g_s, p_s, r_s, dx_s, dot_s, line_s = stage
+        dot_send, dot_recv, dot_own = dot_sems
+        weight_sem, rows_sem, cot_sem, stage_sem = load_sems
+        here = Place(ep_count)
+        sums = Sums(here, sum_bufs, sum_sems)
+        weights = []
+        for i, (src, dst) in enumerate(((gate_ref, gate_v), (up_ref, up_v), (down_ref, down_v))):
+            copy = pltpu.make_async_copy(src, dst, weight_sem.at[i])
+            copy.start()
+            weights.append(copy)
+        greet(plane_devices(here) + [here.across()])
+        gather = Gather(here, block_ref, own_ref, gather_sems)
+        gather.start()
+        sent = []
+
+        def start(copy):
+            copy.start()
+            sent.append(copy)
+
+        def cross_copy(slot, src):
+            index = here.chip(offsets[slot])
+            return remote(src, other_ref.at[index], across_send.at[slot], across_recv.at[slot], here.across())
+
+        def hand_copy(slot, core):
+            index = here.index(here.at(offsets[slot]), core)
+            return remote(
+                other_ref.at[index], other_ref.at[index], hand_send.at[slot], hand_recv.at[slot], here.sibling()
+            )
+
+        start(cross_copy(0, block_ref))
+
+        def chip_of(slot):
+            return here.index(here.at(offsets[slot]), 0) // 2
+
+        def group_of(which):
+            return here.grp if which == 0 else 1 - here.grp
+
+        def cot_copy(which, slot, buffer):
+            return pltpu.make_async_copy(
+                cot_ref.at[group_of(which), chip_of(slot)], cot_v.at[buffer], cot_sem.at[buffer]
+            )
+
+        def rows_copy(src, slot, buffer):
+            return pltpu.make_async_copy(
+                src.at[pl.ds(2 * chip_of(slot), 2)], rows_v.at[buffer], rows_sem.at[buffer]
+            )
+
+        pending = {}
+        stages = {"u": (u_s, u_out), "e": (e_s, e_out), "h": (h_s, h_out), "g": (g_s, g_out), "p": (p_s, p_out), "r": (r_s, r_out)}
+
+        def settle(keys):
+            for key in keys:
+                for copy in pending.pop(key, []):
+                    copy.wait()
+
+        def store(key, which, batch):
+            src, dst = stages[key]
+            sem = list(stages).index(key)
+            count = len(batch) * slots
+            if key == "r":
+                pending[key] = [
+                    pltpu.make_async_copy(src.at[pl.ds(i * slots, slots)], dst.at[chip_of(slot)], stage_sem.at[sem + i])
+                    for i, slot in enumerate(batch)
+                ]
+            else:
+                target = dst.at[which, pl.ds(batch[0] * slots, count)]
+                pending[key] = [pltpu.make_async_copy(src.at[pl.ds(0, count)], target, stage_sem.at[sem])]
+            for copy in pending[key]:
+                copy.start()
+
+        def loop(extent, tile, body):
+            def run(i, carry):
+                body(pl.ds(pl.multiple_of(i * tile, tile), tile))
+                return carry
+
+            lax.fori_loop(0, extent // tile, run, 0)
+
+        def prefetch(which, batch, parity):
+            for i, slot in enumerate(batch):
+                cot_copy(which, slot, 2 * parity + i).start()
+
+        def work(which, batch, parity):
+            count = len(batch) * slots
+            every = pl.ds(0, count)
+            src = own_ref if which == 0 else other_ref
+            for i, slot in enumerate(batch):
+                rows_copy(src, slot, i).start()
+            for i, slot in enumerate(batch):
+                rows_copy(src, slot, i).wait()
+                cot_copy(which, slot, 2 * parity + i).wait()
+            settle("u")
+            for i, slot in enumerate(batch):
+                hot = hot_ref[which, chip_of(slot)]
+
+                def pick_rows(at, i=i, hot=hot):
+                    picked = mm(hot, rows_v[i, :, :, at].reshape(pair, wide))
+                    u_s[pl.ds(i * slots, slots), at] = picked.astype(BF)
+
+                loop(width, wide, pick_rows)
+            store("u", which, batch)
+            logits = mm(u_s[every], router_ref[...])
+            lane = lax.broadcasted_iota(jnp.int32, logits.shape, 1)
+            logits = jnp.where(lane < ep_count, logits, -1e30)
+            powers = jnp.exp(logits - jnp.max(logits, axis=-1, keepdims=True))
+            gate = jnp.sum(jnp.where(lane == here.ep, powers, 0.0), axis=-1, keepdims=True)
+            gate = gate / jnp.sum(powers, axis=-1, keepdims=True)
+            settle("er")
+            for i, slot in enumerate(batch):
+                hot = hot_ref[which, chip_of(slot)]
+
+                def pick_cots(at, i=i, hot=hot):
+                    part = pl.ds(i * slots, slots)
+                    picked = mm(hot, cot_v[2 * parity + i, :, at])
+                    e_s[part, at] = (gate[i * slots : (i + 1) * slots] * picked).astype(BF)
+                    if which == 0:
+                        r_s[part, at] = picked.astype(BF)
+
+                loop(width, wide, pick_cots)
+            store("e", which, batch)
+            settle("hgp")
+
+            def inner(at):
+                gate_pre = mm(u_s[every], gate_v[:, at])
+                up_pre = mm(u_s[every], up_v[:, at])
+                grad = mm_nt(e_s[every], down_v[at, :])
+                sigma = 1.0 / (1.0 + jnp.exp(-gate_pre))
+                swish = gate_pre * sigma
+                h_s[every, at] = (swish * up_pre).astype(BF)
+                g_s[every, at] = (grad * up_pre * sigma * (1.0 + gate_pre * (1.0 - sigma))).astype(BF)
+                p_s[every, at] = (grad * swish).astype(BF)
+
+            loop(hidden_width, tile, inner)
+            for key in "hgp":
+                store(key, which, batch)
+            if which == 1:
+                return
+            dot_s[...] = jnp.zeros_like(dot_s)
+
+            def outer(at):
+                result = mm(h_s[every], down_v[:, at]).astype(BF).astype(F32)
+                dot_s[every] += jnp.sum(result * r_s[every, at].astype(F32), axis=-1, keepdims=True)
+                r_s[every, at] = (gate * result).astype(BF)
+
+            loop(width, wide, outer)
+            store("r", which, batch)
+
+            def back(at):
+                grad = mm_nt(g_s[every], gate_v[at, :]) + mm_nt(p_s[every], up_v[at, :])
+                dx_s[every, at] = grad.astype(BF)
+
+            loop(width, tile, back)
+            for i, slot in enumerate(batch):
+                part = pl.ds(i * slots, slots)
+                chip = chip_of(slot)
+
+                def put(at, slot=slot, part=part, chip=chip):
+                    grads = dx_s[part, at]
+                    for buffer, core in ((sums.mine, here.core), (sums.theirs, 1 - here.core)):
+                        turned = hot_t_ref[which, chip, pl.ds(pl.multiple_of(core * rows, rows), rows)]
+                        buffer[slot, :, at] = mm(turned, grads).astype(BF)
+
+                loop(width, wide, put)
+                sums.give(slot)
+                line = jnp.sum(hot_ref[which, chip].astype(F32) * dot_s[part], axis=0, keepdims=True)
+                for core in range(2):
+                    line_s[slot, core] = jnp.broadcast_to(line[:, core * rows : (core + 1) * rows], (8, rows))
+
+        prefetch(0, batches[0], 0)
+        for copy in weights:
+            copy.wait()
+        for number, batch in enumerate(batches):
+            if number == 0:
+                gather.settle()
+            else:
+                gather.step(number - 1)
+                for slot in batch:
+                    start(cross_copy(slot, own_ref.at[here.chip(offsets[slot])]))
+            gather.side(number - 1)
+            if number + 1 < len(batches):
+                prefetch(0, batches[number + 1], (number + 1) % 2)
+            else:
+                prefetch(1, batches[0], (number + 1) % 2)
+            work(0, batch, number % 2)
+
+        def dot_copy(slot, core, sender_core, source, target):
+            return remote(
+                line_s.at[slot, core], dot_out.at[source], dot_send.at[slot, core], dot_recv.at[slot, sender_core], (here.grp, target)
+            )
+
+        own_dots = pltpu.make_async_copy(line_s.at[0, here.core], dot_out.at[here.ep], dot_own)
+        own_dots.start()
+        start(dot_copy(0, 1 - here.core, here.core, here.ep, here.sibling()[1]))
+        for slot in range(1, ring):
+            for core in range(2):
+                target = here.index(here.at(offsets[slot]), core)
+                start(dot_copy(slot, core, here.core, here.ep, target))
+        count = len(batches)
+
+        def put_sum(at, value):
+            sum_out[at] = value
+
+        for number, batch in enumerate(batches):
+            for slot in batch:
+                index = here.chip(offsets[slot])
+                cross_copy(slot, other_ref.at[index]).wait_recv()
+                start(hand_copy(slot, here.core))
+            if number < far:
+                sums.step(number)
+            else:
+                sums.finish(put_sum)
+            for slot in batch:
+                hand_copy(slot, 1 - here.core).wait_recv()
+            parity = (count + number) % 2
+            if number + 1 < count:
+                prefetch(1, batches[number + 1], 1 - parity)
+            work(1, batch, parity)
+        own_dots.wait()
+        dot_copy(0, 0, 1 - here.core, here.sibling()[1], here.sibling()[1]).wait_recv()
+        for slot in range(1, ring):
+            for core in range(2):
+                source = here.index(here.at(-offsets[slot]), core)
+                dot_copy(slot, 0, core, source, source).wait_recv()
+        gather.finish()
+        for copy in sent:
+            copy.wait_send()
+        settle("uehgp")
+
+    dma = pltpu.SemaphoreType.DMA
+    total = ring * slots
+    most = max(len(batch) for batch in batches) * slots
+    sum_buffers, sum_sems = Sums.scratch(ep_count, rows, width)
+    hbm = pl.BlockSpec(memory_space=pl.ANY)
+    vmem = pl.BlockSpec(memory_space=pltpu.VMEM)
+
+    def low(*shape):
+        return jax.ShapeDtypeStruct(shape, BF)
+
+    def keep(*shape):
+        return pltpu.VMEM(shape, BF)
+
+    return pl.pallas_call(
+        kernel,
+        out_shape=[
+            low(ep_count, rows, width),
+            low(ep_count, rows, width),
+            low(2, total, width),
+            low(2, total, width),
+            low(2, total, hidden_width),
+            low(2, total, hidden_width),
+            low(2, total, hidden_width),
+            low(ring, slots, width),
+            jax.ShapeDtypeStruct((rows, width), F32),
+            jax.ShapeDtypeStruct((ep_count, 8, rows), F32),
+        ],
+        in_specs=[hbm, hbm, vmem, vmem, vmem, hbm, hbm, hbm],
+        out_specs=[hbm] * 8 + [vmem, hbm],
+        scratch_shapes=Gather.scratch(ep_count)
+        + [dma((ring,))] * 4
+        + [keep(*gate_w.shape), keep(*up_w.shape), keep(*down_w.shape), keep(2, 2, rows, width), keep(4, pair, width)]
+        + [keep(most, width), keep(most, width)]
+        + [keep(most, hidden_width)] * 3
+        + [keep(most, width), keep(most, width), pltpu.VMEM((most, 1), F32), pltpu.VMEM((ring, 2, 8, rows), F32)]
+        + sum_buffers
+        + sum_sems
+        + [dma((ring, 2)), dma((ring, 2)), dma]
+        + [dma((3,)), dma((2,)), dma((4,)), dma((7,))],
+        compiler_params=pltpu.CompilerParams(
+            collective_id=collective_id, has_side_effects=True, vmem_limit_bytes=60 << 20
+        ),
+        name=name,
+    )(block, cots, hots, hots_t, router, gate_w, up_w, down_w)
+
+
+class RingSum:
+    def __init__(self, here, term, buffers, sems, more=None):
+        self.here, self.term, self.more = here, term, more
+        self.joint, self.first, self.landed, self.stage = buffers
+        self.side_send, self.side_recv, self.ring_send, self.ring_recv, self.stage_sem = sems
+        self.far = here.ring // 2
+        self.offsets = ring_offsets(here.ring)
+        self.part_rows = self.stage.shape[2]
+        self.waited, self.copies = set(), []
+
+    @staticmethod
+    def scratch(ep_count, rows, width, dtype=BF):
+        ring, far = ep_count // 2, ep_count // 4
+        dma = pltpu.SemaphoreType.DMA
+        shapes = [(ring, rows, width), (2, rows, width), (2, far, rows, width), (2, 2, rows // 2, width)]
+        buffers = [pltpu.VMEM(shape, dtype) for shape in shapes]
+        return buffers + [dma((ring,)), dma((ring,)), dma((2, far, 2)), dma((2, far, 2)), dma((2, 2))]
+
+    def hops(self, way, part):
+        return self.far if way == part else self.far - 1
+
+    def rows(self, part):
+        return pl.ds(part * self.part_rows, self.part_rows)
+
+    def distance(self, way, part, step):
+        distance = max(self.hops(way, part) - step, 0)
+        return distance if way == 0 else -distance
+
+    def load(self, way, part, step):
+        index = self.here.chip(self.distance(way, part, step))
+        return pltpu.make_async_copy(
+            self.term(index).at[self.rows(part)], self.stage.at[way, part], self.stage_sem.at[way, part]
+        )
+
+    def side_copy(self, slot):
+        here = self.here
+        index = here.index(here.at(self.offsets[slot]), 1 - here.core)
+        return remote(
+            self.term(index), self.joint.at[slot], self.side_send.at[slot], self.side_recv.at[slot], here.sibling()
+        )
+
+    def start(self):
+        for way in range(2):
+            for part in range(2):
+                self.load(way, part, 0).start()
+        for slot in reversed(range(len(self.offsets))):
+            copy = self.side_copy(slot)
+            copy.start()
+            self.copies.append(copy)
+
+    def value(self, way, part, step):
+        offset = self.distance(way, part, step)
+        slot = self.offsets.index(self.far if offset == -self.far else offset)
+        if slot not in self.waited:
+            self.waited.add(slot)
+            self.side_copy(slot).wait_recv()
+        self.load(way, part, step).wait()
+        value = self.stage[way, part].astype(F32) + self.joint[slot, self.rows(part)].astype(F32)
+        if self.more is not None:
+            value = value + self.more(offset, self.rows(part))
+        return value
+
+    def ring_copy(self, way, step, part):
+        at = self.rows(part)
+        src = self.first.at[way, at] if step == 0 else self.landed.at[way, step - 1, at]
+        return remote(
+            src,
+            self.landed.at[way, step, at],
+            self.ring_send.at[way, step, part],
+            self.ring_recv.at[way, step, part],
+            self.here.right() if way == 0 else self.here.left(),
+        )
+
+    def step(self, step):
+        for part in range(2):
+            for way in range(2):
+                if step < self.hops(way, part):
+                    value = self.value(way, part, step)
+                    at = self.rows(part)
+                    if step == 0:
+                        self.first[way, at] = value.astype(self.first.dtype)
+                    else:
+                        self.ring_copy(way, step - 1, part).wait_recv()
+                        value = value + self.landed[way, step - 1, at].astype(F32)
+                        self.landed[way, step - 1, at] = value.astype(self.landed.dtype)
+                    copy = self.ring_copy(way, step, part)
+                    copy.start()
+                    self.copies.append(copy)
+                    if step + 1 < self.hops(way, part) or way == 0:
+                        self.load(way, part, step + 1).start()
+
+    def finish(self, put):
+        for part in range(2):
+            value = self.value(0, part, self.hops(0, part))
+            at = self.rows(part)
+            for way in range(2):
+                count = self.hops(way, part)
+                self.ring_copy(way, count - 1, part).wait_recv()
+                value = value + self.landed[way, count - 1, at].astype(F32)
+            put(at, value)
+        for copy in self.copies:
+            copy.wait_send()
+
+
+def sum_all(ep_count, normed_terms, result_terms, output_terms, weight_terms, tiles, expert_rows, name, collective_id):
+    rows, width = normed_terms.shape[1:]
+    units, grads, hidden, gate_grads, up_grads = expert_rows
+    depth_rows, hidden_width = hidden.shape
+    ring = ep_count // 2
+    far = ring // 2
+    out_rows = output_terms.shape[3]
+    weight_rows, weight_cols = weight_terms.shape[2:]
+    slab, wide = 256, 1024
+    dma = pltpu.SemaphoreType.DMA
+
+    def kernel(*refs):
+        ins, outs, scratch = split(refs, 10, 8, len(refs) - 18)
+        dn_ref, eo_ref, go_ref, gw_ref, tile_ref, u_ref, e_ref, h_ref, g_ref, p_ref = ins
+        dn_out, eo_out, go_out, gw_out, tile_out, gate_out, up_out, down_out = outs
+        dn_s, eo_s, go_s, go_more, gw_s, tile_s, work_s = split(scratch, 9, 9, 9, 6, 9, 3, 6)
+        here = Place(ep_count)
+        greet(plane_devices(here) + far_devices(here))
+        sent = []
+
+        def start(copy):
+            copy.start()
+            sent.append(copy)
+
+        tile_send, tile_recv, tile_own = tile_s
+        me = here.grp * ep_count + here.ep
+        own_tile = pltpu.make_async_copy(tile_ref.at[me], tile_out.at[me], tile_own)
+        own_tile.start()
+
+        def tile_copy(turn, offset, source):
+            group = (here.grp + turn) % 2
+            target = (here.ep + offset) % ep_count
+            slot = turn * ep_count + offset
+            return remote(
+                tile_ref.at[group * ep_count + target],
+                tile_out.at[source],
+                tile_send.at[slot],
+                tile_recv.at[slot],
+                (group, target),
+            )
+
+        (gw_x, gw_own, gw_sum, gw_x_send, gw_x_recv, gw_sem), gw_swap = gw_s[:6], gw_s[6:]
+        over = remote(gw_ref.at[1 - here.grp], gw_x, gw_x_send, gw_x_recv, here.across())
+        start(over)
+        gw_load = pltpu.make_async_copy(gw_ref.at[here.grp], gw_own, gw_sem)
+        gw_load.start()
+
+        x_own, x_joint, x_in, go_own_sem, go_send, go_recv = go_more
+        go_load = pltpu.make_async_copy(go_ref.at[1 - here.grp, :, here.core], x_own, go_own_sem)
+        go_load.start()
+        go_side = remote(go_ref.at[1 - here.grp, :, 1 - here.core], x_joint, go_send.at[0], go_recv.at[0], here.sibling())
+        start(go_side)
+        go_over = remote(x_own, x_in, go_send.at[1], go_recv.at[1], here.across())
+        normed = RingSum(here, lambda e: dn_ref.at[e], dn_s[:4], dn_s[4:])
+        normed.start()
+        result = RingSum(here, lambda e: eo_ref.at[e], eo_s[:4], eo_s[4:])
+        result.start()
+        arrived = []
+
+        def from_across(offset, at):
+            if not arrived:
+                arrived.append(True)
+                go_over.wait_recv()
+            chip = here.chip(offset) // 2
+            return x_in[chip, at].astype(F32)
+
+        output = RingSum(here, lambda e: go_ref.at[here.grp, e // 2, e % 2], go_s[:4], go_s[4:], from_across)
+        output.start()
+
+        left, right, sheet, left_sem, right_sem, sheet_sem = work_s
+        parts = [
+            (u_ref, g_ref, 0, gate_out, width),
+            (u_ref, p_ref, 0, up_out, width),
+            (h_ref, e_ref, 0, down_out, hidden_width),
+            (h_ref, e_ref, 1, down_out, hidden_width),
+        ]
+
+        def task(number, begin, end):
+            lhs, rhs, column, out, _ = parts[number]
+
+            def left_copy(i):
+                at = pl.ds(pl.multiple_of(i * slab, slab), slab)
+                return pltpu.make_async_copy(lhs.at[:, at], left.at[i % 2], left_sem.at[i % 2])
+
+            def sheet_copy(i):
+                at = pl.ds(pl.multiple_of(i * slab, slab), slab)
+                return pltpu.make_async_copy(
+                    sheet.at[i % 2], out.at[at, pl.ds(column * wide, wide)], sheet_sem.at[i % 2]
+                )
+
+            if begin == 0:
+                load = pltpu.make_async_copy(rhs.at[:, pl.ds(column * wide, wide)], right, right_sem)
+                load.start()
+            left_copy(begin).start()
+            if begin == 0:
+                load.wait()
+
+            def run(i, carry):
+                left_copy(i).wait()
+
+                @pl.when(i + 1 < end)
+                def _():
+                    left_copy(i + 1).start()
+
+                @pl.when(i >= begin + 2)
+                def _():
+                    sheet_copy(i - 2).wait()
+
+                sheet[i % 2] = mm_tn(left[i % 2], right[...]).astype(sheet.dtype)
+                sheet_copy(i).start()
+                return carry
+
+            lax.fori_loop(begin, end, run, 0)
+            for i in range(max(begin, end - 2), end):
+                sheet_copy(i).wait()
+
+        count, less = width // slab, hidden_width // slab
+        normed.step(0)
+        result.step(0)
+        for turn in range(2):
+            for offset in range(ep_count):
+                if turn + offset > 0:
+                    start(tile_copy(turn, offset, me))
+        go_load.wait()
+        go_side.wait_recv()
+        for chip in range(ring):
+            x_own[chip] = (x_own[chip].astype(F32) + x_joint[chip].astype(F32)).astype(BF)
+        start(go_over)
+        task(0, 0, count // 2)
+        gw_load.wait()
+        over.wait_recv()
+        for e in range(ep_count):
+            gw_sum[e] = (gw_own[e].astype(F32) + gw_x[e].astype(F32)).astype(BF)
+        swap = Exchange(here, lambda e: gw_sum.at[e], lambda e: gw_out.at[e], gw_swap)
+        swap.start()
+        normed.step(1)
+        result.step(1)
+        task(0, count // 2, count)
+        task(1, 0, count // 2)
+        normed.step(2)
+        result.step(2)
+        task(1, count // 2, count)
+        output.step(0)
+        normed.step(3)
+        result.step(3)
+        for step in range(4, far):
+            normed.step(step)
+            result.step(step)
+        task(2, 0, less)
+        output.step(1)
+        task(3, 0, less // 2)
+        output.step(2)
+        task(3, less // 2, less)
+        for step in range(3, far):
+            output.step(step)
+
+        def put(out):
+            def store(at, value):
+                out[at] = value
+
+            return store
+
+        normed.finish(put(dn_out))
+        result.finish(put(eo_out))
+        output.finish(put(go_out))
+        own_tile.wait()
+        for turn in range(2):
+            for offset in range(ep_count):
+                if turn + offset > 0:
+                    source = ((here.grp + turn) % 2) * ep_count + (here.ep + ep_count - offset) % ep_count
+                    tile_copy(turn, offset, source).wait_recv()
+        swap.arrive()
+        swap.finish()
+        for copy in sent:
+            copy.wait_send()
+
+    hbm = pl.BlockSpec(memory_space=pl.ANY)
+    vmem = pl.BlockSpec(memory_space=pltpu.VMEM)
+
+    def keep(*shape):
+        return pltpu.VMEM(shape, BF)
+
+    return pl.pallas_call(
+        kernel,
+        out_shape=[
+            jax.ShapeDtypeStruct((rows, width), F32),
+            jax.ShapeDtypeStruct((rows, width), F32),
+            jax.ShapeDtypeStruct((out_rows, width), F32),
+            jax.ShapeDtypeStruct((ep_count, weight_rows, weight_cols), BF),
+            jax.ShapeDtypeStruct(tiles.shape, tiles.dtype),
+            jax.ShapeDtypeStruct((width, hidden_width), BF),
+            jax.ShapeDtypeStruct((width, hidden_width), BF),
+            jax.ShapeDtypeStruct((hidden_width, width), BF),
+        ],
+        in_specs=[hbm] * 10,
+        out_specs=[vmem] * 3 + [hbm] * 5,
+        scratch_shapes=RingSum.scratch(ep_count, rows, width)
+        + RingSum.scratch(ep_count, rows, width)
+        + RingSum.scratch(ep_count, out_rows, width)
+        + [keep(ring, out_rows, width)] * 3
+        + [dma, dma((2,)), dma((2,))]
+        + [keep(ep_count, weight_rows, weight_cols)] * 3
+        + [dma, dma, dma]
+        + Exchange.scratch(ep_count)
+        + [dma((2 * ep_count,)), dma((2 * ep_count,)), dma]
+        + [keep(2, depth_rows, slab), keep(depth_rows, wide), keep(2, slab, wide), dma((2,)), dma, dma((2,))],
+        compiler_params=pltpu.CompilerParams(
+            collective_id=collective_id, has_side_effects=True, vmem_limit_bytes=60 << 20
+        ),
+        name=name,
+    )(normed_terms, result_terms, output_terms, weight_terms, tiles, units, grads, hidden, gate_grads, up_grads)
 
 
 def rms_scale(values, gain_vec):
@@ -652,79 +1361,23 @@
     r_m = lax.rsqrt(jnp.mean(residual * residual, axis=-1, keepdims=True) + eps)
     n_m = residual * r_m
     normed_mlp = (n_m * gain_second).astype(BF)
-    own_rows, other_rows = gather_both(ep_count, normed_mlp, "gather_normed", 4)
-
     pair = 2 * rows
     slots = -(-2 * capacity // 16) * 16
     chips = ep_count // 2
-
-    def picks(group):
-        mine = lax.dynamic_index_in_dim(chosen_all, group, 0, keepdims=False)[:, me]
-        mine = mine.reshape(chips, pair)
-        slot = jnp.cumsum(mine.astype(jnp.int32), axis=1) - 1
-        hot = (slot[:, None, :] == jnp.arange(slots, dtype=jnp.int32)[None, :, None]) & (mine[:, None, :] > 0)
-        return hot
-
-    def gate_of(normed_rows):
-        probs = jax.nn.softmax(mm(normed_rows, full_router), axis=-1)
-        return lax.dynamic_index_in_dim(probs, me, 1, keepdims=False)
-
-    def take(hot, values):
-        return jnp.einsum(
-            "csp,cpd->csd", hot, values.reshape(chips, pair, width), preferred_element_type=F32
-        ).astype(BF).reshape(-1, width)
-
-    def give(hot, values):
-        return jnp.einsum(
-            "csp,csd->cpd", hot, values.reshape(chips, slots, width), preferred_element_type=F32
-        ).reshape(tokens, width)
-
+    groups = jnp.stack([my_group, 1 - my_group])
+    mine = lax.dynamic_index_in_dim(chosen_all, me, 2, keepdims=False)[groups].reshape(2, chips, pair)
+    slot = jnp.cumsum(mine.astype(jnp.int32), axis=-1) - 1
+    places = jnp.arange(slots, dtype=jnp.int32)
+    hots = ((slot[:, :, None, :] == places[:, None]) & (mine[:, :, None, :] > 0)).astype(BF)
+    hots_t = ((slot[:, :, :, None] == places) & (mine[:, :, :, None] > 0)).astype(BF)
+    router = jnp.pad(full_router, ((0, 0), (0, per_row - ep_count)))
     gate_w, up_w, down_w = w_gate[0], w_up[0], w_down[0]
-    cot_both = cot_both.reshape(grp_count, tokens, width)
-
-    def expert(normed_rows, cot_rows, group):
-        hot = picks(group)
-        hot_low = hot.astype(BF)
-        gate = gate_of(normed_rows)
-        gate_rows = jnp.sum(jnp.where(hot, gate.reshape(chips, 1, pair), 0.0), axis=2).reshape(-1, 1)
-        units = take(hot_low, normed_rows)
-        cot_units = take(hot_low, cot_rows).astype(F32)
-        grad_out = (gate_rows * cot_units).astype(BF)
-        gate_pre = mm(units, gate_w)
-        up_pre = mm(units, up_w)
-        sigma = jax.nn.sigmoid(gate_pre)
-        hidden = (gate_pre * sigma * up_pre).astype(BF)
-        grad_hidden = mm_nt(grad_out, down_w)
-        grad_gate_pre = (grad_hidden * up_pre * sigma * (1.0 + gate_pre * (1.0 - sigma))).astype(BF)
-        grad_up_pre = (grad_hidden * gate_pre * sigma).astype(BF)
-        return hot, hot_low, gate, units, cot_units, grad_out, hidden, grad_gate_pre, grad_up_pre
-
-    own_rows = own_rows.reshape(tokens, width)
-    cot_own = lax.dynamic_index_in_dim(cot_both, my_group, 0, keepdims=False)
-    hot, hot_low, gate, units, cot_units, grad_out, hidden, grad_gate_pre, grad_up_pre = expert(
-        own_rows, cot_own, my_group
-    )
-    result = mm(hidden, down_w).astype(BF)
-    gate_grad_rows = jnp.sum(cot_units * result.astype(F32), axis=-1).reshape(chips, slots, 1)
-    gate_grad = jnp.sum(jnp.where(hot, gate_grad_rows, 0.0), axis=1).reshape(ep_count, 1, rows)
-    grad_units = (mm_nt(grad_gate_pre, gate_w) + mm_nt(grad_up_pre, up_w)).astype(BF)
-    partial_units = give(hot_low, grad_units).astype(BF).reshape(ep_count, rows, width)
-    partial_result = (gate[:, None] * give(hot_low, result)).astype(BF)
-    mixture = lax.psum_scatter(partial_result, "ep", scatter_dimension=0, tiled=True).astype(F32)
-    block_output = (residual + mixture).astype(BF)
-    d_normed_mlp = scatter_sum(ep_count, partial_units, "scatter_units", 5)
-    gate_grads = exchange(
-        ep_count, jnp.broadcast_to(gate_grad, (ep_count, 8, rows)), "exchange_gate_grads", 6
-    )[:, 0]
-
-    _, _, _, units_2, _, grad_out_2, hidden_2, grad_gate_pre_2, grad_up_pre_2 = expert(
-        other_rows.reshape(tokens, width),
-        lax.dynamic_index_in_dim(cot_both, 1 - my_group, 0, keepdims=False),
-        1 - my_group,
-    )
-    grad_gate = (mm_tn(units, grad_gate_pre) + mm_tn(units_2, grad_gate_pre_2))[None]
-    grad_up = (mm_tn(units, grad_up_pre) + mm_tn(units_2, grad_up_pre_2))[None]
-    grad_down = (mm_tn(hidden, grad_out) + mm_tn(hidden_2, grad_out_2))[None]
+    cots = cot_both.reshape(grp_count, chips, pair, width)
+    _, _, units, grad_out, hidden, grad_gate_pre, grad_up_pre, result, d_normed_mlp, gate_grads = experts(
+        ep_count, normed_mlp, cots, hots, hots_t, router, gate_w, up_w, down_w, "experts", 4
+    )
+    gate_grads = gate_grads[:, 0]
+    result_terms = jnp.einsum("cps,csd->cpd", hots_t[0], result, preferred_element_type=F32).astype(BF)
 
     probs = jax.nn.softmax(mm(normed_mlp, full_router), axis=-1)
     d_probs = gate_grads.T
@@ -737,7 +1390,6 @@
     d_proj = d_residual.astype(BF)
     d_attended = mm_nt(d_proj, full_output).astype(BF)
     local_output = mm_tn(att_loc, d_proj).astype(BF)
-    grad_output = lax.psum_scatter(local_output, ("grp", "ep"), scatter_dimension=0, tiled=True).astype(F32)
     d_attended = exchange(
         ep_count, d_attended.reshape(rows, ep_count, cols).transpose(1, 0, 2), "exchange_d_attended", 7
     ).reshape(tokens, cols)
@@ -756,31 +1408,46 @@
     d_lin = jnp.concatenate([d_q_lin, d_k_lin, d_v_lin], axis=1)
     w_all = jnp.concatenate([w_q, w_k, w_v], axis=1)
     partial_normed = mm_nt(d_lin, w_all).astype(BF).reshape(ep_count, rows, width)
-    d_normed = scatter_sum(ep_count, partial_normed, "scatter_normed", 9)
+    local_w = mm_tn(normed_all, d_lin)
+    local_gain_attn = jnp.sum(local_w * w_all.astype(F32), axis=-1) / gain_first
+    owners = grp_count * ep_count
+    heads_own = (jnp.arange(owners) * depth // cols == me)[:, None]
+    tiles = jnp.concatenate(
+        [
+            local_router.reshape(owners, router_rows, per_row),
+            jnp.concatenate([local_gain_attn.reshape(owners, depth), local_gain_mlp.reshape(owners, depth)], axis=1)[:, None],
+            jnp.concatenate(
+                [
+                    jnp.where(heads_own, jnp.tile(grad.reshape(-1, depth), (owners * depth // cols, 1)), 0.0)
+                    for grad in (gain_grad_q, gain_grad_k)
+                ],
+                axis=1,
+            )[:, None],
+            jnp.zeros((owners, 16 - router_rows - 2, per_row), F32),
+        ],
+        axis=1,
+    )
+    d_normed, mixture, grad_output, grad_w, tiles, grad_gate, grad_up, grad_down = sum_all(
+        ep_count,
+        partial_normed,
+        result_terms.reshape(ep_count, rows, width),
+        local_output.reshape(grp_count, chips, 2, depth, width),
+        local_w.astype(BF).reshape(grp_count, ep_count, depth, 3 * cols),
+        tiles,
+        [a.reshape(-1, a.shape[-1]) for a in (units, grad_out, hidden, grad_gate_pre, grad_up_pre)],
+        "sum_all",
+        9,
+    )
+    block_output = (residual + mixture).astype(BF)
     r_a = lax.rsqrt(jnp.mean(inputs * inputs, axis=-1, keepdims=True) + eps)
     n_a = inputs * r_a
-    local_gain_attn = jnp.sum(d_normed * n_a, axis=0)
     d_n = d_normed * gain_first
     input_grad = d_residual + r_a * (d_n - n_a * jnp.mean(n_a * d_n, axis=-1, keepdims=True))
-
-    grad_w = mm_tn(normed_all, d_lin).astype(BF)
-    grad_w = lax.psum_scatter(
-        grad_w.reshape(grp_count, ep_count * depth, 3 * cols), "grp", scatter_dimension=0, tiled=True
-    )
-    grad_w = exchange(ep_count, grad_w.reshape(ep_count, depth, 3 * cols), "exchange_grad_w", 10)
     grad_w = grad_w.reshape(ep_count, depth, 3, cols).transpose(2, 1, 0, 3).reshape(3, depth, width).astype(F32)
-    grad_router = lax.psum_scatter(local_router, ("grp", "ep"), scatter_dimension=0, tiled=True)
-    zeros = jnp.zeros((width,), F32)
-    gain_sums = jnp.stack(
-        [
-            local_gain_attn,
-            lax.dynamic_update_slice(zeros, gain_grad_q, (me * cols,)),
-            lax.dynamic_update_slice(zeros, gain_grad_k, (me * cols,)),
-            local_gain_mlp,
-        ]
-    )
-    gain_sums = lax.psum(gain_sums, ("grp", "ep"))
-    gain_sums = lax.dynamic_slice(gain_sums, (0, (my_group * ep_count + me) * depth), (4, depth))
+    sums = jnp.sum(tiles, axis=0)
+    grad_router = sums[:router_rows].reshape(depth, ep_count)
+    gain_sums = [sums[router_rows, :depth], sums[router_rows + 1, :depth], sums[router_rows + 1, depth:], sums[router_rows, depth:]]
+    grad_gate, grad_up, grad_down = (grad.astype(F32)[None] for grad in (grad_gate, grad_up, grad_down))
     return (
         block_output,
         input_grad,

time: 938 us -> 718 us (0.77)
  matrix products: 239 us -> 79 us
  waiting for transfers between devices: 70.2 us -> 12.1 us
  blocking collectives: 40.7 us -> 0 us
  Pallas kernels: 449 us -> 478 us
    pallas_call x0 -> x2, Pallas kernels: none -> 301 us  [the longest x1 161 us: experts(): pl.pallas_call(kernel, out_shape=[low(ep_count, rows, width), low(ep_coun...]
    pallas_call x10 -> x5, Pallas kernels: 449 us -> 177 us  [comm_call(): pl.pallas_call(kernel, out_shape=out_shape, in_specs=[spec] * len(operand...]
    reduce_scatter x3 -> x0, waiting for transfers between devices: 68.7 us -> none  [the longest x1 68.7 us: per_device(): lax.psum_scatter(local_output, ('grp', 'ep'), scatter_dimension=0, tiled=...]
    dot_general x12 -> x7, matrix products: 83.3 us -> 21.2 us  [mm_tn(): lax.dot_general(a, b, (((0,), (0,)), ((), ())), preferred_element_type=F32)]
    dot_general x16 -> x9, matrix products: 66.5 us -> 21.2 us  [mm(): return jnp.dot(a, b, preferred_element_type=F32)]
    psum x1 -> x0, blocking collectives: 40.7 us -> none  [per_device(): gain_sums = lax.psum(gain_sums, ('grp', 'ep'))]
    dot_general x11 -> x7, matrix products: 53.3 us -> 21 us  [mm_nt(): lax.dot_general(a, b, (((1,), (1,)), ((), ())), preferred_element_type=F32)]
    dot_general x6 -> x1, matrix products: 29.7 us -> 8.24 us  [per_device(): jnp.einsum('cps,csd->cpd', hots_t[0], result, preferred_element_type=F32)]
  transfers between devices with their start and end apart: 6 -> 2, of which waited for: 1 -> 1; matrix products, arithmetic and copies ran while one was open for 32% -> 11% of each run, Pallas kernels for 46% -> 21%
where the time goes in v2:
time: 718 us; the launch traced here: 706 us
  Pallas kernels  478 us (67%)
  other arithmetic  80.1 us (11%)
  matrix products  79 us (11%)
  local copies, waits for them, and re-layouts  41.1 us (6%)
  between operations  15.5 us (2%)
  waiting for transfers between devices  12.1 us (2%)
    pallas_call x5, Pallas kernels, comm_call(): pl.pallas_call(kernel, out_shape=out_shape, in_specs=[spec] * len(operand...  177 us
    pallas_call x1, Pallas kernels, experts(): pl.pallas_call(kernel, out_shape=[low(ep_count, rows, width), low(ep_coun...  161 us
    pallas_call x1, Pallas kernels, sum_all(): pl.pallas_call(kernel, out_shape=[jax.ShapeDtypeStruct((rows, width), F32...  140 us
    dot_general x7, matrix products, mm_tn(): lax.dot_general(a, b, (((0,), (0,)), ((), ())), preferred_element_type=F32)  21.2 us
    dot_general x9, matrix products, mm(): return jnp.dot(a, b, preferred_element_type=F32)  21.2 us
    dot_general x7, matrix products, mm_nt(): lax.dot_general(a, b, (((1,), (1,)), ((), ())), preferred_element_type=F32)  21 us
    convert_element_type x2, other arithmetic, per_device(): normed_all = rms_scale(x_wide, gain_first).astype(BF)  18.2 us
  transfers between devices with their start and end apart: 2, of which 1 were waited for; matrix products, arithmetic and copies ran while one was open for 11% of the time, Pallas kernels for 21%

profile of v2, /device:TPU:0, one launch (start us, length us, event | category | flops | bytes accessed | tf_op | source)
XLA Modules:
  0.0 706.1 jit_solution(2874094924446297890)
XLA Ops:
  11.8 2.1 pad_maximum_fusion.3.w_ref
  13.9 113.4 %gather_inputs.1 = (bf16[16,128,2048]{2,1,0:T(8,128)(2,1)}, bf16[2,16,3,64,128]{4,3,2,1,0:T(8,128)(2,1)}, bf16[2,16,32,128]{3,2,1,0:T(8,128)(2,1)}) custom-call(bf16[128,2048]{1,0:T(8,128)(2,1)} %x_ref.1, bf16[3,64,2048]{2,1,0:T(8,128)(2,1)} %pad_maximum_fusion.3.w_ref, bf16[32,128]{1,0:T(8,128)(2,1)} %pad_maximum_fusion.12.s_ref), custom_call_target="tpu_custom_call" | custom-call | tf_op jit(solution)/shard_map/gather_inputs/pallas_call | solution.py:218
  134.6 5.2 multiply_reduce_fusion
  140.0 9.3 %multiply_convert_fusion = bf16[16,128,2048]{2,1,0:T(8,128)(2,1)} fusion(f32[2048]{0:T(1024)S(1)} %reshape.620, f32[16,128]{1,0:T(8,128)S(1)} %get-tuple-element.143, bf16[16,128,2048]{2,1,0:T(8,128)(2,1)} %get-tuple-element.33), kind=kLoop, calls=%fused_computation.4 | loop fusion | flops 16777216 | bytes 16793600 | tf_op jit(solution)/shard_map/convert_element_type | solution.py:1343
  149.3 6.3 convolution_convert_fusion.4
  156.5 2.9 multiply_reduce_fusion.13
  159.5 2.9 multiply_reduce_fusion.12
  163.0 10.4 %spread_squares.1 = f32[16,32,128]{2,1,0:T(8,128)} custom-call(f32[32,128]{1,0:T(8,128)} %reshape.592.src), custom_call_target="tpu_custom_call" | custom-call | tf_op jit(solution)/shard_map/spread_squares/pallas_call | solution.py:218
  175.0 2.8 fusion.60
  186.7 27.7 %exchange_attended.1 = bf16[16,128,128]{2,1,0:T(8,128)(2,1)} custom-call(bf16[16,128,128]{2,1,0:T(8,128)(2,1)} %bitcast.212), custom_call_target="tpu_custom_call" | custom-call | tf_op jit(solution)/shard_map/exchange_attended/pallas_call | solution.py:218
  219.9 2.8 fusion.3
  222.7 8.9 %fusion.1 = bf16[2048,2048]{1,0:T(8,128)(2,1)} fusion(f32[2048]{0:T(1024)S(1)} %reshape.620, f32[2048]{0:T(1024)S(1)} %get-tuple-element.142, bf16[16,128,2048]{2,1,0:T(8,128)(2,1)} %get-tuple-element.33), kind=kLoop, calls=%fused_computation.3 | loop fusion | flops 16777216 | bytes 16793600 | tf_op jit(solution)/shard_map/convert_element_type | solution.py:1343
  231.6 5.2 multiply_reduce_fusion.11
  238.1 10.7 %all-gather.5.cloned.1.call-done = bf16[4096,2048]{1,0:T(8,128)(2,1)} async-done(((bf16[128,2048]{1,0:T(8,128)(2,1)}), bf16[4096,2048]{1,0:T(8,128)(2,1)}) %all-gather.5.cloned.1.call-update) | async-done | bytes 16777232 | tf_op jit(solution)/shard_map/all_gather | solution.py:1328
  248.8 161.2 %experts.1 = (bf16[16,128,2048]{2,1,0:T(8,128)(2,1)}, bf16[16,128,2048]{2,1,0:T(8,128)(2,1)}, bf16[2,1152,2048]{2,1,0:T(8,128)(2,1)}, bf16[2,1152,2048]{2,1,0:T(...) custom-call(bf16[128,2048]{1,0:T(8,128)(2,1)} %copy-done.11, ...), custom_call_target="tpu_custom_call" | custom-call | tf_op jit(solution)/shard_map/experts/pallas_call | solution.py:850
  415.1 7.1 %convolution_convert_fusion.3 = bf16[128,2048]{1,0:T(8,128)(2,1)} fusion(bf16[2048,2048]{1,0:T(8,128)(2,1)} %all-gather.3.cloned.1.call-done, f32[128,2048]{1,0:T(8,128)S(1)} %multiply_add_fusion), kind=kOutput, calls=%fused_computation.34 | convolution fusion | flops 1074266112 | bytes 9961472 | tf_op jit(solution)/shard_map/dot_general | solution.py:25
  426.2 13.3 %exchange_d_attended.1 = bf16[16,128,128]{2,1,0:T(8,128)(2,1)} custom-call(bf16[16,128,128]{2,1,0:T(8,128)(2,1)} %bitcast.215), custom_call_target="tpu_custom_call" | custom-call | tf_op jit(solution)/shard_map/exchange_d_attended/pallas_call | solution.py:218
  439.5 2.1 convolution_convert_fusion.5
  444.6 3.0 multiply_reduce_fusion.1
  456.7 5.7 convolution_convert_fusion.1
  466.7 4.0 fusion.25
  474.8 4.7 multiply_convert_fusion.1
  481.2 2.4 fusion.51
  490.2 12.2 %spread_dots.1 = f32[16,32,128]{2,1,0:T(8,128)} custom-call(f32[32,128]{1,0:T(8,128)} %reshape.606.src), custom_call_target="tpu_custom_call" | custom-call | tf_op jit(solution)/shard_map/spread_dots/pallas_call | solution.py:218
  507.9 6.8 convolution_convert_fusion
  514.8 6.2 multiply_reduce_fusion.4
  522.0 8.2 %convolution_convert_fusion.2 = bf16[8,256,2048]{2,1,0:T(8,128)(2,1)} fusion(bf16[8,144,2048]{2,1,0:T(8,128)(2,1)} %get-tuple-element.38, pred[2,8,256,144]{3,2,1,0:T(32,128)(4,1)S(1)} %copy-done.38), kind=kOutput, calls=%fused_computation.8 | convolution fusion | flops 1212153856 | bytes 13631488 | tf_op jit(solution)/shard_map/cps,csd->cpd/dot_general | solution.py:1380
  531.0 140.1 %sum_all.1 = (f32[128,2048]{1,0:T(8,128)}, f32[128,2048]{1,0:T(8,128)}, f32[64,2048]{1,0:T(8,128)}, bf16[16,64,384]{2,1,0:T(8,128)(2,1)}, f32[32,16,128]{2,1,0:T...) custom-call(bf16[16,128,2048]{2,1,0:T(8,128)(2,1)} %bitcast.188, ...), custom_call_target="tpu_custom_call" | custom-call | tf_op jit(solution)/shard_map/sum_all/pallas_call | solution.py:1169
  672.9 2.1 add_convert_fusion
  684.9 4.4 bitcast_convert_fusion.2
  689.4 4.4 bitcast_convert_fusion.1
  693.8 4.4 bitcast_convert_fusion
  (308 shorter events, 87.4 us)
Async XLA Ops:
  7.2 224.4 %all-gather.3.cloned.1.call-start = ((), (), s32[]{:S(2)}) async-start(), calls=%async_computation | async-start | bytes 8650752 | tf_op jit(solution)/shard_map/all_gather | solution.py:1327
  7.9 240.9 %all-gather.5.cloned.1.call-start = ((), (), s32[]{:S(2)}) async-start(), calls=%async_computation.1 | async-start | bytes 17301504 | tf_op jit(solution)/shard_map/all_gather | solution.py:1328
  133.1 41.4 %copy-start.68 = (f32[128]{0:T(128)}, f32[128]{0:T(128)S(1)}, u32[]{:S(2)}) copy-start(f32[128]{0:T(128)S(1)} %dynamic_slice.11) | copy-start | bytes 1540
  133.2 41.5 %copy-start.66 = (f32[128]{0:T(128)}, f32[128]{0:T(128)S(1)}, u32[]{:S(2)}) copy-start(f32[128]{0:T(128)S(1)} %dynamic_slice.10) | copy-start | bytes 1540
  133.6 6.2 copy-start.13
  134.6 5.3 copy-start.47
  139.9 9.4 %copy-start.53 = (bf16[2,16,1,64,128]{4,3,2,1,0:T(8,128)(2,1)}, bf16[2,16,1,64,128]{4,3,2,1,0:T(8,128)(2,1)S(1)}, u32[]{:S(2)}) copy-start(bf16[2,16,1,64,128]{4,3,2,1,0:T(8,128)(2,1)S(1)} %get-tuple-element.110) | copy-start | bytes 1572868
  140.0 16.6 %copy-start.41 = (bf16[2,16,1,64,128]{4,3,2,1,0:T(8,128)(2,1)}, bf16[2,16,1,64,128]{4,3,2,1,0:T(8,128)(2,1)S(1)}, u32[]{:S(2)}) copy-start(bf16[2,16,1,64,128]{4,3,2,1,0:T(8,128)(2,1)S(1)} %get-tuple-element.111) | copy-start | bytes 1572868
  140.0 19.5 %copy-start.39 = (bf16[2,16,1,64,128]{4,3,2,1,0:T(8,128)(2,1)}, bf16[2,16,1,64,128]{4,3,2,1,0:T(8,128)(2,1)S(1)}, u32[]{:S(2)}) copy-start(bf16[2,16,1,64,128]{4,3,2,1,0:T(8,128)(2,1)S(1)} %get-tuple-element.109) | copy-start | bytes 1572868
  149.3 7.2 %copy-start = (bf16[16,128,2048]{2,1,0:T(8,128)(2,1)S(1)}, bf16[16,128,2048]{2,1,0:T(8,128)(2,1)}, u32[]{:S(2)}) copy-start(bf16[16,128,2048]{2,1,0:T(8,128)(2,1)} %multiply_convert_fusion) | copy-start | bytes 25165828
  181.9 262.7 %copy-start.63 = (f32[1024]{0:T(1024)}, f32[1024]{0:T(1024)S(1)}, u32[]{:S(2)}) copy-start(f32[1024]{0:T(1024)S(1)} %get-tuple-element.100) | copy-start | bytes 12292
  185.0 32.6 %copy-start.8 = (bf16[128,2048]{1,0:T(8,128)(2,1)S(1)}, bf16[128,2048]{1,0:T(8,128)(2,1)}, u32[]{:S(2)}) copy-start(bf16[128,2048]{1,0:T(8,128)(2,1)} %x_ref.1) | copy-start | bytes 1572868
  185.0 33.3 %slice-start.2 = ((s32[2,8,3]{1,2,0:T(4,128)}), s32[2,8,2]{1,2,0:T(2,128)S(1)}, s32[]{:S(2)}) async-start(s32[2,8,3]{1,2,0:T(4,128)} %copy-done.65), calls=%async_computation.4 | async-start | bytes 4096 | tf_op jit(solution)/shard_map/slice.1
  231.6 6.1 copy-start.14
  248.8 162.1 %copy-start.15 = (bf16[2048,16]{1,0:T(8,128)(2,1)S(1)}, bf16[2048,16]{1,0:T(8,128)(2,1)}, u32[]{:S(2)}) copy-start(bf16[2048,16]{1,0:T(8,128)(2,1)} %copy-done.13) | copy-start | bytes 196612
  426.2 17.0 %copy-start.12 = (bf16[128,2048]{1,0:T(8,128)(2,1)S(1)}, bf16[128,2048]{1,0:T(8,128)(2,1)}, u32[]{:S(2)}) copy-start(bf16[128,2048]{1,0:T(8,128)(2,1)} %copy-done.11) | copy-start | bytes 1572868
  426.2 18.3 %copy-start.2 = (f32[1024,1024]{0,1:T(8,128)S(1)}, f32[1024,1024]{0,1:T(8,128)}, u32[]{:S(2)}) copy-start(f32[1024,1024]{0,1:T(8,128)} %copy-done.1) | copy-start | bytes 12582916
  444.6 5.9 copy-start.4
  484.4 23.4 %copy-start.55 = (bf16[1024,128]{0,1:T(8,128)(2,1)S(1)}, bf16[1024,128]{0,1:T(8,128)(2,1)}, u32[]{:S(2)}) copy-start(bf16[1024,128]{0,1:T(8,128)(2,1)} %fusion.25) | copy-start | bytes 786436
  506.2 8.5 %slice-start = ((s8[8388608]{0:T(1024)(128)(4,1)}), s8[4194304]{0:T(1024)(128)(4,1)S(1)}, s32[]{:S(2)}) async-start(s8[8388608]{0:T(1024)(128)(4,1)} %bitcast.189), calls=%async_computation.2 | async-start | bytes 8388608
  507.9 6.9 slice-start.1
  514.7 7.0 copy-start.74
  514.7 7.0 copy-start.73
  514.7 7.0 copy-start.76
  514.7 7.2 %copy-start.64 = (f32[32,64]{1,0:T(8,128)S(1)}, f32[32,64]{1,0:T(8,128)}, u32[]{:S(2)}) copy-start(f32[32,64]{1,0:T(8,128)} %reshape.613) | copy-start | bytes 24580
  514.8 7.2 %copy-start.38 = (pred[2,8,256,144]{3,2,1,0:T(32,128)(4,1)S(1)}, pred[2,8,256,144]{3,2,1,0:T(32,128)(4,1)}, u32[]{:S(2)}) copy-start(pred[2,8,256,144]{3,2,1,0:T(32,128)(4,1)} %get-tuple-element.128) | copy-start | bytes 1769476
  522.0 8.2 %copy-start.75 = (f32[16]{0:T(128)S(1)}, f32[16]{0:T(128)}, u32[]{:S(2)}) copy-start(f32[16]{0:T(128)} %pad.8.clone) | copy-start | bytes 196
  531.0 144.0 %copy-start.9 = (bf16[128,2048]{1,0:T(8,128)(2,1)S(1)}, bf16[128,2048]{1,0:T(8,128)(2,1)}, u32[]{:S(2)}) copy-start(bf16[128,2048]{1,0:T(8,128)(2,1)} %x_ref.1) | copy-start | bytes 1572868
  531.0 144.0 %copy-start.70 = (f32[128]{0:T(128)S(1)}, f32[128]{0:T(128)}, u32[]{:S(2)}) copy-start(f32[128]{0:T(128)} %add_rsqrt_fusion.1) | copy-start | bytes 1540
  671.2 5.4 copy-start.7
  671.2 7.5 %copy-start.51 = (bf16[16,64,384]{2,1,0:T(8,128)(2,1)S(1)}, bf16[16,64,384]{2,1,0:T(8,128)(2,1)}, u32[]{:S(2)}) copy-start(bf16[16,64,384]{2,1,0:T(8,128)(2,1)} %get-tuple-element.46) | copy-start | bytes 2359300
  679.5 5.4 copy-start.24
  (50 other events, 149.0 us)
Sparse Core Ops, SparseCore 0:
  10.9 106.1 all-gather.2
  119.9 128.7 all-gather.4

commit v3 on v2

v3 whole, which is shorter than its diff:
```python
import math

import jax
import jax.numpy as jnp
from jax import lax
from jax.experimental import pallas as pl
from jax.experimental.pallas import tpu as pltpu
from jax.sharding import PartitionSpec as P

HEAD_DIM = 128
MESH = pl.DeviceIdType.MESH
BF = jnp.bfloat16
F32 = jnp.float32


eps = 1e-05
theta_base = 10000.0


def mm(a, b):
    return jnp.dot(a, b, preferred_element_type=F32)


def mm_nt(a, b):
    return lax.dot_general(a, b, (((1,), (1,)), ((), ())), preferred_element_type=F32)


def mm_tn(a, b):
    return lax.dot_general(a, b, (((0,), (0,)), ((), ())), preferred_element_type=F32)


class Place:
    def __init__(self, ep_count):
        self.grp = lax.axis_index("grp")
        self.ep = lax.axis_index("ep")
        self.count = ep_count
        self.ring = ep_count // 2
        self.half = self.ring // 2
        self.core = self.ep % 2
        y = (self.ep // 2) % 2
        z = self.ep // 4
        self.place = z + y * (self.ring - 1 - 2 * z)

    def index(self, place, core):
        y = place // self.half
        z = place + y * (self.ring - 1 - 2 * place)
        return (z * 2 + y) * 2 + core

    def at(self, offset):
        return (self.place + offset + self.ring) % self.ring

    def chip(self, offset):
        return self.index(self.at(offset), self.core)

    def right(self):
        return (self.grp, self.chip(1))

    def left(self):
        return (self.grp, self.chip(-1))

    def sibling(self):
        return (self.grp, self.index(self.place, 1 - self.core))

    def across(self):
        return (1 - self.grp, self.ep)

    def peer(self, offset):
        return (self.grp, (self.ep + offset + self.count) % self.count)


def greet(devices):
    barrier = pltpu.get_barrier_semaphore()
    for device in devices:
        pl.semaphore_signal(barrier, inc=1, device_id=device, device_id_type=MESH)
    pl.semaphore_wait(barrier, len(devices))


def remote(src, dst, send, recv, device):
    return pltpu.make_async_remote_copy(
        src_ref=src, dst_ref=dst, send_sem=send, recv_sem=recv, device_id=device, device_id_type=MESH
    )


class Gather:
    def __init__(self, here, src, dst, sems):
        self.here, self.src, self.dst = here, src, dst
        self.ring_send, self.ring_recv, self.side_send, self.side_recv, self.own_sem = sems
        self.rows = dst.shape[1] // 2
        self.far = here.ring // 2
        self.started = []

    @staticmethod
    def scratch(ep_count):
        far = ep_count // 4
        ring = pltpu.SemaphoreType.DMA((2, far, 2))
        side = pltpu.SemaphoreType.DMA((2, far + 1, 2))
        return [ring, ring, side, side, pltpu.SemaphoreType.DMA]

    def block(self, index, part):
        return self.dst.at[index, pl.ds(part * self.rows, self.rows)]

    def go(self, copy):
        copy.start()
        self.started.append(copy)

    def hops(self, way, part):
        return self.far if way == part else self.far - 1

    def ring_copy(self, way, step, part, src, index):
        device = self.here.right() if way == 0 else self.here.left()
        return remote(
            src, self.block(index, part), self.ring_send.at[way, step, part], self.ring_recv.at[way, step, part], device
        )

    def side_copy(self, way, step, part, src, index):
        return remote(
            src,
            self.block(index, part),
            self.side_send.at[way, step, part],
            self.side_recv.at[way, step, part],
            self.here.sibling(),
        )

    def start(self):
        here = self.here
        for part in range(2):
            src = self.src.at[pl.ds(part * self.rows, self.rows)]
            for way in range(2):
                if self.hops(way, part) > 0:
                    self.go(self.ring_copy(way, 0, part, src, here.ep))
            self.go(self.side_copy(0, 0, part, src, here.ep))
        self.own = pltpu.make_async_copy(self.src, self.dst.at[here.ep], self.own_sem)
        self.own.start()

    def step(self, step):
        here = self.here
        for part in range(2):
            for way in range(2):
                if step < self.hops(way, part):
                    index = here.chip(-1 - step if way == 0 else 1 + step)
                    src = self.block(index, part)
                    self.ring_copy(way, step, part, src, index).wait_recv()
                    if step + 1 < self.hops(way, part):
                        self.go(self.ring_copy(way, step + 1, part, src, index))
                    self.go(self.side_copy(way, step + 1, part, src, index))

    def side(self, step):
        here = self.here
        for part in range(2):
            for way in range(2):
                if (step < 0 and way == 0) or (0 <= step < self.hops(way, part)):
                    offset = 0 if step < 0 else (-1 - step if way == 0 else 1 + step)
                    index = here.index(here.at(offset), 1 - here.core)
                    self.side_copy(way, step + 1, part, self.block(index, part), index).wait_recv()

    def settle(self):
        self.own.wait()

    def finish(self):
        for copy in self.started:
            copy.wait_send()


class Exchange:
    def __init__(self, here, src, dst, sems):
        self.here, self.src, self.dst = here, src, dst
        self.send, self.recv, self.own_sem = sems

    @staticmethod
    def scratch(ep_count):
        return [
            pltpu.SemaphoreType.DMA((ep_count,)),
            pltpu.SemaphoreType.DMA((ep_count,)),
            pltpu.SemaphoreType.DMA,
        ]

    def start(self):
        here = self.here
        self.own = pltpu.make_async_copy(self.src(here.ep), self.dst(here.ep), self.own_sem)
        self.own.start()
        self.copies = []
        for offset in range(1, here.count):
            device = here.peer(offset)
            copy = remote(self.src(device[1]), self.dst(here.ep), self.send.at[offset], self.recv.at[offset], device)
            copy.start()
            self.copies.append(copy)

    def arrive(self):
        here = self.here
        self.own.wait()
        for offset in range(1, here.count):
            source = here.peer(-offset)[1]
            remote(
                self.dst(source), self.dst(source), self.send.at[offset], self.recv.at[offset], here.peer(offset)
            ).wait_recv()

    def finish(self):
        for copy in self.copies:
            copy.wait_send()


def far_devices(here):
    return [(1 - here.grp, (here.ep + offset) % here.count) for offset in range(here.count)]


def plane_devices(here):
    return [here.peer(offset) for offset in range(1, here.count)]


def split(refs, *sizes):
    groups, start = [], 0
    for size in sizes:
        groups.append(refs[start : start + size])
        start += size
    return groups


def ring_offsets(ring):
    far = ring // 2
    return [0] + [sign * k for k in range(1, far) for sign in (1, -1)] + [far]


def experts(
    ep_count, block, cot_own, cot_other, early, hots, hots_t, router, gate_w, up_w, down_w, name, collective_id
):
    rows, width = block.shape
    hidden_width = gate_w.shape[1]
    slots = hots.shape[2]
    pair = 2 * rows
    ring = ep_count // 2
    offsets = ring_offsets(ring)
    batches = [[0]] + [[2 * k - 1, 2 * k] for k in range(1, ring // 2)] + [[ring - 1]]
    tile, wide = 512, 1024
    far = ring // 2

    def kernel(*refs):
        ins, outs, scratch = split(refs, 9, 13, len(refs) - 22)
        block_ref, cot_ref, cot_far, hot_ref, hot_t_ref, router_ref, gate_ref, up_ref, down_ref = ins
        own_ref, other_ref, u_out, e_out, h_out, g_out, p_out, du_terms, eo_terms, du_joint, sum_out, dot_out, cot_late = outs
        gather_sems, cross, cot_cross, bufs, stage, du_s, dot_sems, load_sems = split(scratch, 5, 4, 4, 5, 11, 8, 3, 5)
        across_send, across_recv, hand_send, hand_recv = cross
        gate_v, up_v, down_v, rows_v, cot_v = bufs
        u_s, e_s, h_s, g_s, p_s, r_s, dx_s, gate_s, dot_s, line_s, term_v = stage
        dot_send, dot_recv, dot_own = dot_sems
        weight_sem, rows_sem, cot_sem, stage_sem, term_sem = load_sems
        here = Place(ep_count)
        sums = RingSum(here, lambda e: du_terms.at[e], du_joint, du_s[:3], du_s[3:])
        weights = []
        for i, (src, dst) in enumerate(((gate_ref, gate_v), (up_ref, up_v), (down_ref, down_v))):
            copy = pltpu.make_async_copy(src, dst, weight_sem.at[i])
            copy.start()
            weights.append(copy)
        greet(plane_devices(here) + [here.across()])
        gather = Gather(here, block_ref, own_ref, gather_sems)
        gather.start()
        sent = []

        def start(copy):
            copy.start()
            sent.append(copy)

        def cross_copy(slot, src):
            index = here.chip(offsets[slot])
            return remote(src, other_ref.at[index], across_send.at[slot], across_recv.at[slot], here.across())

        def hand_copy(slot, core):
            index = here.index(here.at(offsets[slot]), core)
            return remote(
                other_ref.at[index], other_ref.at[index], hand_send.at[slot], hand_recv.at[slot], here.sibling()
            )

        start(cross_copy(0, block_ref))
        cot_over = Crossing(here, lambda e: cot_late.at[e], lambda e: cot_late.at[e], cot_cross)
        for slot in range(early, ring):
            cot_over.send(slot, cot_ref.at[here.chip(offsets[slot])])

        def chip_of(slot):
            return here.index(here.at(offsets[slot]), 0) // 2

        def cot_copy(which, slot, buffer):
            src = cot_ref if which == 0 else (cot_far if slot < early else cot_late)
            return pltpu.make_async_copy(src.at[pl.ds(2 * chip_of(slot), 2)], cot_v.at[buffer], cot_sem.at[buffer])

        def rows_copy(src, slot, buffer):
            return pltpu.make_async_copy(
                src.at[pl.ds(2 * chip_of(slot), 2)], rows_v.at[buffer], rows_sem.at[buffer]
            )

        pending = {}
        stages = {"u": (u_s, u_out), "e": (e_s, e_out), "g": (g_s, g_out), "p": (p_s, p_out)}

        def settle(keys):
            for key in keys:
                for copy in pending.pop(key, []):
                    copy.wait()

        def store(key, which, batch):
            src, dst = stages[key]
            sem = list(stages).index(key)
            count = len(batch) * slots
            at = pl.ds(batch[0] * slots, count)
            target = dst.at[which, at]
            pending[key] = [pltpu.make_async_copy(src.at[pl.ds(0, count)], target, stage_sem.at[sem])]
            for copy in pending[key]:
                copy.start()

        def loop(extent, tile, body):
            def run(i, carry):
                body(pl.ds(pl.multiple_of(i * tile, tile), tile))
                return carry

            lax.fori_loop(0, extent // tile, run, 0)

        def prefetch(which, batch, parity):
            for i, slot in enumerate(batch):
                cot_copy(which, slot, 2 * parity + i).start()

        hidden_copies = {}

        def store_hidden(which, batch):
            at = pl.ds(batch[0] * slots, len(batch) * slots)
            sem = weight_sem.at[3 + batches.index(batch)]
            hidden_copies[batch[0]] = pltpu.make_async_copy(h_s.at[at], h_out.at[which, at], sem)
            hidden_copies[batch[0]].start()

        given = []

        def give(src, first, chip, terms):
            buffer = len(given) % 2
            if len(given) > 1:
                given[-2].wait()

            def put(at):
                spread_rows = mm(hot_t_ref[0, chip], src[pl.ds(first, slots), at]).astype(BF)
                term_v[buffer, :, :, at] = spread_rows.reshape(2, rows, width)

            loop(width, width, put)
            copy = pltpu.make_async_copy(term_v.at[buffer], terms.at[pl.ds(2 * chip, 2)], term_sem.at[buffer])
            copy.start()
            given.append(copy)

        def settle_given():
            for copy in given[-2:]:
                copy.wait()
            given.clear()

        def work(which, batch, parity):
            count = len(batch) * slots
            every = pl.ds(0, count)
            src = own_ref if which == 0 else other_ref
            for i, slot in enumerate(batch):
                rows_copy(src, slot, i).start()
            for i, slot in enumerate(batch):
                rows_copy(src, slot, i).wait()
                cot_copy(which, slot, 2 * parity + i).wait()
            settle("u")
            for i, slot in enumerate(batch):
                hot = hot_ref[which, chip_of(slot)]

                def pick_rows(at, i=i, hot=hot):
                    picked = mm(hot, rows_v[i, :, :, at].reshape(pair, width))
                    u_s[pl.ds(i * slots, slots), at] = picked.astype(BF)

                loop(width, width, pick_rows)
            store("u", which, batch)
            logits = mm(u_s[every], router_ref[...])
            lane = lax.broadcasted_iota(jnp.int32, logits.shape, 1)
            logits = jnp.where(lane < ep_count, logits, -1e30)
            powers = jnp.exp(logits - jnp.max(logits, axis=-1, keepdims=True))
            gate = jnp.sum(jnp.where(lane == here.ep, powers, 0.0), axis=-1, keepdims=True)
            gate = gate / jnp.sum(powers, axis=-1, keepdims=True)
            settle("e")
            for i, slot in enumerate(batch):
                hot = hot_ref[which, chip_of(slot)]

                def pick_cots(at, i=i, hot=hot):
                    part = pl.ds(i * slots, slots)
                    picked = mm(hot, cot_v[2 * parity + i, :, :, at].reshape(pair, width))
                    e_s[part, at] = (gate[i * slots : (i + 1) * slots] * picked).astype(BF)
                    if which == 0:
                        r_s[pl.ds((batch[0] + i) * slots, slots), at] = picked.astype(BF)

                loop(width, width, pick_cots)
            store("e", which, batch)
            settle("gp")
            held = pl.ds(batch[0] * slots, count)
            if batch[0] in hidden_copies:
                hidden_copies.pop(batch[0]).wait()
            gate_s[held] = gate

            def inner(at):
                gate_pre = mm(u_s[every], gate_v[:, at])
                up_pre = mm(u_s[every], up_v[:, at])
                grad = mm_nt(e_s[every], down_v[at, :])
                sigma = 1.0 / (1.0 + jnp.exp(-gate_pre))
                swish = gate_pre * sigma
                h_s[held, at] = (swish * up_pre).astype(BF)
                g_s[every, at] = (grad * up_pre * sigma * (1.0 + gate_pre * (1.0 - sigma))).astype(BF)
                p_s[every, at] = (grad * swish).astype(BF)

            loop(hidden_width, tile, inner)
            for key in "gp":
                store(key, which, batch)
            store_hidden(which, batch)
            if which == 1:
                return None
            return lambda: work_back(batch, every)

        def work_back(batch, every):
            def back(at):
                grad = mm_nt(g_s[every], gate_v[at, :]) + mm_nt(p_s[every], up_v[at, :])
                dx_s[every, at] = grad.astype(BF)

            loop(width, wide, back)
            for i, slot in enumerate(batch):
                part = pl.ds(i * slots, slots)
                give(dx_s, i * slots, chip_of(slot), du_terms)

        def results():
            dot_s[...] = jnp.zeros_like(dot_s)

            def outer(at):
                result = mm(h_s[...], down_v[:, at]).astype(BF).astype(F32)
                dot_s[...] += jnp.sum(result * r_s[:, at].astype(F32), axis=-1, keepdims=True)
                r_s[:, at] = (gate_s[...] * result).astype(BF)

            loop(width, tile, outer)
            for slot in range(ring):
                part = pl.ds(slot * slots, slots)
                line = jnp.sum(hot_ref[0, chip_of(slot)].astype(F32) * dot_s[part], axis=0, keepdims=True)
                for core in range(2):
                    line_s[slot, core] = jnp.broadcast_to(line[:, core * rows : (core + 1) * rows], (8, rows))

        prefetch(0, batches[0], 0)
        for copy in weights:
            copy.wait()
        gather.settle()
        for number, batch in enumerate(batches):
            gather.side(number - 1)
            if number + 1 < len(batches):
                prefetch(0, batches[number + 1], (number + 1) % 2)
            else:
                prefetch(1, batches[0], (number + 1) % 2)
            rest = work(0, batch, number % 2)
            if number < far:
                gather.step(number)
                for slot in batches[number + 1]:
                    start(cross_copy(slot, own_ref.at[here.chip(offsets[slot])]))
            rest()
        def dot_copy(slot, core, sender_core, source, target):
            return remote(
                line_s.at[slot, core],
                dot_out.at[source],
                dot_send.at[slot, core],
                dot_recv.at[slot, sender_core],
                (here.grp, target),
            )

        settle_given()
        sums.start()
        sums.step(0)
        results()
        own_dots = pltpu.make_async_copy(line_s.at[0, here.core], dot_out.at[here.ep], dot_own)
        own_dots.start()

        start(dot_copy(0, 1 - here.core, here.core, here.ep, here.sibling()[1]))
        for slot in range(1, ring):
            for core in range(2):
                target = here.index(here.at(offsets[slot]), core)
                start(dot_copy(slot, core, here.core, here.ep, target))
        count = len(batches)

        def put(out):
            def keep_sum(at, value):
                out[at] = value

            return keep_sum

        for number, batch in enumerate(batches):
            for slot in batch:
                index = here.chip(offsets[slot])
                cross_copy(slot, other_ref.at[index]).wait_recv()
                start(hand_copy(slot, here.core))
            if 0 < number < far:
                sums.step(number)
            if number == 1:
                for slot in range(ring):
                    give(r_s, slot * slots, chip_of(slot), eo_terms)
                settle_given()
            if number == far:
                sums.finish(put(sum_out))
            for slot in batch:
                hand_copy(slot, 1 - here.core).wait_recv()
            parity = (count + number) % 2
            if number + 1 < count:
                late = [slot for slot in batches[number + 1] if slot >= early]
                for slot in late:
                    cot_over.take(slot)
                for slot in late:
                    cot_over.settle(slot)
                prefetch(1, batches[number + 1], 1 - parity)
            work(1, batch, parity)
        own_dots.wait()
        dot_copy(0, 0, 1 - here.core, here.sibling()[1], here.sibling()[1]).wait_recv()
        for slot in range(1, ring):
            for core in range(2):
                source = here.index(here.at(-offsets[slot]), core)
                dot_copy(slot, 0, core, source, source).wait_recv()
        gather.finish()
        cot_over.finish()
        for copy in sent:
            copy.wait_send()
        settle("uegp")
        for copy in hidden_copies.values():
            copy.wait()

    dma = pltpu.SemaphoreType.DMA
    total = ring * slots
    most = max(len(batch) for batch in batches) * slots
    hbm = pl.BlockSpec(memory_space=pl.ANY)
    vmem = pl.BlockSpec(memory_space=pltpu.VMEM)

    def low(*shape):
        return jax.ShapeDtypeStruct(shape, BF)

    def keep(*shape):
        return pltpu.VMEM(shape, BF)

    return pl.pallas_call(
        kernel,
        out_shape=[
            low(ep_count, rows, width),
            low(ep_count, rows, width),
            low(2, total, width),
            low(2, total, width),
            low(2, total, hidden_width),
            low(2, total, hidden_width),
            low(2, total, hidden_width),
            low(ep_count, rows, width),
            low(ep_count, rows, width),
            low(ring, rows, width),
            jax.ShapeDtypeStruct((rows, width), F32),
            jax.ShapeDtypeStruct((ep_count, 8, rows), F32),
            low(ep_count, rows, width),
        ],
        in_specs=[hbm, hbm, hbm, vmem, vmem, vmem, hbm, hbm, hbm],
        out_specs=[hbm] * 10 + [vmem, hbm, hbm],
        scratch_shapes=Gather.scratch(ep_count)
        + [dma((ring,))] * 4
        + Crossing.scratch(ep_count)
        + [keep(*gate_w.shape), keep(*up_w.shape), keep(*down_w.shape), keep(2, 2, rows, width), keep(4, 2, rows, width)]
        + [keep(most, width), keep(most, width), keep(total, hidden_width)]
        + [keep(most, hidden_width)] * 2
        + [keep(total, width), keep(most, width)]
        + [pltpu.VMEM((total, 1), F32), pltpu.VMEM((total, 1), F32), pltpu.VMEM((ring, 2, 8, rows), F32)]
        + [keep(2, 2, rows, width)]
        + RingSum.scratch(ep_count, rows, width)
        + [dma((ring, 2)), dma((ring, 2)), dma]
        + [dma((3 + len(batches),)), dma((2,)), dma((4,)), dma((4,)), dma((2,))],
        compiler_params=pltpu.CompilerParams(
            collective_id=collective_id, has_side_effects=True, vmem_limit_bytes=62 << 20
        ),
        name=name,
    )(block, cot_own, cot_other, hots, hots_t, router, gate_w, up_w, down_w)


class RingSum:
    def __init__(self, here, term, joint, buffers, sems, more=None):
        self.here, self.term, self.joint, self.more = here, term, joint, more
        self.first, self.landed, self.stage = buffers
        self.side_send, self.side_recv, self.ring_send, self.ring_recv, self.stage_sem = sems
        self.far = here.ring // 2
        self.offsets = ring_offsets(here.ring)
        self.part_rows = self.stage.shape[3]
        self.waited, self.copies = set(), []

    @staticmethod
    def scratch(ep_count, rows, width, dtype=BF):
        ring, far = ep_count // 2, ep_count // 4
        dma = pltpu.SemaphoreType.DMA
        shapes = [(2, rows, width), (2, far, rows, width), (2, 2, 2, rows // 2, width)]
        buffers = [pltpu.VMEM(shape, dtype) for shape in shapes]
        return buffers + [dma((ring,)), dma((ring,)), dma((2, far, 2)), dma((2, far, 2)), dma((2, 2, 2))]

    def hops(self, way, part):
        return self.far if way == part else self.far - 1

    def rows(self, part):
        return pl.ds(part * self.part_rows, self.part_rows)

    def distance(self, way, part, step):
        distance = max(self.hops(way, part) - step, 0)
        return distance if way == 0 else -distance

    def slot(self, way, part, step):
        offset = self.distance(way, part, step)
        return self.offsets.index(self.far if offset == -self.far else offset)

    def loads(self, way, part, step):
        index = self.here.chip(self.distance(way, part, step))
        sources = (self.term(index), self.joint.at[self.slot(way, part, step)])
        return [
            pltpu.make_async_copy(
                source.at[self.rows(part)], self.stage.at[way, part, i], self.stage_sem.at[way, part, i]
            )
            for i, source in enumerate(sources)
        ]

    def load(self, way, part, step):
        slot = self.slot(way, part, step)
        if slot not in self.waited:
            self.waited.add(slot)
            self.side_copy(slot).wait_recv()
        for copy in self.loads(way, part, step):
            copy.start()

    def side_copy(self, slot):
        here = self.here
        index = here.index(here.at(self.offsets[slot]), 1 - here.core)
        return remote(
            self.term(index), self.joint.at[slot], self.side_send.at[slot], self.side_recv.at[slot], here.sibling()
        )

    def start(self):
        for slot in reversed(range(len(self.offsets))):
            copy = self.side_copy(slot)
            copy.start()
            self.copies.append(copy)
        for part in range(2):
            for way in range(2):
                self.load(way, part, 0)

    def value(self, way, part, step):
        for copy in self.loads(way, part, step):
            copy.wait()
        value = self.stage[way, part, 0].astype(F32) + self.stage[way, part, 1].astype(F32)
        if self.more is not None:
            value = value + self.more(self.distance(way, part, step), self.rows(part))
        return value

    def ring_copy(self, way, step, part):
        at = self.rows(part)
        src = self.first.at[way, at] if step == 0 else self.landed.at[way, step - 1, at]
        return remote(
            src,
            self.landed.at[way, step, at],
            self.ring_send.at[way, step, part],
            self.ring_recv.at[way, step, part],
            self.here.right() if way == 0 else self.here.left(),
        )

    def step(self, step):
        for part in range(2):
            for way in range(2):
                if step < self.hops(way, part):
                    value = self.value(way, part, step)
                    at = self.rows(part)
                    if step == 0:
                        self.first[way, at] = value.astype(self.first.dtype)
                    else:
                        self.ring_copy(way, step - 1, part).wait_recv()
                        value = value + self.landed[way, step - 1, at].astype(F32)
                        self.landed[way, step - 1, at] = value.astype(self.landed.dtype)
                    copy = self.ring_copy(way, step, part)
                    copy.start()
                    self.copies.append(copy)
                    if step + 1 < self.hops(way, part) or way == 0:
                        self.load(way, part, step + 1)

    def finish(self, put):
        for part in range(2):
            value = self.value(0, part, self.hops(0, part))
            at = self.rows(part)
            for way in range(2):
                count = self.hops(way, part)
                self.ring_copy(way, count - 1, part).wait_recv()
                value = value + self.landed[way, count - 1, at].astype(F32)
            put(at, value)
        for copy in self.copies:
            copy.wait_send()


def rolled(values):
    return pltpu.roll(values, HEAD_DIM // 2, 1)


def as_rows(columns, count):
    shape = (columns[0].shape[0], 128)
    lane = lax.broadcasted_iota(jnp.int32, shape, 1)
    packed = jnp.zeros(shape, F32)
    for i, column in enumerate(columns):
        packed = jnp.where(lane == i, column, packed)
    return packed.T[:count]


def as_columns(tile):
    padded = jnp.concatenate([tile, jnp.zeros((128 - tile.shape[0], tile.shape[1]), F32)], axis=0)
    return padded.T


def backward(
    ep_count, d_att, head, columns, tables, gains, w_all, normed, output_terms, result_terms, tiles, expert_rows, name, collective_id
):
    rows = d_att.shape[1]
    query, key, value, norm_q, norm_k = head
    tokens, cols = query.shape
    width = w_all.shape[0]
    prompt_len = tokens // 2
    units, grads, hidden, gate_grads, up_grads = expert_rows
    depth_rows, hidden_width = hidden.shape
    ring = ep_count // 2
    far = ring // 2
    out_rows = output_terms.shape[3]
    slab, wide, block = 256, 512, 256
    segment = 512
    pieces = tokens // segment
    scale = HEAD_DIM ** (-0.5)
    dma = pltpu.SemaphoreType.DMA

    def kernel(*refs):
        ins, outs, scratch = split(refs, 20, 13, len(refs) - 33)
        (att_ref, q_ref, k_ref, v_ref, nq_ref, nk_ref, col_ref, cos_ref, sin_ref, gain_ref, w_ref, normed_ref) = ins[:12]
        go_ref, eo_ref, tile_ref, u_ref, e_ref, h_ref, g_ref, p_ref = ins[12:]
        dn_out, go_out, eo_out, gw_out, tile_out, late_out, gate_out, up_out, down_out = outs[:9]
        dn_terms, dn_joint, go_joint, eo_joint = outs[9:]
        dn_s, go_s, eo_s, go_more, gw_s, tile_s, late_s, work_s, att_s, dots_s, own_s = split(
            scratch, 8, 8, 8, 6, 7, 3, 4, 6, 8, 5, 5
        )
        here = Place(ep_count)
        greet(plane_devices(here) + far_devices(here))
        sent = []

        def start(copy):
            copy.start()
            sent.append(copy)

        (att_v, dq_s, dk_s, dv_s, lin_s), att_sems = att_s[:5], att_s[5:]
        attended = Exchange(here, lambda e: att_ref.at[e], lambda e: att_v.at[e], att_sems)
        attended.start()

        me = here.grp * ep_count + here.ep

        def tile_copy(turn, offset, source, src, dst, sems):
            group = (here.grp + turn) % 2
            target = (here.ep + offset) % ep_count
            slot = turn * ep_count + offset
            return remote(src(group * ep_count + target), dst.at[source], sems[0].at[slot], sems[1].at[slot], (group, target))

        others = [(turn, offset) for turn in range(2) for offset in range(ep_count) if turn + offset > 0]

        def send_tiles(src, dst, sems):
            own = pltpu.make_async_copy(src(me), dst.at[me], sems[2])
            own.start()
            for turn, offset in others:
                start(tile_copy(turn, offset, me, src, dst, sems))
            return own

        def take_tiles(own, src, dst, sems):
            own.wait()
            for turn, offset in others:
                source = ((here.grp + turn) % 2) * ep_count + (here.ep + ep_count - offset) % ep_count
                tile_copy(turn, offset, source, src, dst, sems).wait_recv()

        x_own, x_joint, x_in, go_own_sem, go_send, go_recv = go_more
        go_load = pltpu.make_async_copy(go_ref.at[1 - here.grp, :, here.core], x_own, go_own_sem)
        go_load.start()
        go_side = remote(go_ref.at[1 - here.grp, :, 1 - here.core], x_joint, go_send.at[0], go_recv.at[0], here.sibling())
        start(go_side)

        def go_over(part):
            at = pl.ds(part * (ring // 2), ring // 2)
            return remote(x_own.at[at], x_in.at[at], go_send.at[1 + part], go_recv.at[1 + part], here.across())

        arrived = []

        def from_across(offset, at):
            if not arrived:
                arrived.append(True)
                for half in range(2):
                    go_over(half).wait_recv()
            return x_in[here.chip(offset) // 2, at].astype(F32)

        output = RingSum(
            here, lambda e: go_ref.at[here.grp, e // 2, e % 2], go_joint, go_s[:3], go_s[3:], from_across
        )
        result = RingSum(here, lambda e: eo_ref.at[e], eo_joint, eo_s[:3], eo_s[3:])

        left, right, sheet, left_sem, right_sem, sheet_sem = work_s
        parts = [(u_ref, g_ref, i, gate_out, width) for i in range(hidden_width // wide)]
        parts += [(u_ref, p_ref, i, up_out, width) for i in range(hidden_width // wide)]
        parts += [(h_ref, e_ref, i, down_out, hidden_width) for i in range(width // wide)]

        def task(lhs, rhs, column, out, end):
            def left_copy(i):
                at = pl.ds(pl.multiple_of(i * slab, slab), slab)
                return pltpu.make_async_copy(lhs.at[:, at], left.at[lax.rem(i, 2)], left_sem.at[lax.rem(i, 2)])

            def sheet_copy(i):
                at = pl.ds(pl.multiple_of(i * slab, slab), slab)
                return pltpu.make_async_copy(
                    sheet.at[lax.rem(i, 2)], out.at[at, pl.ds(column * wide, wide)], sheet_sem.at[lax.rem(i, 2)]
                )

            load = pltpu.make_async_copy(rhs.at[:, pl.ds(column * wide, wide)], right, right_sem)
            load.start()
            left_copy(jnp.int32(0)).start()
            load.wait()

            def run(i, carry):
                left_copy(i).wait()

                @pl.when(i + 1 < end)
                def _():
                    left_copy(i + 1).start()

                @pl.when(i >= 2)
                def _():
                    sheet_copy(i - 2).wait()

                sheet[lax.rem(i, 2)] = mm_tn(left[lax.rem(i, 2)], right[...]).astype(sheet.dtype)
                sheet_copy(i).start()
                return carry

            lax.fori_loop(0, end, run, 0)
            for i in range(max(0, end - 2), end):
                sheet_copy(jnp.int32(i)).wait()

        def tasks(count):
            for _ in range(min(count, len(parts))):
                lhs, rhs, column, out, extent = parts.pop(0)
                task(lhs, rhs, column, out, extent // slab)

        result.start()
        result.step(0)
        own_tiles = send_tiles(lambda i: tile_ref.at[i], tile_out, tile_s)
        go_load.wait()
        go_side.wait_recv()
        for chip in range(ring):
            x_own[chip] = (x_own[chip].astype(F32) + x_joint[chip].astype(F32)).astype(BF)
        start(go_over(0))
        tasks(1)
        attended.arrive()

        dk_s[...] = jnp.zeros_like(dk_s)
        dv_s[...] = jnp.zeros_like(dv_s)
        per = block // rows
        line = lax.broadcasted_iota(jnp.int32, (block, block), 0)
        column_at = lax.broadcasted_iota(jnp.int32, (block, block), 1)
        causal = line >= column_at
        same = causal & (line // rows == column_at // rows)

        def grads_of(first, spans):
            at = pl.ds(first, block)
            q = q_ref[at]
            g = att_v[pl.ds(first // rows, per)].reshape(block, cols)
            log = col_ref[at, 0:1]
            kept = []
            inner = jnp.zeros((block, 1), F32)
            for begin, length, mask in spans:
                keys = pl.ds(begin, length)
                weight = jnp.exp(mm_nt(q, k_ref[keys]) * scale - log)
                if mask is not None:
                    weight = jnp.where(mask, weight, 0.0)
                d_weight = mm_nt(g, v_ref[keys])
                inner = inner + jnp.sum(weight * d_weight, axis=-1, keepdims=True)
                kept.append((keys, weight, d_weight))
            dq = jnp.zeros((block, cols), F32)
            for keys, weight, d_weight in kept:
                d_score = (weight * (d_weight - inner)).astype(BF)
                dq = dq + mm(d_score, k_ref[keys])
                dk_s[keys] += mm_tn(d_score, q)
                dv_s[keys] += mm_tn(weight.astype(BF), g)
            dq_s[at] = dq * scale

        for number in range(prompt_len // block):
            spans = [(0, number * block, None)] if number else []
            grads_of(number * block, spans + [(number * block, block, causal)])

        def later(number, carry):
            first = pl.multiple_of(prompt_len + number * block, block)
            grads_of(first, [(0, prompt_len, None), (first, block, same)])
            return carry

        lax.fori_loop(0, (tokens - prompt_len) // block, later, 0)
        result.step(1)

        dots_v, dots_all, dots_sems = dots_s[0], dots_s[1], dots_s[2:]
        late_v, late_sems = late_s[0], late_s[1:]
        gain_sums = [jnp.zeros((1, cols), F32), jnp.zeros((1, cols), F32)]
        stats = []
        for piece in range(pieces):
            at = pl.ds(piece * segment, segment)
            for kind, (ref, n_ref, factor) in enumerate(((dq_s, nq_ref, 1.0), (dk_s, nk_ref, scale))):
                turned = ref[at] * factor
                turned = turned * cos_ref[at] - rolled(turned) * sin_ref[at]
                gain_sums[kind] = gain_sums[kind] + jnp.sum(turned * n_ref[at], axis=0, keepdims=True)
                turned = turned * gain_ref[kind : kind + 1]
                ref[at] = turned
                stats.append(jnp.sum(turned * n_ref[at], axis=-1, keepdims=True))
        dots_v[...] = as_rows(stats, dots_v.shape[0])
        spread_dots = Exchange(here, lambda e: dots_v, lambda e: dots_all.at[e], dots_sems)
        spread_dots.start()
        gain_tile = jnp.concatenate(gain_sums + [jnp.zeros((6, cols), F32)], axis=0)
        for piece in range(pieces):
            at = pl.ds(piece * segment, segment)
            lin_s[at, 2 * cols : 3 * cols] = dv_s[at].astype(BF)
        slab_v, slab_sem, term_v, term_sem, gw_v = own_s
        slabs = width // slab
        half = slabs // 2

        def slab_at(turn):
            return lax.rem((1 - here.grp) * half + turn, slabs) * slab

        def slab_copy(turn):
            at = pl.ds(pl.multiple_of(slab_at(turn), slab), slab)
            return pltpu.make_async_copy(normed_ref.at[:, at], slab_v.at[turn % 2], slab_sem.at[turn % 2])

        slab_copy(0).start()
        slab_copy(1).start()
        spread_dots.arrive()
        total = dots_all[0]
        for e in range(1, ep_count):
            total = total + dots_all[e]
        total = as_columns(total / width)
        for piece in range(pieces):
            at = pl.ds(piece * segment, segment)
            for kind, (ref, n_ref) in enumerate(((dq_s, nq_ref), (dk_s, nk_ref))):
                lane = 2 * piece + kind
                grad = col_ref[at, 1 + kind : 2 + kind] * (ref[at] - n_ref[at] * total[:, lane : lane + 1])
                lin_s[at, kind * cols : (kind + 1) * cols] = grad.astype(BF)

        (gw_x, gw_sum, gw_x_send, gw_x_recv), gw_swap = gw_s[:4], gw_s[4:]
        per_slab = slab // out_rows
        gain_lines = []

        def projections(turn):
            slab_copy(turn).wait()
            first = slab_at(turn)
            grad = mm_tn(slab_v[turn % 2], lin_s[...])
            if turn + 2 < slabs:
                slab_copy(turn + 2).start()
            weight = w_ref[pl.ds(pl.multiple_of(first, slab), slab)].astype(F32)
            line = as_rows([jnp.sum(grad * weight, axis=-1, keepdims=True)], 8)[0:1]
            owner = first // out_rows
            gw_v[pl.ds(owner, per_slab)] = grad.astype(BF).reshape(per_slab, out_rows, 3 * cols)
            for i in range(per_slab):
                part = line[:, i * out_rows : (i + 1) * out_rows]
                part = jnp.concatenate([part, jnp.zeros((1, cols - out_rows), F32)], axis=1)
                late_v[owner + i] = jnp.concatenate([gain_tile[0:2], part, gain_tile[3:]], axis=0)
            return owner

        def over_copy(turn, owner):
            at = pl.ds(owner - (1 - here.grp) * ep_count, per_slab)
            return remote(gw_v.at[pl.ds(owner, per_slab)], gw_x.at[at], gw_x_send.at[turn], gw_x_recv.at[turn], here.across())

        for turn in range(half):
            start(over_copy(turn, projections(turn)))
        start(go_over(1))
        output.start()

        normed_sum = RingSum(here, lambda e: dn_terms.at[e], dn_joint, dn_s[:3], dn_s[3:])
        offsets = ring_offsets(ring)
        stores = {}
        for turn, slot in enumerate(reversed(range(ring))):
            chip = here.index(here.at(offsets[slot]), 0) // 2
            if turn >= 2:
                stores.pop(turn - 2).wait()
            at = pl.ds(pl.multiple_of(chip * 2 * rows, 2 * rows), 2 * rows)

            def fill(i, carry, at=at, turn=turn):
                wide_at = pl.ds(pl.multiple_of(i * 1024, 1024), 1024)
                part = mm_nt(lin_s[at], w_ref[wide_at]).astype(BF)
                term_v[turn % 2, :, :, wide_at] = part.reshape(2, rows, 1024)
                return carry

            lax.fori_loop(0, width // 1024, fill, 0)
            stores[turn] = pltpu.make_async_copy(
                term_v.at[turn % 2], dn_terms.at[pl.ds(chip * 2, 2)], term_sem.at[turn % 2]
            )
            stores[turn].start()
        for turn in sorted(stores):
            stores[turn].wait()
        normed_sum.start()
        normed_sum.step(0)
        result.step(2)
        for turn in range(half, slabs):
            projections(turn)
        own_late = send_tiles(lambda i: late_v.at[i], late_out, late_sems)
        tasks(1)
        for turn in range(half):
            over_copy(turn, (1 - here.grp) * ep_count + turn * per_slab).wait_recv()
        for e in range(ep_count):
            gw_sum[e] = (gw_v[here.grp * ep_count + e].astype(F32) + gw_x[e].astype(F32)).astype(BF)
        swap = Exchange(here, lambda e: gw_sum.at[e], lambda e: gw_out.at[e], gw_swap)
        swap.start()
        normed_sum.step(1)
        for step in range(3, far):
            result.step(step)
        tasks(2)
        normed_sum.step(2)
        tasks(2)
        for step in range(3, far):
            normed_sum.step(step)
        output.step(0)
        tasks(1)
        output.step(1)
        tasks(1)
        output.step(2)
        for step in range(3, far):
            output.step(step)

        def put(out):
            def store(at, value):
                out[at] = value

            return store

        normed_sum.finish(put(dn_out))
        tasks(len(parts))
        result.finish(put(eo_out))
        output.finish(put(go_out))
        take_tiles(own_tiles, lambda i: tile_ref.at[i], tile_out, tile_s)
        take_tiles(own_late, lambda i: late_v.at[i], late_out, late_sems)
        attended.finish()
        spread_dots.finish()
        swap.arrive()
        swap.finish()
        for copy in sent:
            copy.wait_send()

    hbm = pl.BlockSpec(memory_space=pl.ANY)
    vmem = pl.BlockSpec(memory_space=pltpu.VMEM)
    group_rows = 2 * ep_count

    def keep(*shape):
        return pltpu.VMEM(shape, BF)

    def wide_keep(*shape):
        return pltpu.VMEM(shape, F32)

    return pl.pallas_call(
        kernel,
        out_shape=[
            jax.ShapeDtypeStruct((rows, width), F32),
            jax.ShapeDtypeStruct((out_rows, width), F32),
            jax.ShapeDtypeStruct((rows, width), F32),
            jax.ShapeDtypeStruct((ep_count, out_rows, 3 * cols), BF),
            jax.ShapeDtypeStruct(tiles.shape, F32),
            jax.ShapeDtypeStruct((group_rows, 8, cols), F32),
            jax.ShapeDtypeStruct((width, hidden_width), BF),
            jax.ShapeDtypeStruct((width, hidden_width), BF),
            jax.ShapeDtypeStruct((hidden_width, width), BF),
            jax.ShapeDtypeStruct((ep_count, rows, width), BF),
            jax.ShapeDtypeStruct((ring, rows, width), BF),
            jax.ShapeDtypeStruct((ring, out_rows, width), BF),
            jax.ShapeDtypeStruct((ring, rows, width), BF),
        ],
        in_specs=[hbm] + [vmem] * 10 + [hbm] * 9,
        out_specs=[vmem] * 3 + [hbm] * 10,
        scratch_shapes=RingSum.scratch(ep_count, rows, width)
        + RingSum.scratch(ep_count, out_rows, width)
        + RingSum.scratch(ep_count, rows, width)
        + [keep(ring, out_rows, width)] * 3
        + [dma, dma((3,)), dma((3,))]
        + [keep(ep_count, out_rows, 3 * cols)] * 2
        + [dma((ring,)), dma((ring,))]
        + Exchange.scratch(ep_count)
        + [dma((group_rows,)), dma((group_rows,)), dma]
        + [wide_keep(group_rows, 8, cols), dma((group_rows,)), dma((group_rows,)), dma]
        + [keep(2, depth_rows, slab), keep(depth_rows, wide), keep(2, slab, wide), dma((2,)), dma, dma((2,))]
        + [keep(ep_count, rows, cols)]
        + [wide_keep(tokens, cols)] * 3
        + [keep(tokens, 3 * cols)]
        + Exchange.scratch(ep_count)
        + [wide_keep(8, segment), wide_keep(ep_count, 8, segment)]
        + Exchange.scratch(ep_count)
        + [keep(2, tokens, slab), dma((2,)), keep(2, 2, rows, width), dma((2,))]
        + [keep(group_rows, out_rows, 3 * cols)],
        compiler_params=pltpu.CompilerParams(
            collective_id=collective_id, has_side_effects=True, vmem_limit_bytes=62 << 20
        ),
        name=name,
    )(d_att, query, key, value, norm_q, norm_k, columns, *tables, gains, w_all, normed, output_terms, result_terms, tiles, *expert_rows)


class Crossing:
    def __init__(self, here, out, into, sems):
        self.here, self.out, self.into = here, out, into
        self.across_send, self.across_recv, self.hand_send, self.hand_recv = sems
        self.offsets = ring_offsets(here.ring)
        self.copies = []

    @staticmethod
    def scratch(ep_count):
        return [pltpu.SemaphoreType.DMA((ep_count // 2,))] * 4

    def go(self, copy):
        copy.start()
        self.copies.append(copy)

    def across(self, slot, src, dst):
        return remote(src, dst, self.across_send.at[slot], self.across_recv.at[slot], self.here.across())

    def hand(self, slot, core):
        block = self.into(self.here.index(self.here.at(self.offsets[slot]), core))
        return remote(block, block, self.hand_send.at[slot], self.hand_recv.at[slot], self.here.sibling())

    def send(self, slot, src):
        self.go(self.across(slot, src, self.out(self.here.chip(self.offsets[slot]))))

    def take(self, slot):
        block = self.into(self.here.chip(self.offsets[slot]))
        self.across(slot, block, block).wait_recv()
        self.go(self.hand(slot, self.here.core))

    def settle(self, slot):
        self.hand(slot, 1 - self.here.core).wait_recv()

    def finish(self):
        for copy in self.copies:
            copy.wait_send()


def attention(ep_count, x, weights, small, w_out, cot, tables, early, name, collective_id):
    rows, width = x.shape
    kinds, depth, _ = weights.shape
    cols = width // ep_count
    tokens = rows * ep_count
    prompt_len = tokens // 2
    ring = ep_count // 2
    far = ring // 2
    offsets = ring_offsets(ring)
    batches = [[0]] + [[2 * k - 1, 2 * k] for k in range(1, far)] + [[ring - 1]]
    gain_row = depth * ep_count // 128
    block, segment, chunk = 256, 512, 64
    pieces = tokens // segment
    scale = HEAD_DIM ** (-0.5)
    dma = pltpu.SemaphoreType.DMA

    def kernel(*refs):
        ins, outs, scratch = split(refs, 7, 14, len(refs) - 21)
        x_ref, weights_ref, small_ref, w_ref, cot_ref, cos_ref, sin_ref = ins
        normed_out, w_all, s_out, full_out, cot_out, cot_other = outs[:6]
        q_out, k_out, v_out, nq_out, nk_out, col_out, att_out, x_land = outs[6:]
        x_s, w_s, s_s, cross, w_ring, cot_ring, w_cross, cot_cross, bufs, loads, dots_s, att_s = split(
            scratch, 5, 3, 2, 3, 5, 5, 4, 4, 5, 2, 5, 4
        )
        rows_v, normed_v, columns_v, gain_v, lin_v = bufs
        rows_sem, normed_sem = loads
        here = Place(ep_count)
        greet(plane_devices(here) + [here.across()])

        cross_own, cross_send, cross_recv = cross
        first = pltpu.make_async_copy(small_ref, s_out.at[here.grp, here.ep], cross_own)
        first.start()

        def small_over(group):
            return remote(
                small_ref, s_out.at[group, here.ep], cross_send.at[0], cross_recv.at[0], here.across()
            )

        small_over(here.grp).start()
        gather = Gather(here, x_ref, x_land, x_s)
        gather.start()
        columns_of = Exchange(
            here,
            lambda e: weights_ref.at[:, :, pl.ds(pl.multiple_of(e * cols, cols), cols)],
            lambda e: columns_v.at[here.grp, e],
            w_s,
        )
        columns_of.start()
        full = Gather(here, w_ref, full_out.at[here.grp], w_ring)
        full_over = Crossing(
            here, lambda e: full_out.at[here.grp, e], lambda e: full_out.at[1 - here.grp, e], w_cross
        )
        cots = Gather(here, cot_ref, cot_out, cot_ring)
        cots_over = Crossing(here, lambda e: cot_other.at[e], lambda e: cot_other.at[e], cot_cross)
        full_over.send(0, w_ref)
        cots_over.send(0, cot_ref)

        first.wait()
        small_over(1 - here.grp).wait_recv()
        small_over(here.grp).wait_send()
        small_copies = []
        for offset in range(1, here.count):
            mine = s_out.at[:, here.ep]
            copy = remote(mine, mine, s_s[0].at[offset], s_s[1].at[offset], here.peer(offset))
            copy.start()
            small_copies.append(copy)
        for offset in range(1, here.count):
            source = s_out.at[:, here.peer(-offset)[1]]
            remote(source, source, s_s[0].at[offset], s_s[1].at[offset], here.peer(offset)).wait_recv()

        def gains(row, half, owner):
            lines = []
            for i in range(2):
                tile = s_out[(owner + i) // ep_count, (owner + i) % ep_count, pl.ds(0, 16)].astype(F32)
                lines.append(tile[row : row + 1, half * depth : (half + 1) * depth])
            return jnp.concatenate(lines, axis=1)

        for i in range(width // 128):
            gain_v[:, i * 128 : (i + 1) * 128] = gains(gain_row, 0, 2 * i)
        gain_q, gain_k = gains(gain_row, 1, 2 * here.ep), gains(gain_row + 1, 0, 2 * here.ep)

        def chip_of(slot):
            return here.index(here.at(offsets[slot]), 0) // 2

        stores = []

        def norm(batch):
            loaded = []
            for i, slot in enumerate(batch):
                loaded.append(pltpu.make_async_copy(x_land.at[pl.ds(2 * chip_of(slot), 2)], rows_v.at[i], rows_sem.at[i]))
                loaded[-1].start()
            for i, slot in enumerate(batch):
                loaded[i].wait()
                chip = chip_of(slot)
                for core in range(2):

                    def run(j, carry, i=i, core=core, chip=chip):
                        at = pl.ds(pl.multiple_of(j * chunk, chunk), chunk)
                        wide = rows_v[i, core, at].astype(F32)
                        r = lax.rsqrt(jnp.mean(wide * wide, axis=-1, keepdims=True) + eps)
                        normed_v[2 * chip + core, at] = (wide * r * gain_v[...]).astype(BF)
                        return carry

                    lax.fori_loop(0, rows // chunk, run, 0)
                at = pl.ds(2 * chip, 2)
                stores.append(pltpu.make_async_copy(normed_v.at[at], normed_out.at[at], normed_sem.at[slot]))
                stores[-1].start()

        def project(batch):
            for slot in batch:
                chip = chip_of(slot)
                lin = mm(normed_v[pl.ds(2 * chip, 2)].reshape(2 * rows, width), w_all[...])
                at = pl.ds(pl.multiple_of(chip * 2 * rows, 2 * rows), 2 * rows)
                lin_v[0, at] = lin[:, :cols]
                lin_v[1, at] = lin[:, cols : 2 * cols]
                v_out[at] = lin[:, 2 * cols :].astype(BF)

        over = remote(columns_v.at[here.grp], columns_v.at[here.grp], cross_send.at[1], cross_recv.at[1], here.across())
        gather.settle()
        for number, batch in enumerate(batches):
            gather.side(number - 1)
            norm(batch)
            if number < far:
                gather.step(number)
            if number == 1:
                columns_of.arrive()
                over.start()
            if number == far - 1:
                cots.start()
                full.start()
                remote(
                    columns_v.at[1 - here.grp],
                    columns_v.at[1 - here.grp],
                    cross_send.at[1],
                    cross_recv.at[1],
                    here.across(),
                ).wait_recv()
                for owner in range(2 * ep_count):
                    for kind in range(kinds):
                        w_all[owner * depth : (owner + 1) * depth, kind * cols : (kind + 1) * cols] = columns_v[
                            owner // ep_count, owner % ep_count, kind
                        ]
                for earlier in batches[:number]:
                    project(earlier)
            if number >= far - 1:
                project(batch)

        def pass_on(ring_gather, crossing, step, count):
            ring_gather.step(step)
            for slot in batches[step + 1]:
                if slot < count:
                    crossing.send(slot, ring_gather.dst.at[here.chip(offsets[slot])])

        dots_v, dots_all, dots_sems = dots_s[0], dots_s[1], dots_s[2:]
        stats = []
        for piece in range(pieces):
            at = pl.ds(piece * segment, segment)
            for kind in range(2):
                lin = lin_v[kind, at]
                stats.append(jnp.sum(lin * lin, axis=-1, keepdims=True))
        dots_v[...] = as_rows(stats, dots_v.shape[0])
        spread_dots = Exchange(here, lambda e: dots_v, lambda e: dots_all.at[e], dots_sems)
        spread_dots.start()
        pass_on(full, full_over, 0, ring)
        pass_on(cots, cots_over, 0, early)
        spread_dots.arrive()
        total = dots_all[0]
        for e in range(1, ep_count):
            total = total + dots_all[e]
        r_all = as_columns(lax.rsqrt(total / width + eps))
        lane = lax.broadcasted_iota(jnp.int32, (segment, 128), 1)
        for piece in range(pieces):
            at = pl.ds(piece * segment, segment)
            kept = jnp.zeros((segment, 128), F32)
            for kind, (gain, n_out, out) in enumerate(((gain_q, nq_out, q_out), (gain_k, nk_out, k_out))):
                r = r_all[:, 2 * piece + kind : 2 * piece + kind + 1]
                n = lin_v[kind, at] * r
                n_out[at] = n
                n = n * gain
                out[at] = (n * cos_ref[at] + rolled(n) * sin_ref[at]).astype(BF)
                kept = jnp.where(lane == 1 + kind, r, kept)
            col_out[at] = kept

        att_v, att_sems = att_s[0], att_s[1:]
        per = block // rows
        line = lax.broadcasted_iota(jnp.int32, (block, block), 0)
        column_at = lax.broadcasted_iota(jnp.int32, (block, block), 1)
        causal = line >= column_at
        same = causal & (line // rows == column_at // rows)
        block_lane = lax.broadcasted_iota(jnp.int32, (block, 128), 1)

        def attend(first, spans):
            at = pl.ds(first, block)
            q = q_out[at]
            scores = []
            for begin, length, mask in spans:
                score = mm_nt(q, k_out[pl.ds(begin, length)]) * scale
                scores.append(score if mask is None else jnp.where(mask, score, -1e30))
            top = jnp.max(scores[0], axis=-1, keepdims=True)
            for score in scores[1:]:
                top = jnp.maximum(top, jnp.max(score, axis=-1, keepdims=True))
            powers = [jnp.exp(score - top) for score in scores]
            summed = sum(jnp.sum(power, axis=-1, keepdims=True) for power in powers)
            out = jnp.zeros((block, cols), F32)
            for (begin, length, _), power in zip(spans, powers):
                out = out + mm((power / summed).astype(BF), v_out[pl.ds(begin, length)])
            att_v[pl.ds(first // rows, per)] = out.astype(BF).reshape(per, rows, cols)
            col_out[at] = jnp.where(block_lane == 0, top + jnp.log(summed), col_out[at])

        for number in range(prompt_len // block):
            spans = [(0, number * block, None)] if number else []
            attend(number * block, spans + [(number * block, block, causal)])
        pass_on(full, full_over, 1, ring)
        pass_on(cots, cots_over, 1, early)

        def later(number, carry):
            first = pl.multiple_of(prompt_len + number * block, block)
            attend(first, [(0, prompt_len, None), (first, block, same)])
            return carry

        lax.fori_loop(0, (tokens - prompt_len) // block, later, 0)
        attended = Exchange(here, lambda e: att_v.at[e], lambda e: att_out.at[e], att_sems)
        attended.start()
        for step in range(2, far):
            pass_on(full, full_over, step, ring)
            pass_on(cots, cots_over, step, early)
        attended.arrive()
        for step in range(-1, far):
            full.side(step)
            cots.side(step)
        for slot in range(ring):
            full_over.take(slot)
            if slot < early:
                cots_over.take(slot)
        for slot in range(ring):
            full_over.settle(slot)
            if slot < early:
                cots_over.settle(slot)
        full.settle()
        cots.settle()
        for part in (gather, full, cots, full_over, cots_over, columns_of, spread_dots, attended):
            part.finish()
        over.wait_send()
        for copy in small_copies:
            copy.wait_send()
        for copy in stores:
            copy.wait()

    hbm = pl.BlockSpec(memory_space=pl.ANY)
    vmem = pl.BlockSpec(memory_space=pltpu.VMEM)

    def low(*shape):
        return jax.ShapeDtypeStruct(shape, BF)

    def wide(*shape):
        return jax.ShapeDtypeStruct(shape, F32)

    outs = pl.pallas_call(
        kernel,
        out_shape=[
            low(ep_count, rows, width),
            low(width, kinds * cols),
            low(2, ep_count, *small.shape),
            low(2, ep_count, *w_out.shape),
            low(ep_count, rows, width),
            low(ep_count, rows, width),
            low(tokens, cols),
            low(tokens, cols),
            low(tokens, cols),
            wide(tokens, cols),
            wide(tokens, cols),
            wide(tokens, 128),
            low(ep_count, rows, cols),
            low(ep_count, rows, width),
        ],
        in_specs=[hbm, hbm, hbm, hbm, hbm, vmem, vmem],
        out_specs=[hbm, vmem, vmem, hbm, hbm, hbm] + [vmem] * 6 + [hbm, hbm],
        scratch_shapes=Gather.scratch(ep_count)
        + Exchange.scratch(ep_count)
        + [dma((ep_count,)), dma((ep_count,))]
        + [dma, dma((2,)), dma((2,))]
        + Gather.scratch(ep_count)
        + Gather.scratch(ep_count)
        + Crossing.scratch(ep_count)
        + Crossing.scratch(ep_count)
        + [
            pltpu.VMEM((2, 2, rows, width), BF),
            pltpu.VMEM((ep_count, rows, width), BF),
            pltpu.VMEM((2, ep_count, kinds, depth, cols), BF),
            pltpu.VMEM((1, width), F32),
            pltpu.VMEM((2, tokens, cols), F32),
        ]
        + [dma((2,)), dma((ring,))]
        + [pltpu.VMEM((8, segment), F32), pltpu.VMEM((ep_count, 8, segment), F32)]
        + Exchange.scratch(ep_count)
        + [pltpu.VMEM((ep_count, rows, cols), BF)]
        + Exchange.scratch(ep_count),
        compiler_params=pltpu.CompilerParams(
            collective_id=collective_id, has_side_effects=True, vmem_limit_bytes=56 << 20
        ),
        name=name,
    )(x, weights, small, w_out, cot, *tables)
    return outs[:-1]


def angles_of(position):
    half_dim = HEAD_DIM // 2
    frequency = theta_base ** (-2.0 * jnp.arange(half_dim, dtype=F32) / HEAD_DIM)
    angles = position.astype(F32)[:, None] * frequency[None, :]
    return jnp.cos(angles), jnp.sin(angles)


def per_device(
    block_input,
    cotangent,
    routes,
    w_query,
    w_key,
    w_value,
    w_output,
    w_router,
    gain_attn,
    gain_query,
    gain_key,
    gain_mlp,
    w_gate,
    w_up,
    w_down,
):
    rows, width = block_input.shape
    top_count = routes.shape[1]
    ep_count = lax.axis_size("ep")
    grp_count = lax.axis_size("grp")
    me = lax.axis_index("ep")
    my_group = lax.axis_index("grp")
    tokens = rows * ep_count
    prompt_len = tokens // 2
    capacity = min(rows, rows * top_count * 33 // (32 * ep_count))
    cols = width // ep_count
    scale = HEAD_DIM ** (-0.5)
    depth = w_query.shape[0]

    chosen = jnp.any(routes[:, :, None] == jnp.arange(ep_count, dtype=jnp.int32), axis=1)
    per_row = 128
    router_rows = depth * ep_count // per_row
    gains = jnp.concatenate([gain_attn, gain_query, gain_key, gain_mlp])
    gain_rows = gains.shape[0] // per_row
    small = jnp.concatenate(
        [
            w_router.reshape(router_rows, per_row),
            gains.reshape(gain_rows, per_row),
            jnp.zeros((16 - router_rows - gain_rows, per_row), BF),
            chosen.T.astype(BF),
        ]
    )
    weights = jnp.stack([w_query, w_key, w_value])
    token = jnp.arange(tokens, dtype=jnp.int32)
    position = jnp.where(token < prompt_len, token, prompt_len + (token - prompt_len) % rows)
    cosine, sine = angles_of(position)
    tables = (jnp.concatenate([cosine, cosine], axis=1), jnp.concatenate([-sine, sine], axis=1))
    early = ep_count // 4
    normed_all, w_all, smalls, full_output, cot_own, cot_other, query, key, value, n_q, n_k, columns, tiles = attention(
        ep_count, block_input, weights, small, w_output, cotangent, tables, early, "attention", 1
    )
    normed_all = normed_all.reshape(tokens, width)
    full_output = full_output.reshape(width, width)
    smalls = smalls.reshape(grp_count * ep_count, small.shape[0], per_row)
    full_router = smalls[:, :router_rows].reshape(width, ep_count)
    gains = smalls[:, router_rows : router_rows + gain_rows].reshape(-1, 4, depth).transpose(1, 0, 2).reshape(4, width)
    gain_first, gain_qnorm, gain_knorm, gain_second = (gains[i].astype(F32) for i in range(4))
    chosen_all = smalls[:, 16:].reshape(grp_count, ep_count, ep_count, rows)

    gain_q = lax.dynamic_slice(gain_qnorm, (me * cols,), (cols,))
    gain_k = lax.dynamic_slice(gain_knorm, (me * cols,), (cols,))
    att_loc = tiles.transpose(1, 0, 2).reshape(rows, width)

    inputs = block_input.astype(F32)
    residual = inputs + mm(att_loc, full_output)
    r_m = lax.rsqrt(jnp.mean(residual * residual, axis=-1, keepdims=True) + eps)
    n_m = residual * r_m
    normed_mlp = (n_m * gain_second).astype(BF)
    pair = 2 * rows
    slots = -(-2 * capacity // 16) * 16
    chips = ep_count // 2
    groups = jnp.stack([my_group, 1 - my_group])
    mine = lax.dynamic_index_in_dim(chosen_all, me, 2, keepdims=False)[groups].reshape(2, chips, pair)
    slot = jnp.cumsum(mine.astype(jnp.int32), axis=-1) - 1
    places = jnp.arange(slots, dtype=jnp.int32)
    hots = ((slot[:, :, None, :] == places[:, None]) & (mine[:, :, None, :] > 0)).astype(BF)
    hots_t = ((slot[:, :, :, None] == places) & (mine[:, :, :, None] > 0)).astype(BF)
    router = jnp.pad(full_router, ((0, 0), (0, per_row - ep_count)))
    gate_w, up_w, down_w = w_gate[0], w_up[0], w_down[0]
    _, _, units, grad_out, hidden, grad_gate_pre, grad_up_pre, _, result_terms, _, d_normed_mlp, gate_grads, _ = experts(
        ep_count, normed_mlp, cot_own, cot_other, early, hots, hots_t, router, gate_w, up_w, down_w, "experts", 4
    )
    gate_grads = gate_grads[:, 0]

    probs = jax.nn.softmax(mm(normed_mlp, full_router), axis=-1)
    d_probs = gate_grads.T
    d_logits = (probs * (d_probs - jnp.sum(probs * d_probs, axis=-1, keepdims=True))).astype(BF)
    local_router = mm_tn(normed_mlp, d_logits)
    d_normed_mlp = d_normed_mlp + mm_nt(d_logits, full_router)
    local_gain_mlp = jnp.sum(d_normed_mlp * n_m, axis=0)
    d_n = d_normed_mlp * gain_second
    d_residual = cotangent.astype(F32) + r_m * (d_n - n_m * jnp.mean(n_m * d_n, axis=-1, keepdims=True))
    d_proj = d_residual.astype(BF)
    d_attended = mm_nt(d_proj, full_output).astype(BF)
    local_output = mm_tn(att_loc, d_proj).astype(BF)
    d_attended = d_attended.reshape(rows, ep_count, cols).transpose(1, 0, 2)

    gain_rows_own = jnp.stack([gain_q, gain_k])
    owners = grp_count * ep_count
    tiles = jnp.concatenate(
        [
            local_router.reshape(owners, router_rows, per_row),
            jnp.pad(local_gain_mlp.reshape(owners, 1, depth), ((0, 0), (0, 16 - router_rows - 1), (0, per_row - depth))),
        ],
        axis=1,
    )
    d_normed, grad_output, mixture, grad_w, tiles, late, grad_gate, grad_up, grad_down = backward(
        ep_count,
        d_attended,
        (query, key, value, n_q, n_k),
        columns,
        tables,
        gain_rows_own,
        w_all,
        normed_all,
        local_output.reshape(grp_count, chips, 2, depth, width),
        result_terms,
        tiles,
        [a.reshape(-1, a.shape[-1]) for a in (units, grad_out, hidden, grad_gate_pre, grad_up_pre)],
        "backward",
        9,
    )[:9]
    block_output = (residual + mixture).astype(BF)
    r_a = lax.rsqrt(jnp.mean(inputs * inputs, axis=-1, keepdims=True) + eps)
    n_a = inputs * r_a
    d_n = d_normed * gain_first
    input_grad = d_residual + r_a * (d_n - n_a * jnp.mean(n_a * d_n, axis=-1, keepdims=True))
    my_rows = my_group * ep_count + me
    grad_w = grad_w.reshape(ep_count, depth, 3, cols).transpose(2, 1, 0, 3).reshape(3, depth, width).astype(F32)
    sums = jnp.sum(tiles, axis=0)
    grad_router = sums[:router_rows].reshape(depth, ep_count)
    gain_part = jnp.sum(late[:, 2, :depth], axis=0) / lax.dynamic_slice(gain_first, (my_rows * depth,), (depth,))
    late = jnp.sum(late.reshape(grp_count, ep_count, 8, cols), axis=0)[:, :2].transpose(1, 0, 2).reshape(2, width)
    late = lax.dynamic_slice(late, (0, my_rows * depth), (2, depth))
    gain_sums = [gain_part, late[0], late[1], sums[router_rows, :depth]]
    grad_gate, grad_up, grad_down = (grad.astype(F32)[None] for grad in (grad_gate, grad_up, grad_down))
    return (
        block_output,
        input_grad,
        grad_w[0],
        grad_w[1],
        grad_w[2],
        grad_output,
        grad_router,
        gain_sums[0],
        gain_sums[1],
        gain_sums[2],
        gain_sums[3],
        grad_gate,
        grad_up,
        grad_down,
    )


def plain_scale(values, gain_vec):
    return values * lax.rsqrt(jnp.mean(values * values, axis=-1, keepdims=True) + eps) * gain_vec


def rotate(values, position):
    token_count = values.shape[0]
    by_head = values.reshape(token_count, -1, HEAD_DIM)
    half_dim = HEAD_DIM // 2
    frequency = theta_base ** (-2.0 * jnp.arange(half_dim, dtype=jnp.float32) / HEAD_DIM)
    angles = position.astype(jnp.float32)[:, None] * frequency[None, :]
    cosine = jnp.cos(angles)[:, None, :]
    sine_part = jnp.sin(angles)[:, None, :]
    former = by_head[..., :half_dim]
    latter = by_head[..., half_dim:]
    turned = jnp.concatenate(
        [former * cosine - latter * sine_part, latter * cosine + former * sine_part], axis=-1
    )
    return turned.reshape(token_count, -1)


def masked_scores(query, keys, allowed, scale):
    raw_scores = jnp.einsum("qhd,khd->hqk", query, keys, preferred_element_type=jnp.float32) * scale
    return jnp.where(allowed[None], raw_scores, -1e30)


def plain_attend(query, keys, values, allowed, scale, head_group):
    outputs = []
    log_totals = []
    for head_start in range(0, query.shape[1], head_group):
        head_slice = slice(head_start, head_start + head_group)
        scores = masked_scores(query[:, head_slice], keys[:, head_slice], allowed, scale)
        largest = jnp.max(scores, axis=-1, keepdims=True)
        exponent = jnp.exp(scores - largest)
        summed = jnp.sum(exponent, axis=-1, keepdims=True)
        weights = (exponent / summed).astype(jnp.bfloat16)
        outputs.append(
            jnp.einsum(
                "hqk,khd->qhd", weights, values[:, head_slice], preferred_element_type=jnp.float32
            )
        )
        log_totals.append(largest + jnp.log(summed))
    return (jnp.concatenate(outputs, axis=1), jnp.concatenate(log_totals, axis=0))


def plain_attend_back(query, keys, values, grad_out, log_totals, allowed, scale, head_group):
    query_grads = []
    key_grads = []
    value_grads = []
    for head_start in range(0, query.shape[1], head_group):
        head_slice = slice(head_start, head_start + head_group)
        query_part = query[:, head_slice]
        keys_part = keys[:, head_slice]
        grad_part = grad_out[:, head_slice]
        scores = masked_scores(query_part, keys_part, allowed, scale)
        weights = jnp.where(allowed[None], jnp.exp(scores - log_totals[head_slice]), 0.0)
        grad_weights = jnp.einsum(
            "qhd,khd->hqk", grad_part, values[:, head_slice], preferred_element_type=jnp.float32
        )
        inner = jnp.sum(weights * grad_weights, axis=-1, keepdims=True)
        grad_scores = (weights * (grad_weights - inner)).astype(jnp.bfloat16)
        query_grads.append(
            jnp.einsum("hqk,khd->qhd", grad_scores, keys_part, preferred_element_type=jnp.float32)
            * scale
        )
        key_grads.append(
            jnp.einsum("hqk,qhd->khd", grad_scores, query_part, preferred_element_type=jnp.float32)
            * scale
        )
        value_grads.append(
            jnp.einsum(
                "hqk,qhd->khd",
                weights.astype(jnp.bfloat16),
                grad_part,
                preferred_element_type=jnp.float32,
            )
        )
    return (
        jnp.concatenate(query_grads, axis=1),
        jnp.concatenate(key_grads, axis=1),
        jnp.concatenate(value_grads, axis=1),
    )


def per_device_plain(
    block_input,
    cotangent,
    routes,
    w_query,
    w_key,
    w_value,
    w_output,
    w_router,
    gain_attn,
    gain_query,
    gain_key,
    gain_mlp,
    w_gate,
    w_up,
    w_down,
):
    row_count, model_width = block_input.shape
    top_count = routes.shape[1]
    ep_count = lax.axis_size("ep")
    my_index = lax.axis_index("ep")
    half_count = ep_count // 2
    prompt_len = row_count * half_count
    capacity = min(row_count, row_count * top_count * 33 // (32 * ep_count))
    head_count = model_width // HEAD_DIM
    head_group = math.gcd(4, head_count)
    scale = HEAD_DIM ** (-0.5)
    gathered = (
        lax.all_gather(w_query, ("grp", "ep"), axis=0, tiled=True),
        lax.all_gather(w_key, ("grp", "ep"), axis=0, tiled=True),
        lax.all_gather(w_value, ("grp", "ep"), axis=0, tiled=True),
        lax.all_gather(w_output, ("grp", "ep"), axis=0, tiled=True),
        lax.all_gather(w_router, ("grp", "ep"), axis=0, tiled=True),
        lax.all_gather(gain_attn, ("grp", "ep"), axis=0, tiled=True),
        lax.all_gather(gain_query, ("grp", "ep"), axis=0, tiled=True),
        lax.all_gather(gain_key, ("grp", "ep"), axis=0, tiled=True),
        lax.all_gather(gain_mlp, ("grp", "ep"), axis=0, tiled=True),
    )
    full_query, full_key, full_value, full_output, full_router = (
        gathered[0],
        gathered[1],
        gathered[2],
        gathered[3],
        gathered[4],
    )
    gain_first = gathered[5].astype(jnp.float32)
    gain_qnorm = gathered[6].astype(jnp.float32)
    gain_knorm = gathered[7].astype(jnp.float32)
    gain_second = gathered[8].astype(jnp.float32)
    offsets = jnp.arange(row_count, dtype=jnp.int32)
    in_prompt = my_index < half_count
    position = jnp.where(in_prompt, my_index * row_count + offsets, prompt_len + offsets)
    key_position = jnp.concatenate([jnp.arange(prompt_len, dtype=jnp.int32), prompt_len + offsets])
    from_prompt = jnp.arange(prompt_len + row_count, dtype=jnp.int32) < prompt_len
    allowed = (key_position[None, :] <= position[:, None]) & (
        from_prompt[None, :] | jnp.logical_not(in_prompt)
    )

    def prepare(linear, gain_vec):
        return rotate(plain_scale(linear, gain_vec), position)

    inputs = block_input.astype(jnp.float32)
    normed = plain_scale(inputs, gain_first).astype(jnp.bfloat16)
    query_lin = jnp.dot(normed, full_query, preferred_element_type=jnp.float32)
    key_lin = jnp.dot(normed, full_key, preferred_element_type=jnp.float32)
    value_lin = jnp.dot(normed, full_value, preferred_element_type=jnp.float32)
    query_low = prepare(query_lin, gain_qnorm).astype(jnp.bfloat16)
    key_low = prepare(key_lin, gain_knorm).astype(jnp.bfloat16)
    value_low = value_lin.astype(jnp.bfloat16)
    shared = (
        lax.all_gather(key_low, "ep", axis=0, tiled=True),
        lax.all_gather(value_low, "ep", axis=0, tiled=True),
    )
    keys = jnp.concatenate([shared[0][:prompt_len], key_low]).reshape(-1, head_count, HEAD_DIM)
    values = jnp.concatenate([shared[1][:prompt_len], value_low]).reshape(-1, head_count, HEAD_DIM)
    query = query_low.reshape(row_count, head_count, HEAD_DIM)
    attn_out, log_totals = plain_attend(query, keys, values, allowed, scale, head_group)
    attended = attn_out.reshape(row_count, model_width).astype(jnp.bfloat16)
    residual = inputs + jnp.dot(attended, full_output, preferred_element_type=jnp.float32)
    normed_mlp = plain_scale(residual, gain_second).astype(jnp.bfloat16)
    logits = jnp.dot(normed_mlp, full_router, preferred_element_type=jnp.float32)
    probs = jax.nn.softmax(logits, axis=-1)
    picks = routes[:, :, None] == jnp.arange(ep_count, dtype=jnp.int32)[None, None, :]
    gates = jnp.sum(jnp.where(picks, probs[:, None, :], 0.0), axis=-1)
    hot_table = picks.reshape(-1, ep_count).astype(jnp.int32)
    before = jnp.cumsum(hot_table, axis=0) - hot_table
    slot_index = jnp.sum(before * hot_table, axis=1)
    target = routes.reshape(-1) * capacity + slot_index
    sentinel = row_count * top_count
    source = (
        jnp.full((ep_count * capacity,), sentinel, jnp.int32)
        .at[target]
        .set(jnp.arange(sentinel, dtype=jnp.int32))
    )
    token_of = source // top_count
    padded_rows = jnp.concatenate([normed_mlp, jnp.zeros((1, model_width), jnp.bfloat16)])
    outgoing = padded_rows[token_of].reshape(ep_count, capacity, model_width)
    arrived = lax.all_to_all(outgoing, "ep", split_axis=0, concat_axis=0, tiled=True)
    units = arrived.reshape(-1, model_width)
    gate_w = w_gate[0]
    up_w = w_up[0]
    down_w = w_down[0]
    gate_pre = jnp.dot(units, gate_w, preferred_element_type=jnp.float32)
    up_pre = jnp.dot(units, up_w, preferred_element_type=jnp.float32)
    hidden = (jax.nn.silu(gate_pre) * up_pre).astype(jnp.bfloat16)
    expert_result = jnp.dot(hidden, down_w, preferred_element_type=jnp.float32).astype(jnp.bfloat16)
    returned = lax.all_to_all(
        expert_result.reshape(ep_count, capacity, model_width),
        "ep",
        split_axis=0,
        concat_axis=0,
        tiled=True,
    )
    picked = (
        returned.reshape(-1, model_width)[target]
        .reshape(row_count, top_count, model_width)
        .astype(jnp.float32)
    )
    output_full = residual + jnp.sum(gates[:, :, None] * picked, axis=1)
    block_output = output_full.astype(jnp.bfloat16)
    back_query, back_key, back_value, back_output, back_router = (
        full_query,
        full_key,
        full_value,
        full_output,
        full_router,
    )
    grad_top = cotangent.astype(jnp.float32)
    grad_gates = jnp.sum(grad_top[:, None, :] * picked, axis=-1)
    grad_expert = (
        (gates[:, :, None] * grad_top[:, None, :]).astype(jnp.bfloat16).reshape(-1, model_width)
    )
    padded_grads = jnp.concatenate([grad_expert, jnp.zeros((1, model_width), jnp.bfloat16)])
    grad_outgoing = padded_grads[source].reshape(ep_count, capacity, model_width)
    grad_arrived = lax.all_to_all(
        grad_outgoing, "ep", split_axis=0, concat_axis=0, tiled=True
    ).reshape(-1, model_width)
    grad_hidden = jnp.einsum("nd,fd->nf", grad_arrived, down_w, preferred_element_type=jnp.float32)
    sigma = jax.nn.sigmoid(gate_pre)
    grad_gate_pre = (grad_hidden * up_pre * sigma * (1.0 + gate_pre * (1.0 - sigma))).astype(
        jnp.bfloat16
    )
    grad_up_pre = (grad_hidden * gate_pre * sigma).astype(jnp.bfloat16)
    local_down = jnp.einsum("nf,nd->fd", hidden, grad_arrived, preferred_element_type=jnp.float32)
    local_gate = jnp.einsum("nd,nf->df", units, grad_gate_pre, preferred_element_type=jnp.float32)
    local_up = jnp.einsum("nd,nf->df", units, grad_up_pre, preferred_element_type=jnp.float32)
    grad_units = jnp.einsum("nf,df->nd", grad_gate_pre, gate_w, preferred_element_type=jnp.float32)
    grad_units = grad_units + jnp.einsum(
        "nf,df->nd", grad_up_pre, up_w, preferred_element_type=jnp.float32
    )
    grad_units = grad_units.astype(jnp.bfloat16).reshape(ep_count, capacity, model_width)
    grad_returned = lax.all_to_all(
        grad_units, "ep", split_axis=0, concat_axis=0, tiled=True
    ).reshape(-1, model_width)
    grad_normed_mlp = jnp.sum(
        grad_returned[target].reshape(row_count, top_count, model_width).astype(jnp.float32), axis=1
    )
    expert_sums = (
        lax.psum(local_gate[None].astype(jnp.bfloat16), "grp").astype(jnp.float32),
        lax.psum(local_up[None].astype(jnp.bfloat16), "grp").astype(jnp.float32),
        lax.psum(local_down[None].astype(jnp.bfloat16), "grp").astype(jnp.float32),
    )
    grad_probs = jnp.sum(jnp.where(picks, grad_gates[:, :, None], 0.0), axis=1)
    grad_logits = (
        probs * (grad_probs - jnp.sum(probs * grad_probs, axis=-1, keepdims=True))
    ).astype(jnp.bfloat16)
    local_router = jnp.einsum(
        "rd,re->de", normed_mlp, grad_logits, preferred_element_type=jnp.float32
    )
    grad_normed_mlp = grad_normed_mlp + jnp.einsum(
        "re,de->rd", grad_logits, back_router, preferred_element_type=jnp.float32
    )
    unused_mlp, second_back = jax.vjp(plain_scale, residual, gain_second)
    grad_from_mlp, local_gain_mlp = second_back(grad_normed_mlp)
    grad_residual = grad_top + grad_from_mlp
    grad_proj = grad_residual.astype(jnp.bfloat16)
    local_output = jnp.einsum("rd,re->de", attended, grad_proj, preferred_element_type=jnp.float32)
    grad_attended = jnp.einsum(
        "re,de->rd", grad_proj, back_output, preferred_element_type=jnp.float32
    )
    grad_attended = grad_attended.astype(jnp.bfloat16).reshape(row_count, head_count, HEAD_DIM)
    grad_query_rot, grad_keys, grad_values = plain_attend_back(
        query, keys, values, grad_attended, log_totals, allowed, scale, head_group
    )
    grad_keys = grad_keys.reshape(-1, model_width)
    grad_values = grad_values.reshape(-1, model_width)
    padding = jnp.zeros((ep_count * row_count - prompt_len, model_width), jnp.float32)
    key_share, value_share = (
        lax.psum_scatter(
            jnp.concatenate([grad_keys[:prompt_len], padding]).astype(jnp.bfloat16),
            "ep",
            scatter_dimension=0,
            tiled=True,
        ).astype(jnp.float32),
        lax.psum_scatter(
            jnp.concatenate([grad_values[:prompt_len], padding]).astype(jnp.bfloat16),
            "ep",
            scatter_dimension=0,
            tiled=True,
        ).astype(jnp.float32),
    )
    grad_key_rot = key_share + grad_keys[prompt_len:]
    grad_value_lin = (value_share + grad_values[prompt_len:]).astype(jnp.bfloat16)
    unused_query, query_back = jax.vjp(prepare, query_lin, gain_qnorm)
    grad_query_lin, local_gain_query = query_back(grad_query_rot.reshape(row_count, model_width))
    unused_key, key_back = jax.vjp(prepare, key_lin, gain_knorm)
    grad_key_lin, local_gain_key = key_back(grad_key_rot)
    grad_query_low = grad_query_lin.astype(jnp.bfloat16)
    grad_key_low = grad_key_lin.astype(jnp.bfloat16)
    local_query = jnp.einsum(
        "rd,re->de", normed, grad_query_low, preferred_element_type=jnp.float32
    )
    local_key = jnp.einsum("rd,re->de", normed, grad_key_low, preferred_element_type=jnp.float32)
    local_value = jnp.einsum(
        "rd,re->de", normed, grad_value_lin, preferred_element_type=jnp.float32
    )
    grad_normed = jnp.einsum(
        "re,de->rd", grad_query_low, back_query, preferred_element_type=jnp.float32
    )
    grad_normed = grad_normed + jnp.einsum(
        "re,de->rd", grad_key_low, back_key, preferred_element_type=jnp.float32
    )
    grad_normed = grad_normed + jnp.einsum(
        "re,de->rd", grad_value_lin, back_value, preferred_element_type=jnp.float32
    )
    unused_first, first_back = jax.vjp(plain_scale, inputs, gain_first)
    grad_from_attn, local_gain_attn = first_back(grad_normed)
    input_grad = grad_residual + grad_from_attn
    summed_grads = (
        lax.psum_scatter(local_query, ("grp", "ep"), scatter_dimension=0, tiled=True),
        lax.psum_scatter(local_key, ("grp", "ep"), scatter_dimension=0, tiled=True),
        lax.psum_scatter(local_value, ("grp", "ep"), scatter_dimension=0, tiled=True),
        lax.psum_scatter(local_output, ("grp", "ep"), scatter_dimension=0, tiled=True),
        lax.psum_scatter(local_router, ("grp", "ep"), scatter_dimension=0, tiled=True),
        lax.psum_scatter(local_gain_attn, ("grp", "ep"), scatter_dimension=0, tiled=True),
        lax.psum_scatter(local_gain_query, ("grp", "ep"), scatter_dimension=0, tiled=True),
        lax.psum_scatter(local_gain_key, ("grp", "ep"), scatter_dimension=0, tiled=True),
        lax.psum_scatter(local_gain_mlp, ("grp", "ep"), scatter_dimension=0, tiled=True),
    )
    return (
        block_output,
        input_grad,
        summed_grads[0],
        summed_grads[1],
        summed_grads[2],
        summed_grads[3],
        summed_grads[4],
        summed_grads[5],
        summed_grads[6],
        summed_grads[7],
        summed_grads[8],
        expert_sums[0],
        expert_sums[1],
        expert_sums[2],
    )


def solution(mesh):
    both = ("grp", "ep")
    return jax.shard_map(
        per_device if mesh.shape["grp"] == 2 else per_device_plain,
        mesh=mesh,
        in_specs=(P(both, None),) * 8 + (P(both),) * 4 + (P("ep", None, None),) * 3,
        out_specs=(P(both, None),) * 7 + (P(both),) * 4 + (P("ep", None, None),) * 3,
        check_vma=False,
    )
```

time: 718 us -> 618 us (0.86)
  matrix products: 79 us -> 23.5 us
  Pallas kernels: 478 us -> 518 us
  other arithmetic: 80.1 us -> 43 us
  local copies, waits for them, and re-layouts: 41.1 us -> 25.4 us
  between operations: 15.5 us -> 1.2 us
  waiting for transfers between devices: 12.1 us -> 0 us
    pallas_call x6 -> x2, Pallas kernels: 317 us -> 361 us  [the longest x1 184 us: backward(): pl.pallas_call(kernel, out_shape=[jax.ShapeDtypeStruct((rows, width), F32...]
    convert_element_type x7 -> x1, other arithmetic: 27 us -> 2.62 us  [per_device(): ((slot[:, :, :, None] == places) & (mine[:, :, :, None] > 0)).astype(BF)]
    dot_general x9 -> x2, matrix products: 21.2 us -> 5.03 us  [mm(): return jnp.dot(a, b, preferred_element_type=F32)]
    dot_general x7 -> x0, matrix products: 15.6 us -> none  [the longest x1 8.24 us: per_device(): jnp.einsum('cps,csd->cpd', hots_t[0], result, preferred_element_type=F32)]
    dot_general x7 -> x2, matrix products: 21.2 us -> 9.11 us  [mm_tn(): lax.dot_general(a, b, (((0,), (0,)), ((), ())), preferred_element_type=F32)]
    dot_general x7 -> x2, matrix products: 21 us -> 9.35 us  [mm_nt(): lax.dot_general(a, b, (((1,), (1,)), ((), ())), preferred_element_type=F32)]
    all_gather x2 -> x0, waiting for transfers between devices: 10.7 us -> none  [the longest x1 10.7 us: per_device(): cot_both = lax.all_gather(cotangent, ('grp', 'ep'), axis=0, tiled=True)]
    reshape x9 -> x3, local copies, waits for them, and re-layouts: 11.8 us -> 2.13 us  [the longest x1 2.04 us: per_device(): d_attended = d_attended.reshape(rows, ep_count, cols).transpose(1, 0, 2)]
  transfers between devices with their start and end apart: 2 -> 0, of which waited for: 1 -> 0; matrix products, arithmetic and copies ran while one was open for 11% -> 0% of each run, Pallas kernels for 21% -> 0%
where the time goes in v3:
time: 618 us; the launch traced here: 611 us
  Pallas kernels  518 us (84%)
  other arithmetic  43 us (7%)
  local copies, waits for them, and re-layouts  25.4 us (4%)
  matrix products  23.5 us (4%)
    pallas_call x1, Pallas kernels, backward(): pl.pallas_call(kernel, out_shape=[jax.ShapeDtypeStruct((rows, width), F32...  184 us
    pallas_call x1, Pallas kernels, attention(): pl.pallas_call(kernel, out_shape=[low(ep_count, rows, width), low(width,...  178 us
    pallas_call x1, Pallas kernels, experts(): pl.pallas_call(kernel, out_shape=[low(ep_count, rows, width), low(ep_coun...  157 us
    broadcast_in_dim x3, other arithmetic, per_device(): grad.astype(F32)[None]  13.3 us

profile of v3, /device:TPU:0, one launch (start us, length us, event | category | flops | bytes accessed | tf_op | source)
XLA Modules:
  0.0 611.2 jit_solution(15143586153112315641)
XLA Ops:
  1.5 1.2 fusion.10
  5.1 2.1 pad_maximum_fusion.2.refs_1_
  7.2 3.7 fusion.11
  10.9 1.9 pad_maximum_fusion
  12.9 177.9 %attention.1 = (bf16[16,128,2048]{2,1,0:T(8,128)(2,1)}, bf16[2048,384]{1,0:T(8,128)(2,1)}, bf16[2,16,32,128]{3,2,1,0:T(8,128)(2,1)}, bf16[2,16,64,2048]{3,2,1,0:...) custom-call(bf16[128,2048]{1,0:T(8,128)(2,1)} %refs_0_.1, ...), custom_call_target="tpu_custom_call" | custom-call | tf_op jit(solution)/shard_map/attention/pallas_call | solution.py:1381
  190.7 1.3 copy.69
  196.7 1.2 reduce-window.6
  198.6 1.0 pad.8.refs_5_
  199.5 4.7 multiply_reduce_fusion.2
  205.6 1.5 fusion.3.refs_3_
  207.1 2.6 fusion.1.refs_4_
  209.7 156.6 %experts.1 = (bf16[16,128,2048]{2,1,0:T(8,128)(2,1)}, bf16[16,128,2048]{2,1,0:T(8,128)(2,1)}, bf16[2,1152,2048]{2,1,0:T(8,128)(2,1)}, bf16[2,1152,2048]{2,1,0:T(...) custom-call(bf16[128,2048]{1,0:T(8,128)(2,1)} %copy-done.3, ...), custom_call_target="tpu_custom_call" | custom-call | tf_op jit(solution)/shard_map/experts/pallas_call | solution.py:529
  367.2 1.9 multiply_reduce_fusion
  369.1 1.4 multiply_add_fusion
  370.5 7.4 %convolution_convert_fusion.1 = bf16[128,2048]{1,0:T(8,128)(2,1)} fusion(bf16[2048,2048]{1,0:T(8,128)(2,1)} %bitcast.92, f32[128,2048]{1,0:T(8,128)S(1)} %multiply_add_fusion), kind=kOutput, calls=%fused_computation.10 | convolution fusion | flops 1074266112 | bytes 9961472 | tf_op jit(solution)/shard_map/dot_general | solution.py:25
  378.0 2.0 copy.72
  380.0 2.0 copy.73
  382.1 2.3 fusion.28
  384.5 1.5 reshape.330
  386.7 6.8 %convolution_convert_fusion = bf16[2048,2048]{1,0:T(8,128)(2,1)} fusion(bf16[128,2048]{0,1:T(8,128)(2,1)} %bitcast.95, f32[128,2048]{1,0:T(8,128)S(1)} %multiply_add_fusion), kind=kOutput, calls=%fused_computation.1 | convolution fusion | flops 1078198272 | bytes 9961472 | tf_op jit(solution)/shard_map/dot_general | solution.py:29
  393.5 183.6 %backward.1 = (f32[128,2048]{1,0:T(8,128)}, f32[64,2048]{1,0:T(8,128)}, f32[128,2048]{1,0:T(8,128)}, bf16[16,64,384]{2,1,0:T(8,128)(2,1)}, f32[32,16,128]{2,1,0:...) custom-call(bf16[16,128,128]{2,1,0:T(8,128)(2,1)} %bitcast.106, ...), custom_call_target="tpu_custom_call" | custom-call | tf_op jit(solution)/shard_map/backward/pallas_call | solution.py:1041
  577.1 2.1 add_convert_fusion
  579.2 1.5 fusion.6
  580.8 2.9 fusion.9
  585.2 1.0 reduce_sum.97
  589.0 2.4 reshape.348
  591.4 1.6 fusion.26
  593.3 1.0 copy.86
  594.6 1.0 copy.87
  596.8 4.4 bitcast_convert_fusion.2
  601.2 4.4 bitcast_convert_fusion.1
  605.7 4.4 bitcast_convert_fusion
  (81 shorter events, 18.5 us)
Async XLA Ops:
  7.2 192.3 %copy-start.1 = (bf16[128,2048]{1,0:T(8,128)(2,1)S(1)}, bf16[128,2048]{1,0:T(8,128)(2,1)}, u32[]{:S(2)}) copy-start(bf16[128,2048]{1,0:T(8,128)(2,1)} %refs_0_.1) | copy-start | bytes 1572868
  192.1 12.2 %copy-start.2 = (bf16[128,16,128]{0,2,1:T(8,128)(2,1)}, bf16[128,16,128]{0,2,1:T(8,128)(2,1)S(1)}, u32[]{:S(2)}) copy-start(bf16[128,16,128]{0,2,1:T(8,128)(2,1)S(1)} %copy.69) | copy-start | bytes 1572868
  198.6 5.9 copy-start.4
  204.5 0.8 copy-start.3
  370.5 23.0 %copy-start = (f32[128,2048]{1,0:T(8,128)}, f32[128,2048]{1,0:T(8,128)S(1)}, u32[]{:S(2)}) copy-start(f32[128,2048]{1,0:T(8,128)S(1)} %multiply_add_fusion) | copy-start | bytes 3145732
  591.4 5.4 copy-start.7
  594.3 7.0 %copy-start.6 = (bf16[2048,1024]{1,0:T(8,128)(2,1)S(1)}, bf16[2048,1024]{1,0:T(8,128)(2,1)}, u32[]{:S(2)}) copy-start(bf16[2048,1024]{1,0:T(8,128)(2,1)} %get-tuple-element.72) | copy-start | bytes 12582916
  601.2 4.4 copy-start.5
  605.7 4.5 copy-start.8

commit v4 on v3

--- a/solution.py
+++ b/solution.py
@@ -2,6 +2,7 @@
 
 import jax
 import jax.numpy as jnp
+import numpy as np
 from jax import lax
 from jax.experimental import pallas as pl
 from jax.experimental.pallas import tpu as pltpu
@@ -82,8 +83,8 @@
 
 
 class Gather:
-    def __init__(self, here, src, dst, sems):
-        self.here, self.src, self.dst = here, src, dst
+    def __init__(self, here, src, dst, sems, reach=None):
+        self.here, self.src, self.dst, self.reach = here, src, dst, reach
         self.ring_send, self.ring_recv, self.side_send, self.side_recv, self.own_sem = sems
         self.rows = dst.shape[1] // 2
         self.far = here.ring // 2
@@ -104,6 +105,8 @@
         self.started.append(copy)
 
     def hops(self, way, part):
+        if self.reach is not None:
+            return self.reach
         return self.far if way == part else self.far - 1
 
     def ring_copy(self, way, step, part, src, index):
@@ -129,6 +132,8 @@
                 if self.hops(way, part) > 0:
                     self.go(self.ring_copy(way, 0, part, src, here.ep))
             self.go(self.side_copy(0, 0, part, src, here.ep))
+        if self.reach is not None:
+            return
         self.own = pltpu.make_async_copy(self.src, self.dst.at[here.ep], self.own_sem)
         self.own.start()
 
@@ -221,26 +226,26 @@
 
 
 def experts(
-    ep_count, block, cot_own, cot_other, early, hots, hots_t, router, gate_w, up_w, down_w, name, collective_id
+    ep_count, block, cot_own, cot_other, early, mine, slots, router, gate_w, up_w, down_w, name, collective_id
 ):
     rows, width = block.shape
     hidden_width = gate_w.shape[1]
-    slots = hots.shape[2]
     pair = 2 * rows
     ring = ep_count // 2
     offsets = ring_offsets(ring)
     batches = [[0]] + [[2 * k - 1, 2 * k] for k in range(1, ring // 2)] + [[ring - 1]]
     tile, wide = 512, 1024
     far = ring // 2
+    reach = far // 2
 
     def kernel(*refs):
-        ins, outs, scratch = split(refs, 9, 13, len(refs) - 22)
-        block_ref, cot_ref, cot_far, hot_ref, hot_t_ref, router_ref, gate_ref, up_ref, down_ref = ins
-        own_ref, other_ref, u_out, e_out, h_out, g_out, p_out, du_terms, eo_terms, du_joint, sum_out, dot_out, cot_late = outs
-        gather_sems, cross, cot_cross, bufs, stage, du_s, dot_sems, load_sems = split(scratch, 5, 4, 4, 5, 11, 8, 3, 5)
+        ins, outs, scratch = split(refs, 8, 12, len(refs) - 20)
+        block_ref, cot_ref, cot_far, mine_ref, router_ref, gate_ref, up_ref, down_ref = ins
+        other_ref, u_out, e_out, h_out, g_out, p_out, du_terms, eo_terms, du_joint, sum_out, dot_out, cot_late = outs
+        gather_sems, near_sems, cross, cot_cross, bufs, stage, du_s, dot_sems, load_sems = split(scratch, 5, 5, 4, 4, 6, 12, 8, 3, 5)
         across_send, across_recv, hand_send, hand_recv = cross
-        gate_v, up_v, down_v, rows_v, cot_v = bufs
-        u_s, e_s, h_s, g_s, p_s, r_s, dx_s, gate_s, dot_s, line_s, term_v = stage
+        gate_v, up_v, down_v, rows_v, cot_v, own_ref = bufs
+        u_s, e_s, h_s, g_s, p_s, r_s, dx_s, gate_s, dot_s, line_s, term_v, hot_ref = stage
         dot_send, dot_recv, dot_own = dot_sems
         weight_sem, rows_sem, cot_sem, stage_sem, term_sem = load_sems
         here = Place(ep_count)
@@ -270,6 +275,8 @@
             )
 
         start(cross_copy(0, block_ref))
+        near = Gather(here, other_ref.at[here.ep], other_ref, near_sems, reach)
+        straight = 2 * reach + 1
         cot_over = Crossing(here, lambda e: cot_late.at[e], lambda e: cot_late.at[e], cot_cross)
         for slot in range(early, ring):
             cot_over.send(slot, cot_ref.at[here.chip(offsets[slot])])
@@ -331,7 +338,7 @@
                 given[-2].wait()
 
             def put(at):
-                spread_rows = mm(hot_t_ref[0, chip], src[pl.ds(first, slots), at]).astype(BF)
+                spread_rows = mm_tn(hot_ref[0, chip], src[pl.ds(first, slots), at]).astype(BF)
                 term_v[buffer, :, :, at] = spread_rows.reshape(2, rows, width)
 
             loop(width, width, put)
@@ -347,18 +354,23 @@
         def work(which, batch, parity):
             count = len(batch) * slots
             every = pl.ds(0, count)
-            src = own_ref if which == 0 else other_ref
+            if which == 1:
+                for i, slot in enumerate(batch):
+                    rows_copy(other_ref, slot, i).start()
+                for i, slot in enumerate(batch):
+                    rows_copy(other_ref, slot, i).wait()
             for i, slot in enumerate(batch):
-                rows_copy(src, slot, i).start()
-            for i, slot in enumerate(batch):
-                rows_copy(src, slot, i).wait()
                 cot_copy(which, slot, 2 * parity + i).wait()
             settle("u")
             for i, slot in enumerate(batch):
                 hot = hot_ref[which, chip_of(slot)]
 
                 def pick_rows(at, i=i, hot=hot):
-                    picked = mm(hot, rows_v[i, :, :, at].reshape(pair, width))
+                    if which == 0:
+                        taken = own_ref[pl.ds(2 * chip_of(batch[i]), 2), :, at]
+                    else:
+                        taken = rows_v[i, :, :, at]
+                    picked = mm(hot, taken.reshape(pair, width))
                     u_s[pl.ds(i * slots, slots), at] = picked.astype(BF)
 
                 loop(width, width, pick_rows)
@@ -432,6 +444,15 @@
                     line_s[slot, core] = jnp.broadcast_to(line[:, core * rows : (core + 1) * rows], (8, rows))
 
         prefetch(0, batches[0], 0)
+        upto = lax.broadcasted_iota(jnp.int32, (pair, pair), 0) <= lax.broadcasted_iota(jnp.int32, (pair, pair), 1)
+        mine_all = mine_ref[...]
+        order = mm(mine_all.astype(BF), upto.astype(BF))
+        order = jnp.where(mine_all > 0, order - 1.0, -1.0)
+        place = lax.broadcasted_iota(jnp.int32, (slots, pair), 0).astype(F32)
+        for which in range(2):
+            for chip in range(ring):
+                line = order[which * ring + chip : which * ring + chip + 1]
+                hot_ref[which, chip] = jnp.where(place == line, 1.0, 0.0).astype(BF)
         for copy in weights:
             copy.wait()
         gather.settle()
@@ -445,7 +466,13 @@
             if number < far:
                 gather.step(number)
                 for slot in batches[number + 1]:
-                    start(cross_copy(slot, own_ref.at[here.chip(offsets[slot])]))
+                    if slot >= straight:
+                        start(cross_copy(slot, own_ref.at[here.chip(offsets[slot])]))
+                if number == 1:
+                    cross_copy(0, other_ref.at[here.ep]).wait_recv()
+                    near.start()
+                elif number > 2:
+                    near.step(number - 3)
             rest()
         def dot_copy(slot, core, sender_core, source, target):
             return remote(
@@ -477,10 +504,13 @@
             return keep_sum
 
         for number, batch in enumerate(batches):
-            for slot in batch:
+            far_slots = [slot for slot in batch if slot >= straight]
+            for slot in far_slots:
                 index = here.chip(offsets[slot])
                 cross_copy(slot, other_ref.at[index]).wait_recv()
                 start(hand_copy(slot, here.core))
+            if 0 < number < reach:
+                near.step(number)
             if 0 < number < far:
                 sums.step(number)
             if number == 1:
@@ -489,8 +519,10 @@
                 settle_given()
             if number == far:
                 sums.finish(put(sum_out))
-            for slot in batch:
+            for slot in far_slots:
                 hand_copy(slot, 1 - here.core).wait_recv()
+            if number <= reach:
+                near.side(number - 1)
             parity = (count + number) % 2
             if number + 1 < count:
                 late = [slot for slot in batches[number + 1] if slot >= early]
@@ -507,6 +539,7 @@
                 source = here.index(here.at(-offsets[slot]), core)
                 dot_copy(slot, 0, core, source, source).wait_recv()
         gather.finish()
+        near.finish()
         cot_over.finish()
         for copy in sent:
             copy.wait_send()
@@ -529,7 +562,6 @@
     return pl.pallas_call(
         kernel,
         out_shape=[
-            low(ep_count, rows, width),
             low(ep_count, rows, width),
             low(2, total, width),
             low(2, total, width),
@@ -543,17 +575,18 @@
             jax.ShapeDtypeStruct((ep_count, 8, rows), F32),
             low(ep_count, rows, width),
         ],
-        in_specs=[hbm, hbm, hbm, vmem, vmem, vmem, hbm, hbm, hbm],
-        out_specs=[hbm] * 10 + [vmem, hbm, hbm],
+        in_specs=[hbm, hbm, hbm, vmem, vmem, hbm, hbm, hbm],
+        out_specs=[hbm] * 9 + [vmem, hbm, hbm],
         scratch_shapes=Gather.scratch(ep_count)
+        + Gather.scratch(ep_count)
         + [dma((ring,))] * 4
         + Crossing.scratch(ep_count)
-        + [keep(*gate_w.shape), keep(*up_w.shape), keep(*down_w.shape), keep(2, 2, rows, width), keep(4, 2, rows, width)]
+        + [keep(*gate_w.shape), keep(*up_w.shape), keep(*down_w.shape), keep(2, 2, rows, width), keep(4, 2, rows, width), keep(ep_count, rows, width)]
         + [keep(most, width), keep(most, width), keep(total, hidden_width)]
         + [keep(most, hidden_width)] * 2
         + [keep(total, width), keep(most, width)]
         + [pltpu.VMEM((total, 1), F32), pltpu.VMEM((total, 1), F32), pltpu.VMEM((ring, 2, 8, rows), F32)]
-        + [keep(2, 2, rows, width)]
+        + [keep(2, 2, rows, width), keep(2, ring, slots, pair)]
         + RingSum.scratch(ep_count, rows, width)
         + [dma((ring, 2)), dma((ring, 2)), dma]
         + [dma((3 + len(batches),)), dma((2,)), dma((4,)), dma((4,)), dma((2,))],
@@ -561,7 +594,7 @@
             collective_id=collective_id, has_side_effects=True, vmem_limit_bytes=62 << 20
         ),
         name=name,
-    )(block, cot_own, cot_other, hots, hots_t, router, gate_w, up_w, down_w)
+    )(block, cot_own, cot_other, mine, router, gate_w, up_w, down_w)
 
 
 class RingSum:
@@ -575,12 +608,12 @@
         self.waited, self.copies = set(), []
 
     @staticmethod
-    def scratch(ep_count, rows, width, dtype=BF):
+    def scratch(ep_count, rows, width, summands=2, dtype=BF):
         ring, far = ep_count // 2, ep_count // 4
         dma = pltpu.SemaphoreType.DMA
-        shapes = [(2, rows, width), (2, far, rows, width), (2, 2, 2, rows // 2, width)]
+        shapes = [(2, rows, width), (2, far, rows, width), (2, 2, summands, rows // 2, width)]
         buffers = [pltpu.VMEM(shape, dtype) for shape in shapes]
-        return buffers + [dma((ring,)), dma((ring,)), dma((2, far, 2)), dma((2, far, 2)), dma((2, 2, 2))]
+        return buffers + [dma((ring,)), dma((ring,)), dma((2, far, 2)), dma((2, far, 2)), dma((2, 2, summands))]
 
     def hops(self, way, part):
         return self.far if way == part else self.far - 1
@@ -598,7 +631,9 @@
 
     def loads(self, way, part, step):
         index = self.here.chip(self.distance(way, part, step))
-        sources = (self.term(index), self.joint.at[self.slot(way, part, step)])
+        sources = [self.term(index), self.joint.at[self.slot(way, part, step)]]
+        if self.more is not None:
+            sources.append(self.more(index))
         return [
             pltpu.make_async_copy(
                 source.at[self.rows(part)], self.stage.at[way, part, i], self.stage_sem.at[way, part, i]
@@ -622,10 +657,16 @@
         )
 
     def start(self):
+        self.trade()
+        self.begin()
+
+    def trade(self):
         for slot in reversed(range(len(self.offsets))):
             copy = self.side_copy(slot)
             copy.start()
             self.copies.append(copy)
+
+    def begin(self):
         for part in range(2):
             for way in range(2):
                 self.load(way, part, 0)
@@ -633,10 +674,7 @@
     def value(self, way, part, step):
         for copy in self.loads(way, part, step):
             copy.wait()
-        value = self.stage[way, part, 0].astype(F32) + self.stage[way, part, 1].astype(F32)
-        if self.more is not None:
-            value = value + self.more(self.distance(way, part, step), self.rows(part))
-        return value
+        return sum(self.stage[way, part, i].astype(F32) for i in range(self.stage.shape[2]))
 
     def ring_copy(self, way, step, part):
         at = self.rows(part)
@@ -684,6 +722,12 @@
     return pltpu.roll(values, HEAD_DIM // 2, 1)
 
 
+def turns(table):
+    other = rolled(table)
+    first = lax.broadcasted_iota(jnp.int32, table.shape, 1) < HEAD_DIM // 2
+    return jnp.where(first, table, other), jnp.where(first, -other, table)
+
+
 def as_rows(columns, count):
     shape = (columns[0].shape[0], 128)
     lane = lax.broadcasted_iota(jnp.int32, shape, 1)
@@ -698,10 +742,34 @@
     return padded.T
 
 
+BACKWARD_STEPS = {
+    "sent": (("x", 0), ("x", 1), ("t", 2)),
+    "attended": (("e", 1),),
+    "scores": (("t", 2),),
+    "dots": (("t", 2), ("e", 2)),
+    "columns": (("t", 1),),
+    "terms": (("e", 3),),
+    "swap": (
+        ("d", 1),
+        ("t", 1),
+        ("g", 0),
+        ("t", 1),
+        ("d", 2),
+        ("g", 1),
+        ("t", 1),
+        ("d", 3),
+        ("g", 2),
+        ("t", 1),
+        ("g", 3),
+        ("t", 1),
+    ),
+}
+
+
 def backward(
-    ep_count, d_att, head, columns, tables, gains, w_all, normed, output_terms, result_terms, tiles, expert_rows, name, collective_id
+    ep_count, d_proj, att_loc, w_out, head, columns, table, gains, w_all, normed, result_terms, tiles, expert_rows, name, collective_id
 ):
-    rows = d_att.shape[1]
+    rows = d_proj.shape[0]
     query, key, value, norm_q, norm_k = head
     tokens, cols = query.shape
     width = w_all.shape[0]
@@ -710,21 +778,21 @@
     depth_rows, hidden_width = hidden.shape
     ring = ep_count // 2
     far = ring // 2
-    out_rows = output_terms.shape[3]
-    slab, wide, block = 256, 512, 256
+    out_rows = w_out.shape[1]
+    slab, wide, block = 256, 1024, 256
     segment = 512
     pieces = tokens // segment
     scale = HEAD_DIM ** (-0.5)
     dma = pltpu.SemaphoreType.DMA
 
     def kernel(*refs):
-        ins, outs, scratch = split(refs, 20, 13, len(refs) - 33)
-        (att_ref, q_ref, k_ref, v_ref, nq_ref, nk_ref, col_ref, cos_ref, sin_ref, gain_ref, w_ref, normed_ref) = ins[:12]
-        go_ref, eo_ref, tile_ref, u_ref, e_ref, h_ref, g_ref, p_ref = ins[12:]
+        ins, outs, scratch = split(refs, 20, 16, len(refs) - 36)
+        (proj_ref, att_ref, q_ref, k_ref, v_ref, nq_ref, nk_ref, col_ref, table_ref, gain_ref, w_ref) = ins[:11]
+        full_ref, normed_ref, eo_ref, tile_ref, u_ref, e_ref, h_ref, g_ref, p_ref = ins[11:]
         dn_out, go_out, eo_out, gw_out, tile_out, late_out, gate_out, up_out, down_out = outs[:9]
-        dn_terms, dn_joint, go_joint, eo_joint = outs[9:]
+        dn_terms, dn_joint, go_joint, eo_joint, go_mine, go_theirs, x_in = outs[9:]
         dn_s, go_s, eo_s, go_more, gw_s, tile_s, late_s, work_s, att_s, dots_s, own_s = split(
-            scratch, 8, 8, 8, 6, 7, 3, 4, 6, 8, 5, 5
+            scratch, 8, 8, 8, 5, 6, 3, 4, 6, 9, 5, 5
         )
         here = Place(ep_count)
         greet(plane_devices(here) + far_devices(here))
@@ -734,8 +802,23 @@
             copy.start()
             sent.append(copy)
 
-        (att_v, dq_s, dk_s, dv_s, lin_s), att_sems = att_s[:5], att_s[5:]
-        attended = Exchange(here, lambda e: att_ref.at[e], lambda e: att_v.at[e], att_sems)
+        (att_v, tile_v, dq_s, dk_s, dv_s, lin_s), att_sems = att_s[:6], att_s[6:]
+        slab_v, slab_sem, term_v, term_sem, gw_v = own_s
+
+        def full_copy(number):
+            return pltpu.make_async_copy(
+                full_ref.at[pl.ds(2 * number, 2)], term_v.at[number % 2], term_sem.at[number % 2]
+            )
+
+        for number in range(2):
+            full_copy(number).start()
+        for number in range(ring):
+            full_copy(number).wait()
+            for i in range(2):
+                tile_v[2 * number + i] = mm_nt(proj_ref[...], term_v[number % 2, i]).astype(BF)
+            if number + 2 < ring:
+                full_copy(number + 2).start()
+        attended = Exchange(here, lambda e: tile_v.at[e], lambda e: att_v.at[e], att_sems)
         attended.start()
 
         me = here.grp * ep_count + here.ep
@@ -761,85 +844,137 @@
                 source = ((here.grp + turn) % 2) * ep_count + (here.ep + ep_count - offset) % ep_count
                 tile_copy(turn, offset, source, src, dst, sems).wait_recv()
 
-        x_own, x_joint, x_in, go_own_sem, go_send, go_recv = go_more
-        go_load = pltpu.make_async_copy(go_ref.at[1 - here.grp, :, here.core], x_own, go_own_sem)
-        go_load.start()
-        go_side = remote(go_ref.at[1 - here.grp, :, 1 - here.core], x_joint, go_send.at[0], go_recv.at[0], here.sibling())
-        start(go_side)
+        x_own, x_joint, go_own_sem, go_send, go_recv = go_more
+        go_load = pltpu.make_async_copy(go_theirs.at[:, here.core], x_own, go_own_sem)
+        go_side = remote(go_theirs.at[:, 1 - here.core], x_joint, go_send.at[0], go_recv.at[0], here.sibling())
 
         def go_over(part):
             at = pl.ds(part * (ring // 2), ring // 2)
             return remote(x_own.at[at], x_in.at[at], go_send.at[1 + part], go_recv.at[1 + part], here.across())
 
-        arrived = []
-
-        def from_across(offset, at):
-            if not arrived:
-                arrived.append(True)
-                for half in range(2):
-                    go_over(half).wait_recv()
-            return x_in[here.chip(offset) // 2, at].astype(F32)
-
         output = RingSum(
-            here, lambda e: go_ref.at[here.grp, e // 2, e % 2], go_joint, go_s[:3], go_s[3:], from_across
+            here, lambda e: go_mine.at[e // 2, e % 2], go_joint, go_s[:3], go_s[3:], lambda e: x_in.at[e // 2]
         )
         result = RingSum(here, lambda e: eo_ref.at[e], eo_joint, eo_s[:3], eo_s[3:])
 
         left, right, sheet, left_sem, right_sem, sheet_sem = work_s
-        parts = [(u_ref, g_ref, i, gate_out, width) for i in range(hidden_width // wide)]
-        parts += [(u_ref, p_ref, i, up_out, width) for i in range(hidden_width // wide)]
-        parts += [(h_ref, e_ref, i, down_out, hidden_width) for i in range(width // wide)]
-
-        def task(lhs, rhs, column, out, end):
-            def left_copy(i):
-                at = pl.ds(pl.multiple_of(i * slab, slab), slab)
-                return pltpu.make_async_copy(lhs.at[:, at], left.at[lax.rem(i, 2)], left_sem.at[lax.rem(i, 2)])
-
-            def sheet_copy(i):
-                at = pl.ds(pl.multiple_of(i * slab, slab), slab)
-                return pltpu.make_async_copy(
-                    sheet.at[lax.rem(i, 2)], out.at[at, pl.ds(column * wide, wide)], sheet_sem.at[lax.rem(i, 2)]
+        units = [(u_ref, i) for i in range(width // slab)] + [(h_ref, i) for i in range(hidden_width // slab)]
+        turning = width // slab
+        done = []
+
+        def right_copies(late):
+            if late:
+                return [pltpu.make_async_copy(e_ref, right, right_sem.at[0])]
+            return [
+                pltpu.make_async_copy(src, right.at[:, pl.ds(i * hidden_width, hidden_width)], right_sem.at[i])
+                for i, src in enumerate((g_ref, p_ref))
+            ]
+
+        def left_copy(number):
+            src, i = units[number]
+            return pltpu.make_async_copy(src.at[:, pl.ds(i * slab, slab)], left.at[number % 2], left_sem.at[number % 2])
+
+        def sheet_copies(number):
+            src, i = units[number]
+            at = pl.ds(i * slab, slab)
+            if number >= turning:
+                return [pltpu.make_async_copy(sheet.at[number % 2], down_out.at[at], sheet_sem.at[number % 2, 0, 0])]
+            return [
+                pltpu.make_async_copy(
+                    sheet.at[number % 2, :, pl.ds(j * hidden_width, hidden_width)], out.at[at], sheet_sem.at[number % 2, 0, j]
                 )
-
-            load = pltpu.make_async_copy(rhs.at[:, pl.ds(column * wide, wide)], right, right_sem)
-            load.start()
-            left_copy(jnp.int32(0)).start()
-            load.wait()
+                for j, out in enumerate((gate_out, up_out))
+            ]
+
+        def unit(number):
+            if number in (0, turning):
+                for copy in right_copies(number > 0):
+                    copy.wait()
+            left_copy(number).wait()
+            if number + 1 < len(units):
+                left_copy(number + 1).start()
+            if number >= 2:
+                for copy in sheet_copies(number - 2):
+                    copy.wait()
 
             def run(i, carry):
-                left_copy(i).wait()
-
-                @pl.when(i + 1 < end)
-                def _():
-                    left_copy(i + 1).start()
-
-                @pl.when(i >= 2)
-                def _():
-                    sheet_copy(i - 2).wait()
-
-                sheet[lax.rem(i, 2)] = mm_tn(left[lax.rem(i, 2)], right[...]).astype(sheet.dtype)
-                sheet_copy(i).start()
+                at = pl.ds(pl.multiple_of(i * wide, wide), wide)
+                sheet[number % 2, :, at] = mm_tn(left[number % 2], right[:, at]).astype(sheet.dtype)
                 return carry
 
-            lax.fori_loop(0, end, run, 0)
-            for i in range(max(0, end - 2), end):
-                sheet_copy(jnp.int32(i)).wait()
+            lax.fori_loop(0, width // wide, run, 0)
+            for copy in sheet_copies(number):
+                copy.start()
+            if number + 1 == turning:
+                for copy in right_copies(True):
+                    copy.start()
 
         def tasks(count):
-            for _ in range(min(count, len(parts))):
-                lhs, rhs, column, out, extent = parts.pop(0)
-                task(lhs, rhs, column, out, extent // slab)
-
+            for _ in range(min(count, len(units) - len(done))):
+                unit(len(done))
+                done.append(True)
+
+        for copy in right_copies(False):
+            copy.start()
+        left_copy(0).start()
+        term_copies = []
+
+        def poll(point):
+            for kind, number in BACKWARD_STEPS.get(point, ()):
+                if kind == "t":
+                    tasks(number)
+                elif kind == "e":
+                    result.step(number)
+                elif kind == "d":
+                    normed_sum.step(number)
+                elif kind == "g":
+                    if number == 0:
+                        for half in range(2):
+                            go_over(half).wait_recv()
+                        output.begin()
+                    output.step(number)
+                elif kind == "x":
+                    start(go_over(number))
+
+        own_tiles = send_tiles(lambda i: tile_ref.at[i], tile_out, tile_s)
         result.start()
         result.step(0)
-        own_tiles = send_tiles(lambda i: tile_ref.at[i], tile_out, tile_s)
+        for number in range(2 * ring):
+            first = lax.rem((1 - here.grp) * ring + number, 2 * ring) * cols
+            turned = mm_tn(att_ref[:, pl.ds(pl.multiple_of(first, cols), cols)], proj_ref[...]).astype(BF)
+            buffer, at = number // 2 % 2, number % 2
+            terms = go_theirs if number < ring else go_mine
+            chip = number % ring
+            if at == 0 and number >= 4:
+                for copy in term_copies.pop(0):
+                    copy.wait()
+            sheet[buffer, pl.ds(at * cols, cols)] = turned
+            if at == 1:
+                copies = [
+                    pltpu.make_async_copy(
+                        sheet.at[buffer, pl.ds((2 * i + j) * out_rows, out_rows)],
+                        terms.at[chip - 1 + i, j],
+                        sheet_sem.at[buffer, i, j],
+                    )
+                    for i in range(2)
+                    for j in range(2)
+                ]
+                for copy in copies:
+                    copy.start()
+                term_copies.append(copies)
+            if number == ring + 2:
+                go_load.start()
+                start(go_side)
+        for copies in term_copies:
+            for copy in copies:
+                copy.wait()
         go_load.wait()
         go_side.wait_recv()
         for chip in range(ring):
             x_own[chip] = (x_own[chip].astype(F32) + x_joint[chip].astype(F32)).astype(BF)
-        start(go_over(0))
-        tasks(1)
+        poll("sent")
         attended.arrive()
+        poll("attended")
 
         dk_s[...] = jnp.zeros_like(dk_s)
         dv_s[...] = jnp.zeros_like(dv_s)
@@ -881,8 +1016,9 @@
             grads_of(first, [(0, prompt_len, None), (first, block, same)])
             return carry
 
+        poll("prompt")
         lax.fori_loop(0, (tokens - prompt_len) // block, later, 0)
-        result.step(1)
+        poll("scores")
 
         dots_v, dots_all, dots_sems = dots_s[0], dots_s[1], dots_s[2:]
         late_v, late_sems = late_s[0], late_s[1:]
@@ -890,13 +1026,14 @@
         stats = []
         for piece in range(pieces):
             at = pl.ds(piece * segment, segment)
+            cosine, sine = turns(table_ref[at])
             for kind, (ref, n_ref, factor) in enumerate(((dq_s, nq_ref, 1.0), (dk_s, nk_ref, scale))):
                 turned = ref[at] * factor
-                turned = turned * cos_ref[at] - rolled(turned) * sin_ref[at]
-                gain_sums[kind] = gain_sums[kind] + jnp.sum(turned * n_ref[at], axis=0, keepdims=True)
+                turned = turned * cosine - rolled(turned) * sine
+                gain_sums[kind] = gain_sums[kind] + jnp.sum(turned * n_ref[at].astype(F32), axis=0, keepdims=True)
                 turned = turned * gain_ref[kind : kind + 1]
                 ref[at] = turned
-                stats.append(jnp.sum(turned * n_ref[at], axis=-1, keepdims=True))
+                stats.append(jnp.sum(turned * n_ref[at].astype(F32), axis=-1, keepdims=True))
         dots_v[...] = as_rows(stats, dots_v.shape[0])
         spread_dots = Exchange(here, lambda e: dots_v, lambda e: dots_all.at[e], dots_sems)
         spread_dots.start()
@@ -904,7 +1041,6 @@
         for piece in range(pieces):
             at = pl.ds(piece * segment, segment)
             lin_s[at, 2 * cols : 3 * cols] = dv_s[at].astype(BF)
-        slab_v, slab_sem, term_v, term_sem, gw_v = own_s
         slabs = width // slab
         half = slabs // 2
 
@@ -917,6 +1053,7 @@
 
         slab_copy(0).start()
         slab_copy(1).start()
+        poll("dots")
         spread_dots.arrive()
         total = dots_all[0]
         for e in range(1, ep_count):
@@ -926,10 +1063,10 @@
             at = pl.ds(piece * segment, segment)
             for kind, (ref, n_ref) in enumerate(((dq_s, nq_ref), (dk_s, nk_ref))):
                 lane = 2 * piece + kind
-                grad = col_ref[at, 1 + kind : 2 + kind] * (ref[at] - n_ref[at] * total[:, lane : lane + 1])
+                grad = col_ref[at, 1 + kind : 2 + kind] * (ref[at] - n_ref[at].astype(F32) * total[:, lane : lane + 1])
                 lin_s[at, kind * cols : (kind + 1) * cols] = grad.astype(BF)
 
-        (gw_x, gw_sum, gw_x_send, gw_x_recv), gw_swap = gw_s[:4], gw_s[4:]
+        (gw_x, gw_x_send, gw_x_recv), gw_swap = gw_s[:3], gw_s[3:]
         per_slab = slab // out_rows
         gain_lines = []
 
@@ -942,7 +1079,9 @@
             weight = w_ref[pl.ds(pl.multiple_of(first, slab), slab)].astype(F32)
             line = as_rows([jnp.sum(grad * weight, axis=-1, keepdims=True)], 8)[0:1]
             owner = first // out_rows
-            gw_v[pl.ds(owner, per_slab)] = grad.astype(BF).reshape(per_slab, out_rows, 3 * cols)
+            for kind in range(3):
+                part = grad[:, kind * cols : (kind + 1) * cols].astype(BF)
+                gw_v[pl.ds(owner, per_slab), kind] = part.reshape(per_slab, out_rows, cols)
             for i in range(per_slab):
                 part = line[:, i * out_rows : (i + 1) * out_rows]
                 part = jnp.concatenate([part, jnp.zeros((1, cols - out_rows), F32)], axis=1)
@@ -955,8 +1094,8 @@
 
         for turn in range(half):
             start(over_copy(turn, projections(turn)))
-        start(go_over(1))
-        output.start()
+        poll("columns")
+        output.trade()
 
         normed_sum = RingSum(here, lambda e: dn_terms.at[e], dn_joint, dn_s[:3], dn_s[3:])
         offsets = ring_offsets(ring)
@@ -982,32 +1121,18 @@
             stores[turn].wait()
         normed_sum.start()
         normed_sum.step(0)
-        result.step(2)
+        poll("terms")
         for turn in range(half, slabs):
             projections(turn)
         own_late = send_tiles(lambda i: late_v.at[i], late_out, late_sems)
-        tasks(1)
+        poll("columns_2")
         for turn in range(half):
             over_copy(turn, (1 - here.grp) * ep_count + turn * per_slab).wait_recv()
         for e in range(ep_count):
-            gw_sum[e] = (gw_v[here.grp * ep_count + e].astype(F32) + gw_x[e].astype(F32)).astype(BF)
-        swap = Exchange(here, lambda e: gw_sum.at[e], lambda e: gw_out.at[e], gw_swap)
+            gw_x[e] = (gw_v[here.grp * ep_count + e].astype(F32) + gw_x[e].astype(F32)).astype(BF)
+        swap = Exchange(here, lambda e: gw_x.at[e], lambda e: gw_out.at[:, :, pl.ds(pl.multiple_of(e * cols, cols), cols)], gw_swap)
         swap.start()
-        normed_sum.step(1)
-        for step in range(3, far):
-            result.step(step)
-        tasks(2)
-        normed_sum.step(2)
-        tasks(2)
-        for step in range(3, far):
-            normed_sum.step(step)
-        output.step(0)
-        tasks(1)
-        output.step(1)
-        tasks(1)
-        output.step(2)
-        for step in range(3, far):
-            output.step(step)
+        poll("swap")
 
         def put(out):
             def store(at, value):
@@ -1016,7 +1141,10 @@
             return store
 
         normed_sum.finish(put(dn_out))
-        tasks(len(parts))
+        tasks(len(units))
+        for number in range(len(units) - 2, len(units)):
+            for copy in sheet_copies(number):
+                copy.wait()
         result.finish(put(eo_out))
         output.finish(put(go_out))
         take_tiles(own_tiles, lambda i: tile_ref.at[i], tile_out, tile_s)
@@ -1044,7 +1172,7 @@
             jax.ShapeDtypeStruct((rows, width), F32),
             jax.ShapeDtypeStruct((out_rows, width), F32),
             jax.ShapeDtypeStruct((rows, width), F32),
-            jax.ShapeDtypeStruct((ep_count, out_rows, 3 * cols), BF),
+            jax.ShapeDtypeStruct((3, out_rows, width), BF),
             jax.ShapeDtypeStruct(tiles.shape, F32),
             jax.ShapeDtypeStruct((group_rows, 8, cols), F32),
             jax.ShapeDtypeStruct((width, hidden_width), BF),
@@ -1054,33 +1182,53 @@
             jax.ShapeDtypeStruct((ring, rows, width), BF),
             jax.ShapeDtypeStruct((ring, out_rows, width), BF),
             jax.ShapeDtypeStruct((ring, rows, width), BF),
+            jax.ShapeDtypeStruct((ring, 2, out_rows, width), BF),
+            jax.ShapeDtypeStruct((ring, 2, out_rows, width), BF),
+            jax.ShapeDtypeStruct((ring, out_rows, width), BF),
         ],
-        in_specs=[hbm] + [vmem] * 10 + [hbm] * 9,
-        out_specs=[vmem] * 3 + [hbm] * 10,
+        in_specs=[vmem] * 11 + [hbm] * 9,
+        out_specs=[vmem] * 3 + [hbm] * 13,
         scratch_shapes=RingSum.scratch(ep_count, rows, width)
-        + RingSum.scratch(ep_count, out_rows, width)
+        + RingSum.scratch(ep_count, out_rows, width, 3)
         + RingSum.scratch(ep_count, rows, width)
-        + [keep(ring, out_rows, width)] * 3
+        + [keep(ring, out_rows, width)] * 2
         + [dma, dma((3,)), dma((3,))]
-        + [keep(ep_count, out_rows, 3 * cols)] * 2
+        + [keep(ep_count, 3, out_rows, cols)]
         + [dma((ring,)), dma((ring,))]
         + Exchange.scratch(ep_count)
         + [dma((group_rows,)), dma((group_rows,)), dma]
         + [wide_keep(group_rows, 8, cols), dma((group_rows,)), dma((group_rows,)), dma]
-        + [keep(2, depth_rows, slab), keep(depth_rows, wide), keep(2, slab, wide), dma((2,)), dma, dma((2,))]
-        + [keep(ep_count, rows, cols)]
+        + [keep(2, depth_rows, slab), keep(depth_rows, width), keep(2, slab, width), dma((2,)), dma((2,)), dma((2, 2, 2))]
+        + [keep(ep_count, rows, cols)] * 2
         + [wide_keep(tokens, cols)] * 3
         + [keep(tokens, 3 * cols)]
         + Exchange.scratch(ep_count)
         + [wide_keep(8, segment), wide_keep(ep_count, 8, segment)]
         + Exchange.scratch(ep_count)
         + [keep(2, tokens, slab), dma((2,)), keep(2, 2, rows, width), dma((2,))]
-        + [keep(group_rows, out_rows, 3 * cols)],
+        + [keep(group_rows, 3, out_rows, cols)],
         compiler_params=pltpu.CompilerParams(
-            collective_id=collective_id, has_side_effects=True, vmem_limit_bytes=62 << 20
+            collective_id=collective_id, has_side_effects=True, vmem_limit_bytes=63 << 20
         ),
         name=name,
-    )(d_att, query, key, value, norm_q, norm_k, columns, *tables, gains, w_all, normed, output_terms, result_terms, tiles, *expert_rows)
+    )(
+        d_proj,
+        att_loc,
+        query,
+        key,
+        value,
+        norm_q,
+        norm_k,
+        columns,
+        table,
+        gains,
+        w_all,
+        w_out.reshape(ep_count, cols, width),
+        normed,
+        result_terms,
+        tiles,
+        *expert_rows,
+    )
 
 
 class Crossing:
@@ -1121,7 +1269,19 @@
             copy.wait_send()
 
 
-def attention(ep_count, x, weights, small, w_out, cot, tables, early, name, collective_id):
+ATTENTION_STEPS = {
+    ("x", 0): (("f", -1),),
+    ("x", 1): (("f", 0),),
+    ("x", 2): (("f", 1),),
+    ("x", 3): (("f", 2), ("c", -1)),
+    ("x", 4): (("f", 3),),
+    "dots": (("c", 0),),
+    "prompt": (("c", 1),),
+    "sent": (("c", 2), ("c", 3)),
+}
+
+
+def attention(ep_count, x, weights, small, w_out, cot, table, early, name, collective_id):
     rows, width = x.shape
     kinds, depth, _ = weights.shape
     cols = width // ep_count
@@ -1138,8 +1298,8 @@
     dma = pltpu.SemaphoreType.DMA
 
     def kernel(*refs):
-        ins, outs, scratch = split(refs, 7, 14, len(refs) - 21)
-        x_ref, weights_ref, small_ref, w_ref, cot_ref, cos_ref, sin_ref = ins
+        ins, outs, scratch = split(refs, 6, 14, len(refs) - 20)
+        x_ref, weights_ref, small_ref, w_ref, cot_ref, table_ref = ins
         normed_out, w_all, s_out, full_out, cot_out, cot_other = outs[:6]
         q_out, k_out, v_out, nq_out, nk_out, col_out, att_out, x_land = outs[6:]
         x_s, w_s, s_s, cross, w_ring, cot_ring, w_cross, cot_cross, bufs, loads, dots_s, att_s = split(
@@ -1238,6 +1398,17 @@
                 lin_v[1, at] = lin[:, cols : 2 * cols]
                 v_out[at] = lin[:, 2 * cols :].astype(BF)
 
+        def poll(point):
+            for kind, step in ATTENTION_STEPS.get(point, ()):
+                ring_gather, crossing, count = (full, full_over, ring) if kind == "f" else (cots, cots_over, early)
+                if step < 0:
+                    ring_gather.start()
+                    continue
+                ring_gather.step(step)
+                for slot in batches[step + 1]:
+                    if slot < count:
+                        crossing.send(slot, ring_gather.dst.at[here.chip(offsets[slot])])
+
         over = remote(columns_v.at[here.grp], columns_v.at[here.grp], cross_send.at[1], cross_recv.at[1], here.across())
         gather.settle()
         for number, batch in enumerate(batches):
@@ -1245,12 +1416,11 @@
             norm(batch)
             if number < far:
                 gather.step(number)
+            poll(("x", number))
             if number == 1:
                 columns_of.arrive()
                 over.start()
             if number == far - 1:
-                cots.start()
-                full.start()
                 remote(
                     columns_v.at[1 - here.grp],
                     columns_v.at[1 - here.grp],
@@ -1268,12 +1438,6 @@
             if number >= far - 1:
                 project(batch)
 
-        def pass_on(ring_gather, crossing, step, count):
-            ring_gather.step(step)
-            for slot in batches[step + 1]:
-                if slot < count:
-                    crossing.send(slot, ring_gather.dst.at[here.chip(offsets[slot])])
-
         dots_v, dots_all, dots_sems = dots_s[0], dots_s[1], dots_s[2:]
         stats = []
         for piece in range(pieces):
@@ -1284,8 +1448,7 @@
         dots_v[...] = as_rows(stats, dots_v.shape[0])
         spread_dots = Exchange(here, lambda e: dots_v, lambda e: dots_all.at[e], dots_sems)
         spread_dots.start()
-        pass_on(full, full_over, 0, ring)
-        pass_on(cots, cots_over, 0, early)
+        poll("dots")
         spread_dots.arrive()
         total = dots_all[0]
         for e in range(1, ep_count):
@@ -1295,15 +1458,17 @@
         for piece in range(pieces):
             at = pl.ds(piece * segment, segment)
             kept = jnp.zeros((segment, 128), F32)
+            cosine, sine = turns(table_ref[at])
             for kind, (gain, n_out, out) in enumerate(((gain_q, nq_out, q_out), (gain_k, nk_out, k_out))):
                 r = r_all[:, 2 * piece + kind : 2 * piece + kind + 1]
                 n = lin_v[kind, at] * r
-                n_out[at] = n
+                n_out[at] = n.astype(BF)
                 n = n * gain
-                out[at] = (n * cos_ref[at] + rolled(n) * sin_ref[at]).astype(BF)
+                out[at] = (n * cosine + rolled(n) * sine).astype(BF)
                 kept = jnp.where(lane == 1 + kind, r, kept)
             col_out[at] = kept
 
+        poll("turned")
         att_v, att_sems = att_s[0], att_s[1:]
         per = block // rows
         line = lax.broadcasted_iota(jnp.int32, (block, block), 0)
@@ -1333,8 +1498,7 @@
         for number in range(prompt_len // block):
             spans = [(0, number * block, None)] if number else []
             attend(number * block, spans + [(number * block, block, causal)])
-        pass_on(full, full_over, 1, ring)
-        pass_on(cots, cots_over, 1, early)
+        poll("prompt")
 
         def later(number, carry):
             first = pl.multiple_of(prompt_len + number * block, block)
@@ -1344,9 +1508,7 @@
         lax.fori_loop(0, (tokens - prompt_len) // block, later, 0)
         attended = Exchange(here, lambda e: att_v.at[e], lambda e: att_out.at[e], att_sems)
         attended.start()
-        for step in range(2, far):
-            pass_on(full, full_over, step, ring)
-            pass_on(cots, cots_over, step, early)
+        poll("sent")
         attended.arrive()
         for step in range(-1, far):
             full.side(step)
@@ -1390,13 +1552,13 @@
             low(tokens, cols),
             low(tokens, cols),
             low(tokens, cols),
-            wide(tokens, cols),
-            wide(tokens, cols),
+            low(tokens, cols),
+            low(tokens, cols),
             wide(tokens, 128),
             low(ep_count, rows, cols),
             low(ep_count, rows, width),
         ],
-        in_specs=[hbm, hbm, hbm, hbm, hbm, vmem, vmem],
+        in_specs=[hbm, hbm, hbm, hbm, hbm, vmem],
         out_specs=[hbm, vmem, vmem, hbm, hbm, hbm] + [vmem] * 6 + [hbm, hbm],
         scratch_shapes=Gather.scratch(ep_count)
         + Exchange.scratch(ep_count)
@@ -1422,15 +1584,15 @@
             collective_id=collective_id, has_side_effects=True, vmem_limit_bytes=56 << 20
         ),
         name=name,
-    )(x, weights, small, w_out, cot, *tables)
+    )(x, weights, small, w_out, cot, table)
     return outs[:-1]
 
 
 def angles_of(position):
     half_dim = HEAD_DIM // 2
-    frequency = theta_base ** (-2.0 * jnp.arange(half_dim, dtype=F32) / HEAD_DIM)
-    angles = position.astype(F32)[:, None] * frequency[None, :]
-    return jnp.cos(angles), jnp.sin(angles)
+    frequency = np.float32(theta_base) ** (-2.0 * np.arange(half_dim, dtype=np.float32) / HEAD_DIM)
+    angles = position.astype(np.float32)[:, None] * frequency.astype(np.float32)[None, :]
+    return np.concatenate([np.cos(angles), np.sin(angles)], axis=1).astype(np.float32)
 
 
 def per_device(
@@ -1477,15 +1639,14 @@
         ]
     )
     weights = jnp.stack([w_query, w_key, w_value])
-    token = jnp.arange(tokens, dtype=jnp.int32)
-    position = jnp.where(token < prompt_len, token, prompt_len + (token - prompt_len) % rows)
-    cosine, sine = angles_of(position)
-    tables = (jnp.concatenate([cosine, cosine], axis=1), jnp.concatenate([-sine, sine], axis=1))
+    token = np.arange(tokens)
+    table = jnp.asarray(angles_of(np.where(token < prompt_len, token, prompt_len + (token - prompt_len) % rows)))
     early = ep_count // 4
     normed_all, w_all, smalls, full_output, cot_own, cot_other, query, key, value, n_q, n_k, columns, tiles = attention(
-        ep_count, block_input, weights, small, w_output, cotangent, tables, early, "attention", 1
+        ep_count, block_input, weights, small, w_output, cotangent, table, early, "attention", 1
     )
     normed_all = normed_all.reshape(tokens, width)
+    full_rows = full_output.reshape(grp_count * ep_count, depth, width)
     full_output = full_output.reshape(width, width)
     smalls = smalls.reshape(grp_count * ep_count, small.shape[0], per_row)
     full_router = smalls[:, :router_rows].reshape(width, ep_count)
@@ -1505,16 +1666,12 @@
     pair = 2 * rows
     slots = -(-2 * capacity // 16) * 16
     chips = ep_count // 2
-    groups = jnp.stack([my_group, 1 - my_group])
-    mine = lax.dynamic_index_in_dim(chosen_all, me, 2, keepdims=False)[groups].reshape(2, chips, pair)
-    slot = jnp.cumsum(mine.astype(jnp.int32), axis=-1) - 1
-    places = jnp.arange(slots, dtype=jnp.int32)
-    hots = ((slot[:, :, None, :] == places[:, None]) & (mine[:, :, None, :] > 0)).astype(BF)
-    hots_t = ((slot[:, :, :, None] == places) & (mine[:, :, :, None] > 0)).astype(BF)
+    mine = lax.dynamic_index_in_dim(chosen_all, me, 2, keepdims=False)
+    mine = jnp.where(my_group == 0, mine, mine[::-1]).reshape(2 * chips, pair).astype(F32)
     router = jnp.pad(full_router, ((0, 0), (0, per_row - ep_count)))
     gate_w, up_w, down_w = w_gate[0], w_up[0], w_down[0]
-    _, _, units, grad_out, hidden, grad_gate_pre, grad_up_pre, _, result_terms, _, d_normed_mlp, gate_grads, _ = experts(
-        ep_count, normed_mlp, cot_own, cot_other, early, hots, hots_t, router, gate_w, up_w, down_w, "experts", 4
+    _, units, grad_out, hidden, grad_gate_pre, grad_up_pre, _, result_terms, _, d_normed_mlp, gate_grads, _ = experts(
+        ep_count, normed_mlp, cot_own, cot_other, early, mine, slots, router, gate_w, up_w, down_w, "experts", 4
     )
     gate_grads = gate_grads[:, 0]
 
@@ -1527,9 +1684,6 @@
     d_n = d_normed_mlp * gain_second
     d_residual = cotangent.astype(F32) + r_m * (d_n - n_m * jnp.mean(n_m * d_n, axis=-1, keepdims=True))
     d_proj = d_residual.astype(BF)
-    d_attended = mm_nt(d_proj, full_output).astype(BF)
-    local_output = mm_tn(att_loc, d_proj).astype(BF)
-    d_attended = d_attended.reshape(rows, ep_count, cols).transpose(1, 0, 2)
 
     gain_rows_own = jnp.stack([gain_q, gain_k])
     owners = grp_count * ep_count
@@ -1542,14 +1696,15 @@
     )
     d_normed, grad_output, mixture, grad_w, tiles, late, grad_gate, grad_up, grad_down = backward(
         ep_count,
-        d_attended,
+        d_proj,
+        att_loc,
+        full_rows,
         (query, key, value, n_q, n_k),
         columns,
-        tables,
+        table,
         gain_rows_own,
         w_all,
         normed_all,
-        local_output.reshape(grp_count, chips, 2, depth, width),
         result_terms,
         tiles,
         [a.reshape(-1, a.shape[-1]) for a in (units, grad_out, hidden, grad_gate_pre, grad_up_pre)],
@@ -1562,7 +1717,7 @@
     d_n = d_normed * gain_first
     input_grad = d_residual + r_a * (d_n - n_a * jnp.mean(n_a * d_n, axis=-1, keepdims=True))
     my_rows = my_group * ep_count + me
-    grad_w = grad_w.reshape(ep_count, depth, 3, cols).transpose(2, 1, 0, 3).reshape(3, depth, width).astype(F32)
+    grad_w = [grad_w[i].astype(F32) for i in range(3)]
     sums = jnp.sum(tiles, axis=0)
     grad_router = sums[:router_rows].reshape(depth, ep_count)
     gain_part = jnp.sum(late[:, 2, :depth], axis=0) / lax.dynamic_slice(gain_first, (my_rows * depth,), (depth,))

time: 618 us -> 559 us (0.905)
  Pallas kernels: 518 us -> 491 us
  matrix products: 23.5 us -> 9.82 us
  local copies, waits for them, and re-layouts: 25.4 us -> 14 us
  other arithmetic: 43 us -> 33 us
    pallas_call x1, Pallas kernels: 178 us -> 165 us  [attention(): pl.pallas_call(kernel, out_shape=[low(ep_count, rows, width), low(width,...]
    pallas_call x1, Pallas kernels: 157 us -> 144 us  [experts(): pl.pallas_call(kernel, out_shape=[low(ep_count, rows, width), low(2, tota...]
    dot_general x2 -> x1, matrix products: 9.35 us -> 1.92 us  [mm_nt(): lax.dot_general(a, b, (((1,), (1,)), ((), ())), preferred_element_type=F32)]
    dot_general x2 -> x1, matrix products: 9.11 us -> 2.64 us  [mm_tn(): lax.dot_general(a, b, (((0,), (0,)), ((), ())), preferred_element_type=F32)]
where the time goes in v4:
time: 559 us; the launch traced here: 549 us
  Pallas kernels  491 us (88%)
  other arithmetic  33 us (6%)
  local copies, waits for them, and re-layouts  14 us (3%)
  matrix products  9.82 us (2%)
    pallas_call x1, Pallas kernels, backward(): pl.pallas_call(kernel, out_shape=[jax.ShapeDtypeStruct((rows, width), F32...  181 us
    pallas_call x1, Pallas kernels, attention(): pl.pallas_call(kernel, out_shape=[low(ep_count, rows, width), low(width,...  165 us
    pallas_call x1, Pallas kernels, experts(): pl.pallas_call(kernel, out_shape=[low(ep_count, rows, width), low(2, tota...  144 us
    broadcast_in_dim x3, other arithmetic, per_device(): grad.astype(F32)[None]  16.2 us

profile of v4, /device:TPU:0, one launch (start us, length us, event | category | flops | bytes accessed | tf_op | source)
XLA Modules:
  0.0 548.9 jit_solution(8952048467873747041)
XLA Ops:
  0.7 0.8 maximum_bitcast_fusion
  1.5 1.2 fusion.6
  2.8 0.7 fusion.7
  3.5 0.8 copy.46
  4.4 0.7 pad_maximum_fusion.1.refs_2_
  5.1 2.1 pad_maximum_fusion.refs_1_
  7.2 165.2 %attention.1 = (bf16[16,128,2048]{2,1,0:T(8,128)(2,1)}, bf16[2048,384]{1,0:T(8,128)(2,1)}, bf16[2,16,32,128]{3,2,1,0:T(8,128)(2,1)}, bf16[2,16,64,2048]{3,2,1,0:...) custom-call(bf16[128,2048]{1,0:T(8,128)(2,1)} %refs_0_.1, ...), custom_call_target="tpu_custom_call" | custom-call | tf_op jit(solution)/shard_map/attention/pallas_call | solution.py:1543
  172.3 0.9 slice.72
  174.4 0.8 slice.75
  175.2 0.9 slice.74
  176.2 0.6 reshape.169.refs_3_
  177.2 1.0 pad.8.refs_4_
  178.2 1.9 copy_bitcast_fusion.refs_1_
  180.1 5.0 multiply_reduce_fusion.2
  185.3 0.9 copy-done.3
  186.5 144.2 %experts.1 = (bf16[16,128,2048]{2,1,0:T(8,128)(2,1)}, bf16[2,1152,2048]{2,1,0:T(8,128)(2,1)}, bf16[2,1152,2048]{2,1,0:T(8,128)(2,1)}, bf16[2,1152,1024]{2,1,0:T(...) custom-call(bf16[128,2048]{1,0:T(8,128)(2,1)} %copy-done.3, ...), custom_call_target="tpu_custom_call" | custom-call | tf_op jit(solution)/shard_map/experts/pallas_call | solution.py:562
  330.7 0.8 slice.59
  331.6 1.9 multiply_reduce_fusion
  333.6 2.6 fusion.17
  336.3 1.5 reshape.158
  337.8 0.7 select_maximum_fusion.refs_14_
  338.5 2.2 fusion.15.refs_0_
  340.7 181.5 %backward.1 = (f32[128,2048]{1,0:T(8,128)}, f32[64,2048]{1,0:T(8,128)}, f32[128,2048]{1,0:T(8,128)}, bf16[3,64,2048]{2,1,0:T(8,128)(2,1)}, f32[32,16,128]{2,1,0:...) custom-call(bf16[128,2048]{1,0:T(8,128)(2,1)} %fusion.15.refs_0_, ...), custom_call_target="tpu_custom_call" | custom-call | tf_op jit(solution)/shard_map/backward/pallas_call | solution.py:1169
  522.2 1.6 fusion.2
  523.8 3.9 fusion.5
  527.8 0.6 dynamic-slice_divide_fusion
  529.7 0.7 copy.50
  530.3 1.2 bitcast_convert_fusion.3
  531.5 7.3 %bitcast_convert_fusion.2 = f32[1,2048,1024]{2,1,0:T(8,128)} fusion(bf16[2048,1024]{1,0:T(8,128)(2,1)} %get-tuple-element.71), kind=kLoop, calls=%fused_computation.2 | loop fusion | flops 2097152 | bytes 12582912 | tf_op jit(solution)/shard_map/broadcast_in_dim | solution.py:1727
  538.8 4.4 bitcast_convert_fusion.1
  543.2 4.4 bitcast_convert_fusion
  547.7 0.8 copy.58
  (55 shorter events, 3.7 us)
Async XLA Ops:
  0.6 179.4 %copy-start.1 = (bf16[128,2048]{1,0:T(8,128)(2,1)S(1)}, bf16[128,2048]{1,0:T(8,128)(2,1)}, u32[]{:S(2)}) copy-start(bf16[128,2048]{1,0:T(8,128)(2,1)} %refs_0_.1) | copy-start | bytes 1572868
  177.2 8.0 %copy-start.4 = (bf16[2048,16]{1,0:T(8,128)(2,1)}, bf16[2048,16]{1,0:T(8,128)(2,1)S(1)}, u32[]{:S(2)}) copy-start(bf16[2048,16]{1,0:T(8,128)(2,1)S(1)} %reshape.156) | copy-start | bytes 196612
  185.0 153.5 %copy-start = (f32[128,2048]{1,0:T(8,128)}, f32[128,2048]{1,0:T(8,128)S(1)}, u32[]{:S(2)}) copy-start(f32[128,2048]{1,0:T(8,128)S(1)} %get-tuple-element.130) | copy-start | bytes 3145732
  185.2 0.9 copy-start.3
  333.5 5.0 copy-start.2
  522.2 5.6 %copy-start.10 = (f32[32,8,128]{2,1,0:T(8,128)S(1)}, f32[32,8,128]{2,1,0:T(8,128)}, u32[]{:S(2)}) copy-start(f32[32,8,128]{2,1,0:T(8,128)} %get-tuple-element.70) | copy-start | bytes 393220
  522.2 6.2 %copy-start.9 = (f32[32,16,128]{2,1,0:T(8,128)S(1)}, f32[32,16,128]{2,1,0:T(8,128)}, u32[]{:S(2)}) copy-start(f32[32,16,128]{2,1,0:T(8,128)} %get-tuple-element.69) | copy-start | bytes 786436
  522.2 8.2 %copy-start.7 = (bf16[3,64,2048]{2,1,0:T(8,128)(2,1)S(1)}, bf16[3,64,2048]{2,1,0:T(8,128)(2,1)}, u32[]{:S(2)}) copy-start(bf16[3,64,2048]{2,1,0:T(8,128)(2,1)} %get-tuple-element.67) | copy-start | bytes 2359300
  530.3 8.5 %copy-start.6 = (bf16[2048,1024]{1,0:T(8,128)(2,1)S(1)}, bf16[2048,1024]{1,0:T(8,128)(2,1)}, u32[]{:S(2)}) copy-start(bf16[2048,1024]{1,0:T(8,128)(2,1)} %get-tuple-element.72) | copy-start | bytes 12582916
  538.8 4.4 copy-start.5
  543.2 4.5 copy-start.8

commit v5 on v4

--- a/solution.py
+++ b/solution.py
@@ -377,7 +377,6 @@
             store("u", which, batch)
             logits = mm(u_s[every], router_ref[...])
             lane = lax.broadcasted_iota(jnp.int32, logits.shape, 1)
-            logits = jnp.where(lane < ep_count, logits, -1e30)
             powers = jnp.exp(logits - jnp.max(logits, axis=-1, keepdims=True))
             gate = jnp.sum(jnp.where(lane == here.ep, powers, 0.0), axis=-1, keepdims=True)
             gate = gate / jnp.sum(powers, axis=-1, keepdims=True)
@@ -743,12 +742,12 @@
 
 
 BACKWARD_STEPS = {
-    "sent": (("x", 0), ("x", 1), ("t", 2)),
-    "attended": (("e", 1),),
-    "scores": (("t", 2),),
-    "dots": (("t", 2), ("e", 2)),
+    "sent": (("x", 0), ("x", 1), ("t", 1)),
+    "attended": (("e", 2),),
+    "scores": (("e", 3),),
+    "dots": (("t", 2),),
     "columns": (("t", 1),),
-    "terms": (("e", 3),),
+    "columns_2": (("t", 1),),
     "swap": (
         ("d", 1),
         ("t", 1),
@@ -756,10 +755,10 @@
         ("t", 1),
         ("d", 2),
         ("g", 1),
-        ("t", 1),
+        ("t", 2),
         ("d", 3),
         ("g", 2),
-        ("t", 1),
+        ("t", 2),
         ("g", 3),
         ("t", 1),
     ),
@@ -787,15 +786,25 @@
 
     def kernel(*refs):
         ins, outs, scratch = split(refs, 20, 16, len(refs) - 36)
-        (proj_ref, att_ref, q_ref, k_ref, v_ref, nq_ref, nk_ref, col_ref, table_ref, gain_ref, w_ref) = ins[:11]
+        proj_ref, gain_ref = ins[0], ins[9]
+        held = ins[1:9] + ins[10:11]
         full_ref, normed_ref, eo_ref, tile_ref, u_ref, e_ref, h_ref, g_ref, p_ref = ins[11:]
         dn_out, go_out, eo_out, gw_out, tile_out, late_out, gate_out, up_out, down_out = outs[:9]
         dn_terms, dn_joint, go_joint, eo_joint, go_mine, go_theirs, x_in = outs[9:]
-        dn_s, go_s, eo_s, go_more, gw_s, tile_s, late_s, work_s, att_s, dots_s, own_s = split(
-            scratch, 8, 8, 8, 5, 6, 3, 4, 6, 9, 5, 5
+        dn_s, go_s, eo_s, go_more, gw_s, tile_s, late_s, work_s, att_s, dots_s, own_s, held_s = split(
+            scratch, 8, 8, 8, 5, 6, 3, 4, 6, 9, 5, 5, 10
         )
+        att_ref, q_ref, k_ref, v_ref, nq_ref, nk_ref, col_ref, table_ref, w_ref = held_s[:9]
+        held_copies = [
+            pltpu.make_async_copy(src, dst, held_s[9].at[i]) for i, (src, dst) in enumerate(zip(held, held_s[:9]))
+        ]
+        for copy in held_copies:
+            copy.start()
         here = Place(ep_count)
         greet(plane_devices(here) + far_devices(here))
+        result = RingSum(here, lambda e: eo_ref.at[e], eo_joint, eo_s[:3], eo_s[3:])
+        result.start()
+        result.step(0)
         sent = []
 
         def start(copy):
@@ -814,12 +823,14 @@
             full_copy(number).start()
         for number in range(ring):
             full_copy(number).wait()
+            both = mm_nt(proj_ref[...], term_v[number % 2].reshape(2 * cols, width)).astype(BF)
             for i in range(2):
-                tile_v[2 * number + i] = mm_nt(proj_ref[...], term_v[number % 2, i]).astype(BF)
+                tile_v[2 * number + i] = both[:, i * cols : (i + 1) * cols]
             if number + 2 < ring:
                 full_copy(number + 2).start()
         attended = Exchange(here, lambda e: tile_v.at[e], lambda e: att_v.at[e], att_sems)
         attended.start()
+        result.step(1)
 
         me = here.grp * ep_count + here.ep
 
@@ -855,7 +866,6 @@
         output = RingSum(
             here, lambda e: go_mine.at[e // 2, e % 2], go_joint, go_s[:3], go_s[3:], lambda e: x_in.at[e // 2]
         )
-        result = RingSum(here, lambda e: eo_ref.at[e], eo_joint, eo_s[:3], eo_s[3:])
 
         left, right, sheet, left_sem, right_sem, sheet_sem = work_s
         units = [(u_ref, i) for i in range(width // slab)] + [(h_ref, i) for i in range(hidden_width // slab)]
@@ -936,35 +946,32 @@
                 elif kind == "x":
                     start(go_over(number))
 
-        own_tiles = send_tiles(lambda i: tile_ref.at[i], tile_out, tile_s)
-        result.start()
-        result.step(0)
-        for number in range(2 * ring):
-            first = lax.rem((1 - here.grp) * ring + number, 2 * ring) * cols
-            turned = mm_tn(att_ref[:, pl.ds(pl.multiple_of(first, cols), cols)], proj_ref[...]).astype(BF)
-            buffer, at = number // 2 % 2, number % 2
-            terms = go_theirs if number < ring else go_mine
-            chip = number % ring
-            if at == 0 and number >= 4:
+        for copy in held_copies:
+            copy.wait()
+        for number in range(ring):
+            first = lax.rem((1 - here.grp) * ring + 2 * number, 2 * ring) * cols
+            buffer, chip = number % 2, 2 * number % ring
+            terms = go_theirs if number < ring // 2 else go_mine
+            if number >= 2:
                 for copy in term_copies.pop(0):
                     copy.wait()
-            sheet[buffer, pl.ds(at * cols, cols)] = turned
-            if at == 1:
-                copies = [
-                    pltpu.make_async_copy(
-                        sheet.at[buffer, pl.ds((2 * i + j) * out_rows, out_rows)],
-                        terms.at[chip - 1 + i, j],
-                        sheet_sem.at[buffer, i, j],
-                    )
-                    for i in range(2)
-                    for j in range(2)
-                ]
-                for copy in copies:
-                    copy.start()
-                term_copies.append(copies)
-            if number == ring + 2:
+            if number == ring // 2 + 1:
                 go_load.start()
                 start(go_side)
+            turned = mm_tn(att_ref[:, pl.ds(pl.multiple_of(first, cols), 2 * cols)], proj_ref[...])
+            sheet[buffer] = turned.astype(BF)
+            copies = [
+                pltpu.make_async_copy(
+                    sheet.at[buffer, pl.ds((2 * i + j) * out_rows, out_rows)],
+                    terms.at[chip + i, j],
+                    sheet_sem.at[buffer, i, j],
+                )
+                for i in range(2)
+                for j in range(2)
+            ]
+            for copy in copies:
+                copy.start()
+            term_copies.append(copies)
         for copies in term_copies:
             for copy in copies:
                 copy.wait()
@@ -1121,6 +1128,7 @@
             stores[turn].wait()
         normed_sum.start()
         normed_sum.step(0)
+        own_tiles = send_tiles(lambda i: tile_ref.at[i], tile_out, tile_s)
         poll("terms")
         for turn in range(half, slabs):
             projections(turn)
@@ -1186,7 +1194,7 @@
             jax.ShapeDtypeStruct((ring, 2, out_rows, width), BF),
             jax.ShapeDtypeStruct((ring, out_rows, width), BF),
         ],
-        in_specs=[vmem] * 11 + [hbm] * 9,
+        in_specs=[vmem] + [hbm] * 8 + [vmem] + [hbm] * 10,
         out_specs=[vmem] * 3 + [hbm] * 13,
         scratch_shapes=RingSum.scratch(ep_count, rows, width)
         + RingSum.scratch(ep_count, out_rows, width, 3)
@@ -1206,7 +1214,11 @@
         + [wide_keep(8, segment), wide_keep(ep_count, 8, segment)]
         + Exchange.scratch(ep_count)
         + [keep(2, tokens, slab), dma((2,)), keep(2, 2, rows, width), dma((2,))]
-        + [keep(group_rows, 3, out_rows, cols)],
+        + [keep(group_rows, 3, out_rows, cols)]
+        + [keep(rows, width)]
+        + [keep(tokens, cols)] * 5
+        + [wide_keep(tokens, cols)] * 2
+        + [keep(width, 3 * cols), dma((9,))],
         compiler_params=pltpu.CompilerParams(
             collective_id=collective_id, has_side_effects=True, vmem_limit_bytes=63 << 20
         ),
@@ -1300,11 +1312,12 @@
     def kernel(*refs):
         ins, outs, scratch = split(refs, 6, 14, len(refs) - 20)
         x_ref, weights_ref, small_ref, w_ref, cot_ref, table_ref = ins
-        normed_out, w_all, s_out, full_out, cot_out, cot_other = outs[:6]
-        q_out, k_out, v_out, nq_out, nk_out, col_out, att_out, x_land = outs[6:]
-        x_s, w_s, s_s, cross, w_ring, cot_ring, w_cross, cot_cross, bufs, loads, dots_s, att_s = split(
-            scratch, 5, 3, 2, 3, 5, 5, 4, 4, 5, 2, 5, 4
+        normed_out, w_final, s_out, full_out, cot_out, cot_other = outs[:6]
+        finals, att_out, x_land = outs[6:12], outs[12], outs[13]
+        x_s, w_s, s_s, cross, w_ring, cot_ring, w_cross, cot_cross, bufs, loads, dots_s, att_s, held = split(
+            scratch, 5, 3, 2, 3, 5, 5, 4, 4, 5, 2, 5, 4, 8
         )
+        w_all, q_out, k_out, v_out, nq_out, nk_out, col_out, held_sem = held
         rows_v, normed_v, columns_v, gain_v, lin_v = bufs
         rows_sem, normed_sem = loads
         here = Place(ep_count)
@@ -1366,6 +1379,11 @@
             return here.index(here.at(offsets[slot]), 0) // 2
 
         stores = []
+
+        def leave(src, dst, number):
+            stores.append(pltpu.make_async_copy(src, dst, held_sem.at[number]))
+            stores[-1].start()
+
 
         def norm(batch):
             loaded = []
@@ -1433,6 +1451,7 @@
                         w_all[owner * depth : (owner + 1) * depth, kind * cols : (kind + 1) * cols] = columns_v[
                             owner // ep_count, owner % ep_count, kind
                         ]
+                leave(w_all, w_final, 0)
                 for earlier in batches[:number]:
                     project(earlier)
             if number >= far - 1:
@@ -1468,6 +1487,8 @@
                 kept = jnp.where(lane == 1 + kind, r, kept)
             col_out[at] = kept
 
+        for number, src in enumerate((q_out, k_out, v_out, nq_out, nk_out)):
+            leave(src, finals[number], 1 + number)
         poll("turned")
         att_v, att_sems = att_s[0], att_s[1:]
         per = block // rows
@@ -1506,8 +1527,9 @@
             return carry
 
         lax.fori_loop(0, (tokens - prompt_len) // block, later, 0)
-        attended = Exchange(here, lambda e: att_v.at[e], lambda e: att_out.at[e], att_sems)
+        attended = Exchange(here, lambda e: att_v.at[e], lambda e: att_out.at[:, pl.ds(pl.multiple_of(e * cols, cols), cols)], att_sems)
         attended.start()
+        leave(col_out, finals[5], 6)
         poll("sent")
         attended.arrive()
         for step in range(-1, far):
@@ -1555,11 +1577,11 @@
             low(tokens, cols),
             low(tokens, cols),
             wide(tokens, 128),
-            low(ep_count, rows, cols),
+            low(rows, width),
             low(ep_count, rows, width),
         ],
         in_specs=[hbm, hbm, hbm, hbm, hbm, vmem],
-        out_specs=[hbm, vmem, vmem, hbm, hbm, hbm] + [vmem] * 6 + [hbm, hbm],
+        out_specs=[hbm, hbm, vmem] + [hbm] * 11,
         scratch_shapes=Gather.scratch(ep_count)
         + Exchange.scratch(ep_count)
         + [dma((ep_count,)), dma((ep_count,))]
@@ -1579,7 +1601,10 @@
         + [pltpu.VMEM((8, segment), F32), pltpu.VMEM((ep_count, 8, segment), F32)]
         + Exchange.scratch(ep_count)
         + [pltpu.VMEM((ep_count, rows, cols), BF)]
-        + Exchange.scratch(ep_count),
+        + Exchange.scratch(ep_count)
+        + [pltpu.VMEM((width, kinds * cols), BF)]
+        + [pltpu.VMEM((tokens, cols), BF)] * 5
+        + [pltpu.VMEM((tokens, 128), F32), dma((7,))],
         compiler_params=pltpu.CompilerParams(
             collective_id=collective_id, has_side_effects=True, vmem_limit_bytes=56 << 20
         ),
@@ -1642,7 +1667,7 @@
     token = np.arange(tokens)
     table = jnp.asarray(angles_of(np.where(token < prompt_len, token, prompt_len + (token - prompt_len) % rows)))
     early = ep_count // 4
-    normed_all, w_all, smalls, full_output, cot_own, cot_other, query, key, value, n_q, n_k, columns, tiles = attention(
+    normed_all, w_all, smalls, full_output, cot_own, cot_other, query, key, value, n_q, n_k, columns, att_loc = attention(
         ep_count, block_input, weights, small, w_output, cotangent, table, early, "attention", 1
     )
     normed_all = normed_all.reshape(tokens, width)
@@ -1656,7 +1681,6 @@
 
     gain_q = lax.dynamic_slice(gain_qnorm, (me * cols,), (cols,))
     gain_k = lax.dynamic_slice(gain_knorm, (me * cols,), (cols,))
-    att_loc = tiles.transpose(1, 0, 2).reshape(rows, width)
 
     inputs = block_input.astype(F32)
     residual = inputs + mm(att_loc, full_output)
@@ -1668,10 +1692,9 @@
     chips = ep_count // 2
     mine = lax.dynamic_index_in_dim(chosen_all, me, 2, keepdims=False)
     mine = jnp.where(my_group == 0, mine, mine[::-1]).reshape(2 * chips, pair).astype(F32)
-    router = jnp.pad(full_router, ((0, 0), (0, per_row - ep_count)))
     gate_w, up_w, down_w = w_gate[0], w_up[0], w_down[0]
     _, units, grad_out, hidden, grad_gate_pre, grad_up_pre, _, result_terms, _, d_normed_mlp, gate_grads, _ = experts(
-        ep_count, normed_mlp, cot_own, cot_other, early, mine, slots, router, gate_w, up_w, down_w, "experts", 4
+        ep_count, normed_mlp, cot_own, cot_other, early, mine, slots, full_router, gate_w, up_w, down_w, "experts", 4
     )
     gate_grads = gate_grads[:, 0]
 

time: 559 us -> 553 us (0.989)
  no operation moved by 1% of the time
where the time goes in v5:
time: 553 us; the launch traced here: 543 us
  Pallas kernels  488 us (88%)
  other arithmetic  32.9 us (6%)
  local copies, waits for them, and re-layouts  10.8 us (2%)
  matrix products  9.85 us (2%)
    pallas_call x1, Pallas kernels, backward(): pl.pallas_call(kernel, out_shape=[jax.ShapeDtypeStruct((rows, width), F32...  180 us
    pallas_call x1, Pallas kernels, attention(): pl.pallas_call(kernel, out_shape=[low(ep_count, rows, width), low(width,...  163 us
    pallas_call x1, Pallas kernels, experts(): pl.pallas_call(kernel, out_shape=[low(ep_count, rows, width), low(2, tota...  144 us
    broadcast_in_dim x3, other arithmetic, per_device(): grad.astype(F32)[None]  16.2 us

profile of v5, /device:TPU:0, one launch (start us, length us, event | category | flops | bytes accessed | tf_op | source)
XLA Modules:
  0.0 542.7 jit_solution(15726724208447149091)
XLA Ops:
  0.7 0.8 maximum_bitcast_fusion
  1.4 1.2 fusion.6
  2.7 0.7 fusion.7
  3.5 0.8 copy.43
  4.3 0.7 pad_maximum_fusion.1.refs_2_
  5.0 2.1 pad_maximum_fusion.refs_1_
  7.1 163.5 %attention.1 = (bf16[16,128,2048]{2,1,0:T(8,128)(2,1)}, bf16[2048,384]{1,0:T(8,128)(2,1)}, bf16[2,16,32,128]{3,2,1,0:T(8,128)(2,1)}, bf16[2,16,64,2048]{3,2,1,0:...) custom-call(bf16[128,2048]{1,0:T(8,128)(2,1)} %refs_0_.1, ...), custom_call_target="tpu_custom_call" | custom-call | tf_op jit(solution)/shard_map/attention/pallas_call | solution.py:1565
  170.6 0.9 slice.72
  172.1 0.6 pad_maximum_fusion.2.refs_9_
  172.6 0.8 slice.75
  173.5 0.9 slice.74
  174.5 0.6 reshape.165.refs_3_
  175.5 5.2 multiply_reduce_fusion.2
  181.2 0.6 copy-done.5
  181.8 144.2 %experts.1 = (bf16[16,128,2048]{2,1,0:T(8,128)(2,1)}, bf16[2,1152,2048]{2,1,0:T(8,128)(2,1)}, bf16[2,1152,2048]{2,1,0:T(8,128)(2,1)}, bf16[2,1152,1024]{2,1,0:T(...) custom-call(bf16[128,2048]{1,0:T(8,128)(2,1)} %copy-done.5, ...), custom_call_target="tpu_custom_call" | custom-call | tf_op jit(solution)/shard_map/experts/pallas_call | solution.py:561
  326.1 0.8 slice.59
  327.0 1.7 multiply_reduce_fusion
  328.8 2.6 fusion.17
  331.5 1.5 reshape.154
  333.0 0.7 select_maximum_fusion.refs_14_
  333.7 2.2 fusion.15.refs_0_
  335.9 180.0 %backward.1 = (f32[128,2048]{1,0:T(8,128)}, f32[64,2048]{1,0:T(8,128)}, f32[128,2048]{1,0:T(8,128)}, bf16[3,64,2048]{2,1,0:T(8,128)(2,1)}, f32[32,16,128]{2,1,0:...) custom-call(bf16[128,2048]{1,0:T(8,128)(2,1)} %fusion.15.refs_0_, ...), custom_call_target="tpu_custom_call" | custom-call | tf_op jit(solution)/shard_map/backward/pallas_call | solution.py:1177
  516.0 1.6 fusion.2
  517.6 3.9 fusion.5
  521.6 0.6 dynamic-slice_divide_fusion
  522.3 0.5 slice_bitcast_fusion.2
  523.4 0.7 copy.46
  524.1 1.2 bitcast_convert_fusion.3
  525.3 7.3 %bitcast_convert_fusion.2 = f32[1,2048,1024]{2,1,0:T(8,128)} fusion(bf16[2048,1024]{1,0:T(8,128)(2,1)} %get-tuple-element.71), kind=kLoop, calls=%fused_computation.2 | loop fusion | flops 2097152 | bytes 12582912 | tf_op jit(solution)/shard_map/broadcast_in_dim | solution.py:1750
  532.6 4.4 bitcast_convert_fusion.1
  537.0 4.4 bitcast_convert_fusion
  541.5 0.8 copy.49
  (55 shorter events, 2.6 us)
Async XLA Ops:
  175.5 5.4 copy-start.3
  180.6 153.1 %copy-start = (f32[128,2048]{1,0:T(8,128)}, f32[128,2048]{1,0:T(8,128)S(1)}, u32[]{:S(2)}) copy-start(f32[128,2048]{1,0:T(8,128)S(1)} %get-tuple-element.130) | copy-start | bytes 3145732
  180.8 0.9 copy-start.5
  181.8 145.1 %copy-start.4 = (bf16[2048,16]{1,0:T(8,128)(2,1)S(1)}, bf16[2048,16]{1,0:T(8,128)(2,1)}, u32[]{:S(2)}) copy-start(bf16[2048,16]{1,0:T(8,128)(2,1)} %copy-done.3) | copy-start | bytes 196612
  328.7 5.0 copy-start.2
  335.9 180.1 %copy-start.1 = (bf16[128,2048]{1,0:T(8,128)(2,1)S(1)}, bf16[128,2048]{1,0:T(8,128)(2,1)}, u32[]{:S(2)}) copy-start(bf16[128,2048]{1,0:T(8,128)(2,1)} %refs_0_.1) | copy-start | bytes 1572868
  515.9 5.6 %copy-start.11 = (f32[32,8,128]{2,1,0:T(8,128)S(1)}, f32[32,8,128]{2,1,0:T(8,128)}, u32[]{:S(2)}) copy-start(f32[32,8,128]{2,1,0:T(8,128)} %get-tuple-element.70) | copy-start | bytes 393220
  515.9 6.2 %copy-start.10 = (f32[32,16,128]{2,1,0:T(8,128)S(1)}, f32[32,16,128]{2,1,0:T(8,128)}, u32[]{:S(2)}) copy-start(f32[32,16,128]{2,1,0:T(8,128)} %get-tuple-element.69) | copy-start | bytes 786436
  515.9 8.2 %copy-start.8 = (bf16[3,64,2048]{2,1,0:T(8,128)(2,1)S(1)}, bf16[3,64,2048]{2,1,0:T(8,128)(2,1)}, u32[]{:S(2)}) copy-start(bf16[3,64,2048]{2,1,0:T(8,128)(2,1)} %get-tuple-element.67) | copy-start | bytes 2359300
  524.1 8.5 %copy-start.7 = (bf16[2048,1024]{1,0:T(8,128)(2,1)S(1)}, bf16[2048,1024]{1,0:T(8,128)(2,1)}, u32[]{:S(2)}) copy-start(bf16[2048,1024]{1,0:T(8,128)(2,1)} %get-tuple-element.72) | copy-start | bytes 12582916
  532.6 4.4 copy-start.6
  537.0 4.5 copy-start.9

commit v6 on v5

--- a/solution.py
+++ b/solution.py
@@ -1295,7 +1295,7 @@
 
 def attention(ep_count, x, weights, small, w_out, cot, table, early, name, collective_id):
     rows, width = x.shape
-    kinds, depth, _ = weights.shape
+    kinds, depth = len(weights), weights[0].shape[0]
     cols = width // ep_count
     tokens = rows * ep_count
     prompt_len = tokens // 2
@@ -1310,12 +1310,13 @@
     dma = pltpu.SemaphoreType.DMA
 
     def kernel(*refs):
-        ins, outs, scratch = split(refs, 6, 14, len(refs) - 20)
-        x_ref, weights_ref, small_ref, w_ref, cot_ref, table_ref = ins
+        ins, outs, scratch = split(refs, 5 + kinds, 14, len(refs) - 19 - kinds)
+        x_ref, small_ref, w_ref, cot_ref, table_ref = ins[:5]
+        weight_refs = ins[5:]
         normed_out, w_final, s_out, full_out, cot_out, cot_other = outs[:6]
         finals, att_out, x_land = outs[6:12], outs[12], outs[13]
         x_s, w_s, s_s, cross, w_ring, cot_ring, w_cross, cot_cross, bufs, loads, dots_s, att_s, held = split(
-            scratch, 5, 3, 2, 3, 5, 5, 4, 4, 5, 2, 5, 4, 8
+            scratch, 5, 3 * kinds, 2, 3, 5, 5, 4, 4, 5, 2, 5, 4, 8
         )
         w_all, q_out, k_out, v_out, nq_out, nk_out, col_out, held_sem = held
         rows_v, normed_v, columns_v, gain_v, lin_v = bufs
@@ -1335,13 +1336,17 @@
         small_over(here.grp).start()
         gather = Gather(here, x_ref, x_land, x_s)
         gather.start()
-        columns_of = Exchange(
-            here,
-            lambda e: weights_ref.at[:, :, pl.ds(pl.multiple_of(e * cols, cols), cols)],
-            lambda e: columns_v.at[here.grp, e],
-            w_s,
-        )
-        columns_of.start()
+        columns_of = [
+            Exchange(
+                here,
+                lambda e, ref=ref: ref.at[:, pl.ds(pl.multiple_of(e * cols, cols), cols)],
+                lambda e, kind=kind: columns_v.at[here.grp, e, kind],
+                w_s[3 * kind : 3 * kind + 3],
+            )
+            for kind, ref in enumerate(weight_refs)
+        ]
+        for part in columns_of:
+            part.start()
         full = Gather(here, w_ref, full_out.at[here.grp], w_ring)
         full_over = Crossing(
             here, lambda e: full_out.at[here.grp, e], lambda e: full_out.at[1 - here.grp, e], w_cross
@@ -1436,7 +1441,8 @@
                 gather.step(number)
             poll(("x", number))
             if number == 1:
-                columns_of.arrive()
+                for part in columns_of:
+                    part.arrive()
                 over.start()
             if number == far - 1:
                 remote(
@@ -1545,7 +1551,7 @@
                 cots_over.settle(slot)
         full.settle()
         cots.settle()
-        for part in (gather, full, cots, full_over, cots_over, columns_of, spread_dots, attended):
+        for part in (gather, full, cots, full_over, cots_over, *columns_of, spread_dots, attended):
             part.finish()
         over.wait_send()
         for copy in small_copies:
@@ -1580,10 +1586,10 @@
             low(rows, width),
             low(ep_count, rows, width),
         ],
-        in_specs=[hbm, hbm, hbm, hbm, hbm, vmem],
+        in_specs=[hbm, hbm, hbm, hbm, vmem] + [hbm] * kinds,
         out_specs=[hbm, hbm, vmem] + [hbm] * 11,
         scratch_shapes=Gather.scratch(ep_count)
-        + Exchange.scratch(ep_count)
+        + Exchange.scratch(ep_count) * kinds
         + [dma((ep_count,)), dma((ep_count,))]
         + [dma, dma((2,)), dma((2,))]
         + Gather.scratch(ep_count)
@@ -1609,7 +1615,7 @@
             collective_id=collective_id, has_side_effects=True, vmem_limit_bytes=56 << 20
         ),
         name=name,
-    )(x, weights, small, w_out, cot, table)
+    )(x, small, w_out, cot, table, *weights)
     return outs[:-1]
 
 
@@ -1663,7 +1669,7 @@
             chosen.T.astype(BF),
         ]
     )
-    weights = jnp.stack([w_query, w_key, w_value])
+    weights = (w_query, w_key, w_value)
     token = np.arange(tokens)
     table = jnp.asarray(angles_of(np.where(token < prompt_len, token, prompt_len + (token - prompt_len) % rows)))
     early = ep_count // 4

time: 553 us -> 551 us (level)
  no operation moved by 1% of the time
where the time goes in v6:
time: 551 us; the launch traced here: 541 us
  Pallas kernels  488 us (89%)
  other arithmetic  30.9 us (6%)
  local copies, waits for them, and re-layouts  10.8 us (2%)
  matrix products  9.86 us (2%)
    pallas_call x1, Pallas kernels, backward(): pl.pallas_call(kernel, out_shape=[jax.ShapeDtypeStruct((rows, width), F32...  180 us
    pallas_call x1, Pallas kernels, attention(): pl.pallas_call(kernel, out_shape=[low(ep_count, rows, width), low(width,...  164 us
    pallas_call x1, Pallas kernels, experts(): pl.pallas_call(kernel, out_shape=[low(ep_count, rows, width), low(2, tota...  144 us
    broadcast_in_dim x3, other arithmetic, per_device(): grad.astype(F32)[None]  16.2 us

profile of v6, /device:TPU:0, one launch (start us, length us, event | category | flops | bytes accessed | tf_op | source)
XLA Modules:
  0.0 541.3 jit_solution(8171384719248746658)
XLA Ops:
  0.7 0.8 maximum_bitcast_fusion
  1.4 1.2 fusion.6
  2.7 0.7 fusion.7
  3.5 0.8 copy.43
  4.3 0.7 pad_maximum_fusion.refs_1_
  5.0 164.1 %attention.1 = (bf16[16,128,2048]{2,1,0:T(8,128)(2,1)}, bf16[2048,384]{1,0:T(8,128)(2,1)}, bf16[2,16,32,128]{3,2,1,0:T(8,128)(2,1)}, bf16[2,16,64,2048]{3,2,1,0:...) custom-call(bf16[128,2048]{1,0:T(8,128)(2,1)} %refs_0_.1, ...), custom_call_target="tpu_custom_call" | custom-call | tf_op jit(solution)/shard_map/attention/pallas_call | solution.py:1571
  169.1 0.9 slice.72
  170.6 0.6 pad_maximum_fusion.1.refs_9_
  171.2 0.8 slice.75
  172.0 0.9 slice.74
  173.0 0.6 reshape.165.refs_3_
  174.0 5.2 multiply_reduce_fusion.2
  179.7 0.6 copy-done.5
  180.3 144.2 %experts.1 = (bf16[16,128,2048]{2,1,0:T(8,128)(2,1)}, bf16[2,1152,2048]{2,1,0:T(8,128)(2,1)}, bf16[2,1152,2048]{2,1,0:T(8,128)(2,1)}, bf16[2,1152,1024]{2,1,0:T(...) custom-call(bf16[128,2048]{1,0:T(8,128)(2,1)} %copy-done.5, ...), custom_call_target="tpu_custom_call" | custom-call | tf_op jit(solution)/shard_map/experts/pallas_call | solution.py:561
  324.6 0.8 slice.59
  325.5 1.7 multiply_reduce_fusion
  327.3 2.6 fusion.17
  330.0 1.5 reshape.154
  331.5 0.7 select_maximum_fusion.refs_14_
  332.2 2.2 fusion.15.refs_0_
  334.4 180.1 %backward.1 = (f32[128,2048]{1,0:T(8,128)}, f32[64,2048]{1,0:T(8,128)}, f32[128,2048]{1,0:T(8,128)}, bf16[3,64,2048]{2,1,0:T(8,128)(2,1)}, f32[32,16,128]{2,1,0:...) custom-call(bf16[128,2048]{1,0:T(8,128)(2,1)} %fusion.15.refs_0_, ...), custom_call_target="tpu_custom_call" | custom-call | tf_op jit(solution)/shard_map/backward/pallas_call | solution.py:1177
  514.5 1.6 fusion.2
  516.2 3.9 fusion.5
  520.1 0.6 dynamic-slice_divide_fusion
  520.9 0.5 slice_bitcast_fusion.2
  521.4 0.5 slice_bitcast_fusion.1
  522.0 0.7 copy.46
  522.7 1.2 bitcast_convert_fusion.3
  523.9 7.3 %bitcast_convert_fusion.2 = f32[1,2048,1024]{2,1,0:T(8,128)} fusion(bf16[2048,1024]{1,0:T(8,128)(2,1)} %get-tuple-element.71), kind=kLoop, calls=%fused_computation.2 | loop fusion | flops 2097152 | bytes 12582912 | tf_op jit(solution)/shard_map/broadcast_in_dim | solution.py:1756
  531.1 4.4 bitcast_convert_fusion.1
  535.6 4.4 bitcast_convert_fusion
  540.0 0.8 copy.49
  (54 shorter events, 2.1 us)
Async XLA Ops:
  174.0 5.4 copy-start.3
  179.2 153.1 %copy-start = (f32[128,2048]{1,0:T(8,128)}, f32[128,2048]{1,0:T(8,128)S(1)}, u32[]{:S(2)}) copy-start(f32[128,2048]{1,0:T(8,128)S(1)} %get-tuple-element.130) | copy-start | bytes 3145732
  179.4 0.9 copy-start.5
  180.3 145.1 %copy-start.4 = (bf16[2048,16]{1,0:T(8,128)(2,1)S(1)}, bf16[2048,16]{1,0:T(8,128)(2,1)}, u32[]{:S(2)}) copy-start(bf16[2048,16]{1,0:T(8,128)(2,1)} %copy-done.3) | copy-start | bytes 196612
  327.2 5.0 copy-start.2
  334.4 180.1 %copy-start.1 = (bf16[128,2048]{1,0:T(8,128)(2,1)S(1)}, bf16[128,2048]{1,0:T(8,128)(2,1)}, u32[]{:S(2)}) copy-start(bf16[128,2048]{1,0:T(8,128)(2,1)} %refs_0_.1) | copy-start | bytes 1572868
  514.5 5.6 %copy-start.11 = (f32[32,8,128]{2,1,0:T(8,128)S(1)}, f32[32,8,128]{2,1,0:T(8,128)}, u32[]{:S(2)}) copy-start(f32[32,8,128]{2,1,0:T(8,128)} %get-tuple-element.70) | copy-start | bytes 393220
  514.5 6.2 %copy-start.10 = (f32[32,16,128]{2,1,0:T(8,128)S(1)}, f32[32,16,128]{2,1,0:T(8,128)}, u32[]{:S(2)}) copy-start(f32[32,16,128]{2,1,0:T(8,128)} %get-tuple-element.69) | copy-start | bytes 786436
  514.5 8.2 %copy-start.8 = (bf16[3,64,2048]{2,1,0:T(8,128)(2,1)S(1)}, bf16[3,64,2048]{2,1,0:T(8,128)(2,1)}, u32[]{:S(2)}) copy-start(bf16[3,64,2048]{2,1,0:T(8,128)(2,1)} %get-tuple-element.67) | copy-start | bytes 2359300
  522.7 8.5 %copy-start.7 = (bf16[2048,1024]{1,0:T(8,128)(2,1)S(1)}, bf16[2048,1024]{1,0:T(8,128)(2,1)}, u32[]{:S(2)}) copy-start(bf16[2048,1024]{1,0:T(8,128)(2,1)} %get-tuple-element.72) | copy-start | bytes 12582916
  531.1 4.4 copy-start.6
  535.6 4.5 copy-start.9
